TPU v7x, 32 devices: a whole 2x2x4 slice. The times are simulated.
32 devices in a mesh: ctx: 8 (over z, y), wt: 4 (over x, core).
Axes of the slice: x: 2, y: 2, z: 4, core: 2. Of those that a mesh axis runs over, the one named last changes fastest.
Arguments:
- tokens: bfloat16 [4, 8, 320, 1024], P('wt', 'ctx'), may hold values from -6 to 6
- cotangent: bfloat16 [4, 8, 320, 1024], P('wt', 'ctx'), may hold values from -6 to 6
- w_query: bfloat16 [1024, 1024], P('wt', 'ctx'), may hold values from -0.1875 to 0.1875
- w_key: bfloat16 [1024, 1024], P('wt', 'ctx'), may hold values from -0.1875 to 0.1875
- w_value: bfloat16 [1024, 1024], P('wt', 'ctx'), may hold values from -0.1875 to 0.1875
- w_out: bfloat16 [1024, 1024], P('wt', 'ctx'), may hold values from -1 to 1
- gain_attn: bfloat16 [1024], P('wt'), may hold values from 0.5 to 1.5
- gain_ffn: bfloat16 [1024], P('wt'), may hold values from 0.5 to 1.5
- w_router: bfloat16 [1024, 3], P('wt'), may hold values from -0.125 to 0.125
- rel_bias: bfloat16 [32, 16], P(None, 'wt'), may hold values from -4 to 4
- exp_gate: bfloat16 [3, 1024, 2816], P(None, 'wt', 'ctx'), may hold values from -0.1875 to 0.1875
- exp_up: bfloat16 [3, 1024, 2816], P(None, 'wt', 'ctx'), may hold values from -0.1875 to 0.1875
- exp_down: bfloat16 [3, 2816, 1024], P(None, 'ctx', 'wt'), may hold values from -0.3125 to 0.3125
- bucket_table: int32 [768], replicated, may hold values from 0 to 31
- expert_ids: int32 [4, 8, 320, 2], P('wt', 'ctx'), may hold values from 0 to 2, as said below
- priority: int32 [4, 8, 320], P('wt', 'ctx'), may hold values from 0 to 319, each once within a row
Outputs:
- output: bfloat16 [4, 8, 320, 1024], P('wt', 'ctx')
- grad_tokens: bfloat16 [4, 8, 320, 1024], P('wt', 'ctx')
- grad_query: float32 [1024, 1024], P('wt', 'ctx')
- grad_key: float32 [1024, 1024], P('wt', 'ctx')
- grad_value: float32 [1024, 1024], P('wt', 'ctx')
- grad_out: float32 [1024, 1024], P('wt', 'ctx')
- grad_gain_attn: float32 [1024], P('wt')
- grad_gain_ffn: float32 [1024], P('wt')
- grad_router: float32 [1024, 3], P('wt')
- grad_rel_bias: float32 [32, 16], P(None, 'wt')
- grad_exp_gate: float32 [3, 1024, 2816], P(None, 'wt', 'ctx')
- grad_exp_up: float32 [3, 1024, 2816], P(None, 'wt', 'ctx')
- grad_exp_down: float32 [3, 2816, 1024], P(None, 'ctx', 'wt')
Inputs may be any that keep to these rules, and one draw needn't show every extreme that they name: `expert_ids`: each token names 2 different experts. `priority`: within each block the 320 ranks are a permutation.
All inputs are finite; a program needn't handle non-finite values.
Results may differ from a plain program's by a relative error of at most 0.018.
Values may be sent and summed in bfloat16 or wider, within the bound.
No kernel may reach another device: no remote copies, remote signals or barrier semaphores. Data moves between devices by JAX's collectives and lax.ppermute only.
A program may use at most 384 MiB of HBM per device.

v0:
```python
import jax
import jax.numpy as jnp
from jax import lax
from jax.sharding import PartitionSpec as P

HEADS = 16
HEAD_DIM = 64
BUCKETS = 32
EXPERTS = 3
TOP = 2
LEN = 256
CAP = 267


epsilon = 1e-06
precise = lax.Precision.HIGHEST


def rms_norm(values, gain_vec):
    return (
        values * lax.rsqrt(jnp.mean(values * values, axis=-1, keepdims=True) + epsilon) * gain_vec
    )


def gelu_product(gate_pre, up_pre):
    return jax.nn.gelu(gate_pre, approximate=True) * up_pre


def routing(expert_ids, priority, capacity, expert_count):
    tok_rows = expert_ids.shape[0]
    top_count = expert_ids.shape[1]
    expert = expert_ids.T.reshape(-1)
    rank_key = (
        jnp.arange(top_count, dtype=jnp.int32)[:, None] * tok_rows + priority[None, :]
    ).reshape(-1)
    earlier = (expert[:, None] == expert[None, :]) & (rank_key[None, :] < rank_key[:, None])
    places = jnp.sum(earlier.astype(jnp.int32), axis=1)
    keep_mask = places < capacity
    slot_ids = expert * capacity + jnp.minimum(places, capacity - 1)
    slot_hits = jnp.where(
        (slot_ids[:, None] == jnp.arange(expert_count * capacity, dtype=jnp.int32)[None, :])
        & keep_mask[:, None],
        1.0,
        0.0,
    )
    dispatch = jnp.sum(slot_hits.reshape(top_count, tok_rows, expert_count * capacity), axis=0).T
    return (keep_mask, slot_ids, slot_hits, dispatch)


def gate_values(logits, expert_ids, keep_mask):
    chances = jax.nn.softmax(logits, axis=-1)
    picked = jnp.take_along_axis(chances, expert_ids, axis=1).T.reshape(-1)
    return jnp.where(keep_mask, picked, 0.0)


def toeplitz(reversed_bias, top_start, row_total, key_total):
    window_len = row_total + key_total
    window = lax.dynamic_slice_in_dim(reversed_bias, top_start, window_len, 1)
    tiled = jnp.tile(window, (1, row_total))[:, : row_total * (window_len - 1)]
    return tiled.reshape(window.shape[0], row_total, window_len - 1)[:, :, row_total - 1 :]


def toeplitz_back(grad_block, row_total, key_total):
    window_len = row_total + key_total
    head_total = grad_block.shape[0]
    placed = jnp.pad(grad_block, ((0, 0), (0, 0), (row_total - 1, 0))).reshape(
        head_total, row_total * (window_len - 1)
    )
    placed = jnp.pad(placed, ((0, 0), (0, row_total)))
    return jnp.sum(placed.reshape(head_total, row_total, window_len), axis=1)


def add_window(table, piece, start):
    current = lax.dynamic_slice_in_dim(table, start, piece.shape[1], 1)
    return lax.dynamic_update_slice_in_dim(table, current + piece, start, 1)


def sweep(step_fn, start_state, prompt_items, local_items):
    state_mid, stacked = lax.scan(step_fn, start_state, prompt_items)
    state_end, last_out = step_fn(state_mid, local_items)
    return (state_end, stacked, last_out)


def local(
    tokens,
    cotangent,
    w_query,
    w_key,
    w_value,
    w_out,
    gain_attn,
    gain_ffn,
    w_router,
    rel_bias,
    exp_gate,
    exp_up,
    exp_down,
    bucket_table,
    expert_ids,
    priority,
):
    tok_rows = tokens.shape[2]
    model_width = tokens.shape[3]
    ctx_count = lax.axis_size("ctx")
    my_block = lax.axis_index("ctx")
    prompt_rows = tok_rows - LEN
    cont_rows = tok_rows - prompt_rows
    prompt_len = prompt_rows * ctx_count
    dist_count = bucket_table.shape[0]
    head_count = HEADS
    head_width = HEAD_DIM
    score_scale = HEAD_DIM ** (-0.5)
    steps_count = max(1, ctx_count // 8)
    block_keys = prompt_len // steps_count
    cols_query, cols_key, cols_value, cols_out, cols_gate, cols_up, cols_down = (
        lax.all_gather(w_query, "ctx", axis=1, tiled=True),
        lax.all_gather(w_key, "ctx", axis=1, tiled=True),
        lax.all_gather(w_value, "ctx", axis=1, tiled=True),
        lax.all_gather(w_out, "ctx", axis=1, tiled=True),
        lax.all_gather(exp_gate, "ctx", axis=2, tiled=True),
        lax.all_gather(exp_up, "ctx", axis=2, tiled=True),
        lax.all_gather(exp_down, "ctx", axis=1, tiled=True),
    )
    gathered = (
        lax.all_gather(cols_query, "wt", axis=0, tiled=True),
        lax.all_gather(cols_key, "wt", axis=0, tiled=True),
        lax.all_gather(cols_value, "wt", axis=0, tiled=True),
        lax.all_gather(cols_out, "wt", axis=0, tiled=True),
        lax.all_gather(cols_gate, "wt", axis=1, tiled=True),
        lax.all_gather(cols_up, "wt", axis=1, tiled=True),
        lax.all_gather(cols_down, "wt", axis=2, tiled=True),
        lax.all_gather(gain_attn, "wt", axis=0, tiled=True),
        lax.all_gather(gain_ffn, "wt", axis=0, tiled=True),
        lax.all_gather(w_router, "wt", axis=0, tiled=True),
        lax.all_gather(rel_bias, "wt", axis=1, tiled=True),
    )
    (
        full_query,
        full_key,
        full_value,
        full_out,
        full_gate,
        full_up,
        full_down,
        full_gain_attn,
        full_gain_ffn,
        full_router,
        full_bias,
    ) = gathered
    gain_attn_f = full_gain_attn.astype(jnp.float32)
    gain_ffn_f = full_gain_ffn.astype(jnp.float32)
    source = tokens[0, 0].astype(jnp.float32)
    normed_attn = rms_norm(source, gain_attn_f)
    normed_attn_low = normed_attn.astype(jnp.bfloat16)
    query_low = jnp.dot(normed_attn_low, full_query, preferred_element_type=jnp.float32).astype(
        jnp.bfloat16
    )
    key_low = jnp.dot(normed_attn_low, full_key, preferred_element_type=jnp.float32).astype(
        jnp.bfloat16
    )
    value_low = jnp.dot(normed_attn_low, full_value, preferred_element_type=jnp.float32).astype(
        jnp.bfloat16
    )
    far_keys, far_values = (
        lax.all_gather(key_low[:prompt_rows], "ctx", axis=0, tiled=True),
        lax.all_gather(value_low[:prompt_rows], "ctx", axis=0, tiled=True),
    )
    row_index = jnp.arange(tok_rows, dtype=jnp.int32)
    query_pos = jnp.where(
        row_index < prompt_rows,
        my_block * prompt_rows + row_index,
        prompt_len + row_index - prompt_rows,
    )
    bucket_onehot = jnp.where(
        bucket_table[:, None] == jnp.arange(BUCKETS, dtype=jnp.int32)[None, :], 1.0, 0.0
    )
    bias_rows = jnp.dot(bucket_onehot, full_bias.astype(jnp.float32), precision=precise).T
    reversed_bias = jnp.concatenate([bias_rows[:, ::-1], jnp.zeros_like(bias_rows)], axis=1)
    prompt_starts = jnp.arange(steps_count, dtype=jnp.int32) * block_keys
    local_start = jnp.asarray(prompt_len, dtype=jnp.int32)
    query_heads = query_low.reshape(tok_rows, head_count, head_width)

    def blocks_of(far_array):
        return far_array.reshape(steps_count, block_keys, model_width)

    def window_starts(key_start):
        prompt_top = dist_count - my_block * prompt_rows + key_start - prompt_rows
        cont_top = dist_count - prompt_len + key_start - cont_rows
        return (prompt_top, cont_top)

    def block_scores(key_block, key_start):
        key_total = key_block.shape[0]
        key_heads = key_block.reshape(key_total, head_count, head_width)
        logit_raw = (
            jnp.einsum("qhd,khd->hqk", query_heads, key_heads, preferred_element_type=jnp.float32)
            * score_scale
        )
        key_pos = key_start + jnp.arange(key_total, dtype=jnp.int32)
        offset = query_pos[:, None] - key_pos[None, :]
        prompt_top, cont_top = window_starts(key_start)
        bias_block = jnp.concatenate(
            [
                toeplitz(reversed_bias, prompt_top, prompt_rows, key_total),
                toeplitz(reversed_bias, cont_top, cont_rows, key_total),
            ],
            axis=1,
        )
        return jnp.where(offset[None] >= 0, logit_raw + bias_block, -1e30)

    def stats_step(state_in, block_item):
        run_max, run_sum = state_in
        scores = block_scores(block_item[0], block_item[1])
        new_max = jnp.maximum(run_max, jnp.max(scores, axis=-1))
        new_sum = run_sum * jnp.exp(run_max - new_max) + jnp.sum(
            jnp.exp(scores - new_max[..., None]), axis=-1
        )
        return ((new_max, new_sum), None)

    start_stats = (
        jnp.full((head_count, tok_rows), -1e30, jnp.float32),
        jnp.zeros((head_count, tok_rows), jnp.float32),
    )
    (row_max, row_sum), unused_a, unused_b = sweep(
        stats_step,
        start_stats,
        (blocks_of(far_keys), prompt_starts),
        (key_low[prompt_rows:], local_start),
    )

    def mix_step(state_in, block_item):
        scores = block_scores(block_item[0], block_item[2])
        weights = (jnp.exp(scores - row_max[..., None]) / row_sum[..., None]).astype(jnp.bfloat16)
        value_heads = block_item[1].reshape(-1, head_count, head_width)
        return (
            state_in
            + jnp.einsum("hqk,khd->qhd", weights, value_heads, preferred_element_type=jnp.float32),
            None,
        )

    mixed_exact, unused_c, unused_d = sweep(
        mix_step,
        jnp.zeros((tok_rows, head_count, head_width), jnp.float32),
        (blocks_of(far_keys), blocks_of(far_values), prompt_starts),
        (key_low[prompt_rows:], value_low[prompt_rows:], local_start),
    )
    mixed_low = mixed_exact.reshape(tok_rows, model_width).astype(jnp.bfloat16)
    hidden = source + jnp.dot(mixed_low, full_out, preferred_element_type=jnp.float32)
    normed_ffn_low = rms_norm(hidden, gain_ffn_f).astype(jnp.bfloat16)
    route_ids = expert_ids[0, 0]
    keep_mask, slot_ids, slot_hits, dispatch = routing(route_ids, priority[0, 0], CAP, EXPERTS)
    inputs = (
        jnp.dot(dispatch.astype(jnp.bfloat16), normed_ffn_low, preferred_element_type=jnp.float32)
        .astype(jnp.bfloat16)
        .reshape(EXPERTS, CAP, model_width)
    )
    gate_pre = jnp.einsum("ecd,edf->ecf", inputs, full_gate, preferred_element_type=jnp.float32)
    up_pre = jnp.einsum("ecd,edf->ecf", inputs, full_up, preferred_element_type=jnp.float32)
    inner_low = gelu_product(gate_pre, up_pre).astype(jnp.bfloat16)
    expert_out = jnp.einsum(
        "ecf,efd->ecd", inner_low, full_down, preferred_element_type=jnp.float32
    ).reshape(EXPERTS * CAP, model_width)
    logits = jnp.dot(normed_ffn_low, full_router, preferred_element_type=jnp.float32)
    weight_pair = gate_values(logits, route_ids, keep_mask)
    picked_rows = jnp.take(expert_out, slot_ids, axis=0)
    combined = jnp.sum(
        (picked_rows * weight_pair[:, None]).reshape(TOP, tok_rows, model_width), axis=0
    )
    output = (hidden + combined).astype(jnp.bfloat16).reshape(1, 1, tok_rows, model_width)
    back_keys, back_values = (far_keys, far_values)
    (
        back_query,
        back_key,
        back_value,
        back_out,
        back_gate,
        back_up,
        back_down,
        back_gain_attn,
        back_gain_ffn,
        back_router,
        back_bias,
    ) = gathered
    grad_final = cotangent[0, 0].astype(jnp.float32)
    grad_pair = jnp.where(
        keep_mask, jnp.sum(jnp.tile(grad_final, (TOP, 1)) * picked_rows, axis=-1), 0.0
    )
    slot_weight = jnp.dot(weight_pair, slot_hits, precision=precise)
    grad_expert_out = (
        (jnp.dot(dispatch, grad_final, precision=precise) * slot_weight[:, None])
        .astype(jnp.bfloat16)
        .reshape(EXPERTS, CAP, model_width)
    )
    grad_inner = jnp.einsum(
        "ecd,efd->ecf", grad_expert_out, back_down, preferred_element_type=jnp.float32
    )
    unused_e, inner_pull = jax.vjp(gelu_product, gate_pre, up_pre)
    grad_gate_pre, grad_up_pre = inner_pull(grad_inner)
    grad_gate_low = grad_gate_pre.astype(jnp.bfloat16)
    grad_up_low = grad_up_pre.astype(jnp.bfloat16)
    grad_gate_w = jnp.einsum(
        "ecd,ecf->edf", inputs, grad_gate_low, preferred_element_type=jnp.float32
    )
    grad_up_w = jnp.einsum("ecd,ecf->edf", inputs, grad_up_low, preferred_element_type=jnp.float32)
    grad_down_w = jnp.einsum(
        "ecf,ecd->efd", inner_low, grad_expert_out, preferred_element_type=jnp.float32
    )
    grad_inputs = jnp.einsum(
        "ecf,edf->ecd", grad_gate_low, back_gate, preferred_element_type=jnp.float32
    ) + jnp.einsum("ecf,edf->ecd", grad_up_low, back_up, preferred_element_type=jnp.float32)

    def gate_of_logits(logit_values):
        return gate_values(logit_values, route_ids, keep_mask)

    unused_f, gate_pull = jax.vjp(gate_of_logits, logits)
    (grad_logits,) = gate_pull(grad_pair)
    grad_router_w = jnp.dot(normed_ffn_low.astype(jnp.float32).T, grad_logits, precision=precise)
    grad_normed_ffn = jnp.dot(grad_logits, back_router.astype(jnp.float32).T, precision=precise)
    grad_normed_ffn = grad_normed_ffn + jnp.dot(
        dispatch.T, grad_inputs.reshape(EXPERTS * CAP, model_width), precision=precise
    )
    unused_g, ffn_norm_pull = jax.vjp(rms_norm, hidden, back_gain_ffn.astype(jnp.float32))
    grad_hidden_part, grad_gain_ffn_w = ffn_norm_pull(grad_normed_ffn)
    grad_hidden = grad_final + grad_hidden_part
    grad_hidden_low = grad_hidden.astype(jnp.bfloat16)
    grad_out_w = jnp.dot(mixed_low.T, grad_hidden_low, preferred_element_type=jnp.float32)
    grad_mixed = jnp.dot(grad_hidden_low, back_out.T, preferred_element_type=jnp.float32).astype(
        jnp.bfloat16
    )
    grad_mixed_heads = grad_mixed.reshape(tok_rows, head_count, head_width)
    row_delta = jnp.sum(grad_mixed_heads.astype(jnp.float32) * mixed_exact, axis=-1).T

    def grad_step(state_in, block_item):
        grad_query_acc, grad_reversed = state_in
        key_block, value_block, key_start = block_item
        key_total = key_block.shape[0]
        scores = block_scores(key_block, key_start)
        chances = jnp.exp(scores - row_max[..., None]) / row_sum[..., None]
        value_heads = value_block.reshape(-1, head_count, head_width)
        key_heads = key_block.reshape(-1, head_count, head_width)
        grad_chance = jnp.einsum(
            "qhd,khd->hqk", grad_mixed_heads, value_heads, preferred_element_type=jnp.float32
        )
        grad_value_block = jnp.einsum(
            "hqk,qhd->khd",
            chances.astype(jnp.bfloat16),
            grad_mixed_heads,
            preferred_element_type=jnp.float32,
        )
        grad_scores = chances * (grad_chance - row_delta[..., None])
        prompt_top, cont_top = window_starts(key_start)
        grad_reversed = add_window(
            grad_reversed,
            toeplitz_back(grad_scores[:, :prompt_rows], prompt_rows, key_total),
            prompt_top,
        )
        grad_reversed = add_window(
            grad_reversed,
            toeplitz_back(grad_scores[:, prompt_rows:], cont_rows, key_total),
            cont_top,
        )
        grad_scores_low = grad_scores.astype(jnp.bfloat16)
        grad_query_acc = grad_query_acc + score_scale * jnp.einsum(
            "hqk,khd->qhd", grad_scores_low, key_heads, preferred_element_type=jnp.float32
        )
        grad_key_block = score_scale * jnp.einsum(
            "hqk,qhd->khd", grad_scores_low, query_heads, preferred_element_type=jnp.float32
        )
        return (
            (grad_query_acc, grad_reversed),
            (grad_key_block.reshape(-1, model_width), grad_value_block.reshape(-1, model_width)),
        )

    start_grads = (
        jnp.zeros((tok_rows, head_count, head_width), jnp.float32),
        jnp.zeros((head_count, 2 * dist_count), jnp.float32),
    )
    (
        (grad_query_exact, grad_reversed),
        (far_grad_keys, far_grad_values),
        (near_grad_keys, near_grad_values),
    ) = sweep(
        grad_step,
        start_grads,
        (blocks_of(back_keys), blocks_of(back_values), prompt_starts),
        (key_low[prompt_rows:], value_low[prompt_rows:], local_start),
    )
    own_grad_keys, own_grad_values = (
        lax.psum_scatter(
            far_grad_keys.reshape(prompt_len, model_width), "ctx", scatter_dimension=0, tiled=True
        ),
        lax.psum_scatter(
            far_grad_values.reshape(prompt_len, model_width), "ctx", scatter_dimension=0, tiled=True
        ),
    )
    grad_key_low = jnp.concatenate([own_grad_keys, near_grad_keys], axis=0).astype(jnp.bfloat16)
    grad_value_low = jnp.concatenate([own_grad_values, near_grad_values], axis=0).astype(
        jnp.bfloat16
    )
    grad_query_low = grad_query_exact.reshape(tok_rows, model_width).astype(jnp.bfloat16)
    grad_query_w = jnp.dot(normed_attn_low.T, grad_query_low, preferred_element_type=jnp.float32)
    grad_key_w = jnp.dot(normed_attn_low.T, grad_key_low, preferred_element_type=jnp.float32)
    grad_value_w = jnp.dot(normed_attn_low.T, grad_value_low, preferred_element_type=jnp.float32)
    grad_normed_attn = jnp.dot(grad_query_low, back_query.T, preferred_element_type=jnp.float32)
    grad_normed_attn = grad_normed_attn + jnp.dot(
        grad_key_low, back_key.T, preferred_element_type=jnp.float32
    )
    grad_normed_attn = grad_normed_attn + jnp.dot(
        grad_value_low, back_value.T, preferred_element_type=jnp.float32
    )
    unused_h, attn_norm_pull = jax.vjp(rms_norm, source, back_gain_attn.astype(jnp.float32))
    grad_source_part, grad_gain_attn_w = attn_norm_pull(grad_normed_attn)
    grad_tokens = (
        (grad_hidden + grad_source_part).astype(jnp.bfloat16).reshape(1, 1, tok_rows, model_width)
    )
    grad_bias_rows = grad_reversed[:, :dist_count][:, ::-1]
    grad_bias_w = jnp.dot(bucket_onehot.T, grad_bias_rows.T, precision=precise)
    small_gain_attn, small_gain_ffn, small_router, small_bias = lax.psum(
        (grad_gain_attn_w, grad_gain_ffn_w, grad_router_w, grad_bias_w), "ctx"
    )
    row_parts = (
        lax.psum_scatter(
            grad_query_w.astype(jnp.bfloat16), "wt", scatter_dimension=0, tiled=True
        ).astype(jnp.float32),
        lax.psum_scatter(
            grad_key_w.astype(jnp.bfloat16), "wt", scatter_dimension=0, tiled=True
        ).astype(jnp.float32),
        lax.psum_scatter(
            grad_value_w.astype(jnp.bfloat16), "wt", scatter_dimension=0, tiled=True
        ).astype(jnp.float32),
        lax.psum_scatter(
            grad_out_w.astype(jnp.bfloat16), "wt", scatter_dimension=0, tiled=True
        ).astype(jnp.float32),
        lax.psum_scatter(
            grad_gate_w.astype(jnp.bfloat16), "wt", scatter_dimension=1, tiled=True
        ).astype(jnp.float32),
        lax.psum_scatter(
            grad_up_w.astype(jnp.bfloat16), "wt", scatter_dimension=1, tiled=True
        ).astype(jnp.float32),
        lax.psum_scatter(
            grad_down_w.astype(jnp.bfloat16), "wt", scatter_dimension=2, tiled=True
        ).astype(jnp.float32),
        lax.psum_scatter(
            small_gain_attn.astype(jnp.bfloat16), "wt", scatter_dimension=0, tiled=True
        ).astype(jnp.float32),
        lax.psum_scatter(
            small_gain_ffn.astype(jnp.bfloat16), "wt", scatter_dimension=0, tiled=True
        ).astype(jnp.float32),
        lax.psum_scatter(
            small_router.astype(jnp.bfloat16), "wt", scatter_dimension=0, tiled=True
        ).astype(jnp.float32),
        lax.psum_scatter(
            small_bias.astype(jnp.bfloat16), "wt", scatter_dimension=1, tiled=True
        ).astype(jnp.float32),
    )
    res_query, res_key, res_value, res_out, res_gate, res_up, res_down = (
        lax.psum_scatter(row_parts[0], "ctx", scatter_dimension=1, tiled=True),
        lax.psum_scatter(row_parts[1], "ctx", scatter_dimension=1, tiled=True),
        lax.psum_scatter(row_parts[2], "ctx", scatter_dimension=1, tiled=True),
        lax.psum_scatter(row_parts[3], "ctx", scatter_dimension=1, tiled=True),
        lax.psum_scatter(row_parts[4], "ctx", scatter_dimension=2, tiled=True),
        lax.psum_scatter(row_parts[5], "ctx", scatter_dimension=2, tiled=True),
        lax.psum_scatter(row_parts[6], "ctx", scatter_dimension=1, tiled=True),
    )
    res_gain_attn, res_gain_ffn, res_router, res_bias = (
        row_parts[7],
        row_parts[8],
        row_parts[9],
        row_parts[10],
    )
    return (
        output,
        grad_tokens,
        res_query,
        res_key,
        res_value,
        res_out,
        res_gain_attn,
        res_gain_ffn,
        res_router,
        res_bias,
        res_gate,
        res_up,
        res_down,
    )


def solution(mesh):
    return jax.shard_map(
        local,
        mesh=mesh,
        in_specs=(
            P("wt", "ctx", None, None),
            P("wt", "ctx", None, None),
            P("wt", "ctx"),
            P("wt", "ctx"),
            P("wt", "ctx"),
            P("wt", "ctx"),
            P("wt"),
            P("wt"),
            P("wt", None),
            P(None, "wt"),
            P(None, "wt", "ctx"),
            P(None, "wt", "ctx"),
            P(None, "ctx", "wt"),
            P(),
            P("wt", "ctx", None, None),
            P("wt", "ctx", None),
        ),
        out_specs=(
            P("wt", "ctx", None, None),
            P("wt", "ctx", None, None),
            P("wt", "ctx"),
            P("wt", "ctx"),
            P("wt", "ctx"),
            P("wt", "ctx"),
            P("wt"),
            P("wt"),
            P("wt", None),
            P(None, "wt"),
            P(None, "wt", "ctx"),
            P(None, "wt", "ctx"),
            P(None, "ctx", "wt"),
        ),
        check_vma=False,
    )
```

profile of v0, /device:TPU:0, one launch (start us, length us, event | category | flops | bytes accessed | tf_op | source)
XLA Modules:
  0.0 2363.7 jit_solution(10261924012226726133)
XLA Ops:
  7.3 31.2 %all_gather.61 = bf16[256,1024]{1,0:T(8,128)(2,1)} all-gather(bf16[256,128]{1,0:T(8,128)(2,1)} %param.20), channel_id=1, replica_groups=mesh['ctx'=8,'wt'=4] {'ctx'}, dimensions={1}, use_global_device_ids=true | all-gather | bytes 589824 | tf_op jit(solution)/shard_map/all_gather | solution.py:118
  38.5 28.8 %all_gather.66 = bf16[256,1024]{1,0:T(8,128)(2,1)} all-gather(bf16[256,128]{1,0:T(8,128)(2,1)} %param.19), channel_id=1, replica_groups=mesh['ctx'=8,'wt'=4] {'ctx'}, dimensions={1}, use_global_device_ids=true | all-gather | bytes 589824 | tf_op jit(solution)/shard_map/all_gather | solution.py:117
  111.6 31.2 %all_gather.70 = bf16[256,1024]{1,0:T(8,128)(2,1)} all-gather(bf16[256,128]{1,0:T(8,128)(2,1)S(1)} %copy-done.62), channel_id=1, replica_groups=mesh['ctx'=8,'wt'=4] {'ctx'}, dimensions={1}, use_global_device_ids=true | all-gather | bytes 589824 | tf_op jit(solution)/shard_map/all_gather | solution.py:119
  142.9 29.5 %all-gather.28.cloned.1.call-done = bf16[3,256,2816]{1,2,0:T(8,128)(2,1)} async-done(((bf16[3,256,352]{1,2,0:T(8,128)(2,1)}), bf16[3,256,2816]{1,2,0:T(8,128)(2,1)}) %all-gather.28.cloned.1.call-update) | async-done | bytes 4325392 | tf_op jit(solution)/shard_map/all_gather | solution.py:120
  179.0 69.2 %all-gather.32.cloned.1.call-done = bf16[3,256,2816]{1,2,0:T(8,128)(2,1)} async-done(((bf16[3,256,352]{1,2,0:T(8,128)(2,1)}), bf16[3,256,2816]{1,2,0:T(8,128)(2,1)}) %all-gather.32.cloned.1.call-update) | async-done | bytes 4325392 | tf_op jit(solution)/shard_map/all_gather | solution.py:121
  254.8 68.7 %all-gather.36.cloned.1.call-done = bf16[3,2816,256]{2,1,0:T(8,128)(2,1)} async-done(((bf16[3,352,256]{2,1,0:T(8,128)(2,1)}), bf16[3,2816,256]{2,1,0:T(8,128)(2,1)}) %all-gather.36.cloned.1.call-update) | async-done | bytes 4325392 | tf_op jit(solution)/shard_map/all_gather | solution.py:122
  519.7 44.9 %all-gather.30.cloned.1.call-done = bf16[3,1024,2816]{2,1,0:T(8,128)(2,1)} async-done(((bf16[3,256,2816]{2,1,0:T(8,128)(2,1)}), bf16[3,1024,2816]{2,1,0:T(8,128)(2,1)}) %all-gather.30.cloned.1.call-update) | async-done | bytes 17301520 | tf_op jit(solution)/shard_map/all_gather | solution.py:129
  578.2 97.8 %all-gather.34.cloned.1.call-done = bf16[3,1024,2816]{2,1,0:T(8,128)(2,1)} async-done(((bf16[3,256,2816]{2,1,0:T(8,128)(2,1)}), bf16[3,1024,2816]{2,1,0:T(8,128)(2,1)}) %all-gather.34.cloned.1.call-update) | async-done | bytes 17301520 | tf_op jit(solution)/shard_map/all_gather | solution.py:130
  689.3 101.7 %all-gather.38.cloned.1.call-done = bf16[3,2816,1024]{2,1,0:T(8,128)(2,1)} async-done(((bf16[3,2816,256]{2,1,0:T(8,128)(2,1)}), bf16[3,2816,1024]{2,1,0:T(8,128)(2,1)}) %all-gather.38.cloned.1.call-update) | async-done | bytes 17301520 | tf_op jit(solution)/shard_map/all_gather | solution.py:131
  839.0 33.0 %scatter_fusion = f32[320,3]{0,1:T(4,128)S(1)} fusion(f32[320,3]{0,1:T(4,128)S(1)} %broadcast_in_dim.211, s32[640]{0:T(1024)S(1)} %copy-done.8, f32[640]{0:T(1024)S(1)} %reshape.593), kind=kCustom, calls=%fused_computation.2 | custom fusion | flops 640 | bytes 12800 | tf_op jit(solution)/shard_map/transpose(jvp(jit(take_along_axis)))/scatter-add | solution.py:52
  1001.9 62.6 %reduce-scatter.54.cloned.1.call-done = f32[64,1024]{1,0:T(8,128)} async-done(((f32[512,1024]{1,0:T(8,128)}), f32[64,1024]{1,0:T(8,128)}) %reduce-scatter.54.cloned.1.call-update) | async-done | bytes 262160
  1210.9 35.1 %all-reduce.12 = (bf16[1024]{0:T(1024)(128)(2,1)S(1)}, bf16[1024]{0:T(1024)(128)(2,1)S(1)}, bf16[1024,3]{0,1:T(4,128)(2,1)S(1)}, bf16[32,16]{0,1:T(8,128)(2,1)S(1)}) all-reduce(f32[1024]{0:T(1024)S(1)} %get-tuple-element.179, f32[1024]{0:T(1024)S(1)} %copy-done.74, ...), channel_id=1, replica_groups=mesh['ctx'=8,'wt'=4] {'ctx'}, use_global_device_ids=true, to_apply=%region_28.29 | all-reduce | flops 5632 | bytes 33792 | tf_op jit(solution)/shard_map/psum | solution.py:417
  1267.5 59.8 %reduce-scatter.46.cloned.1.call-done = bf16[3,256,2816]{2,1,0:T(8,128)(2,1)} async-done(((bf16[3,1024,2816]{2,1,0:T(8,128)(2,1)}), bf16[3,256,2816]{2,1,0:T(8,128)(2,1)}) %reduce-scatter.46.cloned.1.call-update) | async-done | bytes 4325392 | tf_op jit(solution)/shard_map/reduce_scatter | solution.py:436
  1363.3 31.8 %reduce-scatter.40.cloned.1.call-done = bf16[256,1024]{1,0:T(8,128)(2,1)} async-done(((bf16[1024,1024]{1,0:T(8,128)(2,1)}), bf16[256,1024]{1,0:T(8,128)(2,1)}) %reduce-scatter.40.cloned.1.call-update) | async-done | bytes 524304 | tf_op jit(solution)/shard_map/reduce_scatter | solution.py:430
  1397.4 31.8 %reduce-scatter.32.cloned.1.call-done = bf16[256,1024]{1,0:T(8,128)(2,1)} async-done(((bf16[1024,1024]{1,0:T(8,128)(2,1)}), bf16[256,1024]{1,0:T(8,128)(2,1)}) %reduce-scatter.32.cloned.1.call-update) | async-done | bytes 524304 | tf_op jit(solution)/shard_map/reduce_scatter | solution.py:424
  1431.4 31.8 %reduce-scatter.36.cloned.1.call-done = bf16[256,1024]{1,0:T(8,128)(2,1)} async-done(((bf16[1024,1024]{1,0:T(8,128)(2,1)}), bf16[256,1024]{1,0:T(8,128)(2,1)}) %reduce-scatter.36.cloned.1.call-update) | async-done | bytes 524304 | tf_op jit(solution)/shard_map/reduce_scatter | solution.py:427
  1465.4 129.7 %reduce-scatter.48.cloned.1.call-done = bf16[3,2816,256]{2,1,0:T(8,128)(2,1)} async-done(((bf16[3,2816,1024]{2,1,0:T(8,128)(2,1)}), bf16[3,2816,256]{2,1,0:T(8,128)(2,1)}) %reduce-scatter.48.cloned.1.call-update) | async-done | bytes 4325392 | tf_op jit(solution)/shard_map/reduce_scatter | solution.py:439
  1619.9 155.6 %reduce-scatter.58.cloned.1.call-done = f32[352,768]{1,0:T(8,128)} async-done(((f32[2816,768]{1,0:T(8,128)}), f32[352,768]{1,0:T(8,128)}) %reduce-scatter.58.cloned.1.call-update) | async-done | bytes 1081360
  1778.4 153.6 %reduce-scatter.60.cloned.1.call-done = f32[352,768]{1,0:T(8,128)} async-done(((f32[2816,768]{1,0:T(8,128)}), f32[352,768]{1,0:T(8,128)}) %reduce-scatter.60.cloned.1.call-update) | async-done | bytes 1081360
  1934.8 64.0 %reduce-scatter.30.cloned.1.call-done = f32[256,128]{1,0:T(8,128)} async-done(((f32[256,1024]{1,0:T(8,128)}), f32[256,128]{1,0:T(8,128)}) %reduce-scatter.30.cloned.1.call-update) | async-done | bytes 131088 | tf_op jit(solution)/shard_map/reduce_scatter | solution.py:456
  1998.9 67.2 %reduce-scatter.42.cloned.1.call-done = f32[256,128]{1,0:T(8,128)} async-done(((f32[256,1024]{1,0:T(8,128)}), f32[256,128]{1,0:T(8,128)}) %reduce-scatter.42.cloned.1.call-update) | async-done | bytes 131088 | tf_op jit(solution)/shard_map/reduce_scatter | solution.py:459
  2066.0 66.7 %reduce-scatter.34.cloned.1.call-done = f32[256,128]{1,0:T(8,128)} async-done(((f32[256,1024]{1,0:T(8,128)}), f32[256,128]{1,0:T(8,128)}) %reduce-scatter.34.cloned.1.call-update) | async-done | bytes 131088 | tf_op jit(solution)/shard_map/reduce_scatter | solution.py:457
  2132.8 67.3 %reduce-scatter.38.cloned.1.call-done = f32[256,128]{1,0:T(8,128)} async-done(((f32[256,1024]{1,0:T(8,128)}), f32[256,128]{1,0:T(8,128)}) %reduce-scatter.38.cloned.1.call-update) | async-done | bytes 131088 | tf_op jit(solution)/shard_map/reduce_scatter | solution.py:458
  2200.1 156.7 %reduce-scatter.50.cloned.1.call-done = f32[3,352,256]{2,1,0:T(8,128)} async-done(((f32[3,2816,256]{2,1,0:T(8,128)}), f32[3,352,256]{2,1,0:T(8,128)}) %reduce-scatter.50.cloned.1.call-update) | async-done | bytes 1081360 | tf_op jit(solution)/shard_map/reduce_scatter | solution.py:462
  (482 shorter events, 696.5 us)
Async XLA Ops:
  68.7 254.8 %all-gather.36.cloned.1.call-start = ((), (), s32[]{:S(2)}) async-start(), calls=%async_computation.27 | async-start | bytes 4866048 | tf_op jit(solution)/shard_map/all_gather | solution.py:122
  69.3 387.6 %all-gather.20.cloned.1.call-start = ((), (), s32[]{:S(2)}) async-start(), calls=%async_computation.19 | async-start | bytes 2621440 | tf_op jit(solution)/shard_map/all_gather | solution.py:125
  97.5 374.9 %all-gather.18.cloned.1.call-start = ((), (), s32[]{:S(2)}) async-start(), calls=%async_computation.18 | async-start | bytes 1179648 | tf_op jit(solution)/shard_map/all_gather | solution.py:166
  107.5 367.2 %all-gather.24.cloned.1.call-start = ((), (), s32[]{:S(2)}) async-start(), calls=%async_computation.21 | async-start | bytes 1179648 | tf_op jit(solution)/shard_map/all_gather | solution.py:165
  111.6 385.2 %all-gather.26.cloned.1.call-start = ((), (), s32[]{:S(2)}) async-start(), calls=%async_computation.22 | async-start | bytes 2621440 | tf_op jit(solution)/shard_map/all_gather | solution.py:128
  142.9 421.7 %all-gather.30.cloned.1.call-start = ((), (), s32[]{:S(2)}) async-start(), calls=%async_computation.24 | async-start | bytes 21626880 | tf_op jit(solution)/shard_map/all_gather | solution.py:129
  179.0 496.9 %all-gather.34.cloned.1.call-start = ((), (), s32[]{:S(2)}) async-start(), calls=%async_computation.26 | async-start | bytes 21626880 | tf_op jit(solution)/shard_map/all_gather | solution.py:130
  254.7 536.3 %all-gather.38.cloned.1.call-start = ((), (), s32[]{:S(2)}) async-start(), calls=%async_computation.28 | async-start | bytes 21626880 | tf_op jit(solution)/shard_map/all_gather | solution.py:131
  323.5 670.7 %reduce-scatter.52.cloned.1.call-start = ((), (), s32[]{:S(2)}) async-start(), calls=%async_computation.41 | async-start | bytes 2359296
  934.5 312.5 %reduce-scatter.44.cloned.1.call-start = ((), (), s32[]{:S(2)}) async-start(), calls=%async_computation.37 | async-start | bytes 21626880 | tf_op jit(solution)/shard_map/reduce_scatter | solution.py:433
  949.9 377.4 %reduce-scatter.46.cloned.1.call-start = ((), (), s32[]{:S(2)}) async-start(), calls=%async_computation.38 | async-start | bytes 21626880 | tf_op jit(solution)/shard_map/reduce_scatter | solution.py:436
  965.1 396.1 %reduce-scatter.28.cloned.1.call-start = ((), (), s32[]{:S(2)}) async-start(), calls=%async_computation.29 | async-start | bytes 2621440 | tf_op jit(solution)/shard_map/reduce_scatter | solution.py:421
  984.1 411.1 %reduce-scatter.40.cloned.1.call-start = ((), (), s32[]{:S(2)}) async-start(), calls=%async_computation.35 | async-start | bytes 2621440 | tf_op jit(solution)/shard_map/reduce_scatter | solution.py:430
  987.9 441.3 %reduce-scatter.32.cloned.1.call-start = ((), (), s32[]{:S(2)}) async-start(), calls=%async_computation.31 | async-start | bytes 2621440 | tf_op jit(solution)/shard_map/reduce_scatter | solution.py:424
  1000.4 462.8 %reduce-scatter.36.cloned.1.call-start = ((), (), s32[]{:S(2)}) async-start(), calls=%async_computation.33 | async-start | bytes 2621440 | tf_op jit(solution)/shard_map/reduce_scatter | solution.py:427
  1069.9 525.2 %reduce-scatter.48.cloned.1.call-start = ((), (), s32[]{:S(2)}) async-start(), calls=%async_computation.39 | async-start | bytes 21626880 | tf_op jit(solution)/shard_map/reduce_scatter | solution.py:439
  1088.5 529.8 %reduce-scatter.56.cloned.1.call-start = ((), (), s32[]{:S(2)}) async-start(), calls=%async_computation.43 | async-start | bytes 327680
  1246.9 528.6 %reduce-scatter.58.cloned.1.call-start = ((), (), s32[]{:S(2)}) async-start(), calls=%async_computation.44 | async-start | bytes 9732096
  1267.4 664.5 %reduce-scatter.60.cloned.1.call-start = ((), (), s32[]{:S(2)}) async-start(), calls=%async_computation.45 | async-start | bytes 9732096
  1347.4 651.5 %reduce-scatter.30.cloned.1.call-start = ((), (), s32[]{:S(2)}) async-start(), calls=%async_computation.30 | async-start | bytes 1179648 | tf_op jit(solution)/shard_map/reduce_scatter | solution.py:456
  1363.3 702.8 %reduce-scatter.42.cloned.1.call-start = ((), (), s32[]{:S(2)}) async-start(), calls=%async_computation.36 | async-start | bytes 1179648 | tf_op jit(solution)/shard_map/reduce_scatter | solution.py:459
  1397.3 735.4 %reduce-scatter.34.cloned.1.call-start = ((), (), s32[]{:S(2)}) async-start(), calls=%async_computation.32 | async-start | bytes 1179648 | tf_op jit(solution)/shard_map/reduce_scatter | solution.py:457
  1431.3 768.7 %reduce-scatter.38.cloned.1.call-start = ((), (), s32[]{:S(2)}) async-start(), calls=%async_computation.34 | async-start | bytes 1179648 | tf_op jit(solution)/shard_map/reduce_scatter | solution.py:458
  1465.3 891.5 %reduce-scatter.50.cloned.1.call-start = ((), (), s32[]{:S(2)}) async-start(), calls=%async_computation.40 | async-start | bytes 9732096 | tf_op jit(solution)/shard_map/reduce_scatter | solution.py:462
  (109 other events, 3761.1 us)
Sparse Core Ops, SparseCore 0:
  90.6 81.8 all-gather.27
  174.5 73.6 all-gather.31
  250.2 73.2 all-gather.35
  348.5 40.1 all-gather.17
  391.4 38.8 all-gather.23
  454.8 109.7 all-gather.29
  566.1 109.7 all-gather.33
  677.3 113.6 all-gather.37
  926.5 67.6 reduce-scatter.51
  997.6 66.8 reduce-scatter.53
  1067.0 128.2 reduce-scatter.43
  1197.9 129.2 reduce-scatter.45
  1329.7 31.4 reduce-scatter.27
  1363.7 31.4 reduce-scatter.39
  1397.7 31.4 reduce-scatter.31
  1431.7 31.4 reduce-scatter.35
  1465.8 129.2 reduce-scatter.47
  1622.0 153.4 reduce-scatter.57
  1779.4 152.5 reduce-scatter.59
  1935.9 62.8 reduce-scatter.29
  2003.1 62.9 reduce-scatter.41
  2069.9 62.8 reduce-scatter.33
  2137.1 62.8 reduce-scatter.37
  2204.2 152.4 reduce-scatter.49
  (5 shorter events, 104.0 us)
where the time goes:
time: 2370 us; the launch traced here: 2360 us
  waiting for transfers between devices  1510 us (64%)
  local copies, waits for them, and re-layouts  334 us (14%)
  matrix products  239 us (10%)
  blocking collectives  181 us (8%)
  other arithmetic  76.4 us (3%)
    unnamed x34, waiting for transfers between devices  382 us
    reduce_scatter x1, waiting for transfers between devices, local(): lax.psum_scatter(row_parts[6], 'ctx', scatter_dimension=1, tiled=True)  157 us
    reduce_scatter x1, waiting for transfers between devices, local(): lax.psum_scatter(grad_down_w.astype(jnp.bfloat16), 'wt', scatter_dimensio...  130 us
    unnamed x225, local copies, waits for them, and re-layouts  112 us
    all_gather x1, waiting for transfers between devices, local(): lax.all_gather(cols_down, 'wt', axis=2, tiled=True)  102 us
    all_gather x1, waiting for transfers between devices, local(): lax.all_gather(cols_up, 'wt', axis=1, tiled=True)  97.8 us
    all_gather x1, waiting for transfers between devices, local(): lax.all_gather(exp_up, 'ctx', axis=2, tiled=True)  69.2 us
    all_gather x1, waiting for transfers between devices, local(): lax.all_gather(exp_down, 'ctx', axis=1, tiled=True)  68.7 us
  transfers between devices with their start and end apart: 29, of which 22 were waited for; matrix products, arithmetic and copies ran while one was open for 21% of the time, Pallas kernels for 0%

commit v1 on v0

--- a/solution.py
+++ b/solution.py
@@ -1,6 +1,10 @@
+import functools
+
 import jax
 import jax.numpy as jnp
 from jax import lax
+from jax.experimental import pallas as pl
+from jax.experimental.pallas import tpu as pltpu
 from jax.sharding import PartitionSpec as P
 
 HEADS = 16
@@ -484,9 +488,588 @@
     )
 
 
+BF = jnp.bfloat16
+F32 = jnp.float32
+FAST_CTX = 8
+FAST_WT = 4
+NEG = -1e30
+
+SWAP_Y = [(i, i ^ 1) for i in range(8)]
+UP_Z = [(i, i + 2) for i in range(6)]
+DOWN_Z = [(i, i - 2) for i in range(2, 8)]
+SWAP_C = [(i, i ^ 1) for i in range(4)]
+SWAP_X = [(i, i ^ 2) for i in range(4)]
+
+
+def move_y(v):
+    return lax.ppermute(v, "ctx", SWAP_Y)
+
+
+def move_x(v):
+    return lax.ppermute(v, "wt", SWAP_X)
+
+
+def move_c(v):
+    return lax.ppermute(v, "wt", SWAP_C)
+
+
+def up_z(v):
+    return lax.ppermute(v, "ctx", UP_Z)
+
+
+def down_z(v):
+    return lax.ppermute(v, "ctx", DOWN_Z)
+
+
+def shift_z(v, s):
+    return lax.ppermute(v, "ctx", [(i, (i + 2 * s) % 8) for i in range(8)])
+
+
+def after(v, *deps):
+    return lax.optimization_barrier((v,) + deps)[0]
+
+
+def dot_nt(a, b):
+    return lax.dot_general(a, b, (((1,), (1,)), ((), ())), preferred_element_type=F32)
+
+
+def dot_tn(a, b):
+    return lax.dot_general(a, b, (((0,), (0,)), ((), ())), preferred_element_type=F32)
+
+
+def dot_nn(a, b):
+    return jnp.dot(a, b, preferred_element_type=F32)
+
+
+def params(limit=56 * 2**20):
+    return pltpu.CompilerParams(vmem_limit_bytes=limit)
+
+
+ANY = pl.BlockSpec(memory_space=pl.ANY)
+SMEM = pl.BlockSpec(memory_space=pltpu.SMEM)
+
+
+def spread_all(unit):
+    pieces = []
+    for s in range(4):
+        v = unit if s == 0 else shift_z(unit, s)
+        if s % 2 == 0:
+            a = move_y(v)
+            quad = {(0, 0): v, (1, 0): a, (0, 1): move_x(v), (1, 1): move_x(a)}
+        else:
+            b = move_x(v)
+            quad = {(0, 0): v, (0, 1): b, (1, 0): move_y(v), (1, 1): move_y(b)}
+        for ry in range(2):
+            for rx in range(2):
+                piece = quad[(ry, rx)]
+                pieces.append(((s, ry, rx, 0), piece))
+                pieces.append(((s, ry, rx, 1), move_c(piece)))
+    return pieces
+
+
+def place_kernel(keys, idx, *refs):
+    count = len(keys)
+    ins, wkv, wq, wo, sem = refs[:count], refs[count], refs[count + 1], refs[count + 2], refs[count + 3]
+    z, y, x, c = idx[0], idx[1], idx[2], idx[3]
+    copies = []
+    for n, (s, ry, rx, rc) in enumerate(keys):
+        row = pl.multiple_of(((x ^ rx) * 2 + (c ^ rc)) * 256, 256)
+        col = pl.multiple_of((lax.rem(z + 4 - s, 4) * 2 + (y ^ ry)) * 128, 128)
+        rows, cols = pl.ds(row, 256), pl.ds(col, 128)
+        copies.append(pltpu.make_async_copy(ins[n].at[0], wq.at[rows, cols], sem.at[n, 0]))
+        copies.append(pltpu.make_async_copy(ins[n].at[pl.ds(1, 2)], wkv.at[:, rows, cols], sem.at[n, 1]))
+        copies.append(pltpu.make_async_copy(ins[n].at[3], wo.at[rows, cols], sem.at[n, 2]))
+    for copy in copies:
+        copy.start()
+    for copy in copies:
+        copy.wait()
+
+
+def place_weights(idx, pieces):
+    keys = [k for k, _ in pieces]
+    return pl.pallas_call(
+        functools.partial(place_kernel, keys),
+        out_shape=(
+            jax.ShapeDtypeStruct((2, 1024, 1024), BF),
+            jax.ShapeDtypeStruct((1024, 1024), BF),
+            jax.ShapeDtypeStruct((1024, 1024), BF),
+        ),
+        in_specs=[SMEM] + [ANY] * len(keys),
+        out_specs=(ANY, ANY, ANY),
+        scratch_shapes=[pltpu.SemaphoreType.DMA((len(keys), 3))],
+        compiler_params=params(),
+    )(idx, *[v for _, v in pieces])
+
+
+def attend_kernel(w_ref, q_ref, k_ref, v_ref, p_ref, o_ref, bc_ref, bp_ref):
+    q, k, v = q_ref[...], k_ref[...], v_ref[...]
+    lane = lax.broadcasted_iota(jnp.int32, (1, 128), 1)
+    outs = []
+    for h in range(2):
+        base_c, base_p = w_ref[h, 0], w_ref[h, 1]
+        for a in range(32):
+            bc_ref[8 * a : 8 * a + 8, :] = pltpu.roll(base_c, 1024 - (248 - 8 * a), 1)[:, :768]
+        for a in range(8):
+            shift = 56 - 8 * a
+            bp_ref[8 * a : 8 * a + 8, :] = (pltpu.roll(base_p, 1024 - shift, 1) if shift else base_p)[:, :512]
+        mine = (lane < 64) if h == 0 else (lane >= 64)
+        qh = jnp.where(mine, q, jnp.zeros_like(q))
+        sc = dot_nt(qh[64:], k) * 0.125 + bc_ref[...]
+        sp = dot_nt(qh[:64], k[:512]) * 0.125 + bp_ref[...]
+
+        def soft(s):
+            e = jnp.exp(s - jnp.max(s, axis=-1, keepdims=True))
+            return (e / jnp.sum(e, axis=-1, keepdims=True)).astype(BF)
+
+        pc, pp = soft(sc), soft(sp)
+        p_ref[h, 64:, :] = pc
+        p_ref[h, :64, :512] = pp
+        p_ref[h, :64, 512:] = jnp.zeros((64, 256), BF)
+        outs.append(jnp.concatenate([dot_nn(pp, v[:512]), dot_nn(pc, v)], axis=0))
+    o_ref[...] = jnp.where(lane < 64, outs[0], outs[1]).astype(BF)
+
+
+def attend(bias_rows, q, k, v):
+    rows, keys = q.shape[0], k.shape[0]
+    return pl.pallas_call(
+        attend_kernel,
+        grid=(8,),
+        out_shape=(
+            jax.ShapeDtypeStruct((16, rows, keys), BF),
+            jax.ShapeDtypeStruct((rows, 1024), BF),
+        ),
+        in_specs=[
+            pl.BlockSpec((2, 2, 8, 1024), lambda j: (j, 0, 0, 0)),
+            pl.BlockSpec((rows, 128), lambda j: (0, j)),
+            pl.BlockSpec((keys, 128), lambda j: (0, j)),
+            pl.BlockSpec((keys, 128), lambda j: (0, j)),
+        ],
+        out_specs=(
+            pl.BlockSpec((2, rows, keys), lambda j: (j, 0, 0)),
+            pl.BlockSpec((rows, 128), lambda j: (0, j)),
+        ),
+        scratch_shapes=[pltpu.VMEM((256, 768), F32), pltpu.VMEM((64, 512), F32)],
+        compiler_params=params(),
+        cost_estimate=pl.CostEstimate(flops=8 * 320 * 768 * 512, bytes_accessed=14 * 2**20, transcendentals=2**22),
+    )(bias_rows, q, k, v)
+
+
+def attend_back_kernel(p_ref, q_ref, k_ref, v_ref, g_ref, dq_ref, dk_ref, dv_ref, db_ref):
+    q, k, v, g = q_ref[...], k_ref[...], v_ref[...], g_ref[...]
+    lane = lax.broadcasted_iota(jnp.int32, (1, 128), 1)
+    parts = []
+    for h in range(2):
+        mine = (lane < 64) if h == 0 else (lane >= 64)
+        gh = jnp.where(mine, g, jnp.zeros_like(g))
+        p = p_ref[h]
+        pf = p.astype(F32)
+        dp = dot_nt(gh, v)
+        delta = jnp.sum(pf * dp, axis=-1, keepdims=True)
+        ds = pf * (dp - delta)
+        low = ds.astype(BF)
+        acc_c = jnp.zeros((8, 1024), F32)
+        for a in range(32):
+            part = jnp.concatenate([ds[64 + 8 * a : 72 + 8 * a], jnp.zeros((8, 256), F32)], axis=1)
+            acc_c = acc_c + pltpu.roll(part, 248 - 8 * a, 1) if a < 31 else acc_c + part
+        acc_p = jnp.zeros((8, 1024), F32)
+        for a in range(8):
+            part = jnp.concatenate([ds[8 * a : 8 * a + 8, :512], jnp.zeros((8, 512), F32)], axis=1)
+            acc_p = acc_p + (pltpu.roll(part, 56 - 8 * a, 1) if a < 7 else part)
+        db_ref[h, 0] = acc_c
+        db_ref[h, 1] = acc_p
+        parts.append((dot_nn(low, k) * 0.125, dot_tn(low, q) * 0.125, dot_tn(p, g)))
+    for n, ref in enumerate((dq_ref, dk_ref, dv_ref)):
+        ref[...] = jnp.where(lane < 64, parts[0][n], parts[1][n]).astype(BF)
+
+
+def attend_back(p, q, k, v, g):
+    rows, keys = q.shape[0], k.shape[0]
+    head = lambda n: pl.BlockSpec((n, 128), lambda j: (0, j))
+    return pl.pallas_call(
+        attend_back_kernel,
+        grid=(8,),
+        out_shape=(
+            jax.ShapeDtypeStruct((rows, 1024), BF),
+            jax.ShapeDtypeStruct((keys, 1024), BF),
+            jax.ShapeDtypeStruct((keys, 1024), BF),
+            jax.ShapeDtypeStruct((16, 2, 8, 1024), F32),
+        ),
+        in_specs=[
+            pl.BlockSpec((2, rows, keys), lambda j: (j, 0, 0)),
+            head(rows),
+            head(keys),
+            head(keys),
+            head(rows),
+        ],
+        out_specs=(
+            head(rows),
+            head(keys),
+            head(keys),
+            pl.BlockSpec((2, 2, 8, 1024), lambda j: (j, 0, 0, 0)),
+        ),
+        compiler_params=params(),
+        cost_estimate=pl.CostEstimate(flops=20 * 320 * 768 * 512, bytes_accessed=14 * 2**20, transcendentals=0),
+    )(p, q, k, v, g)
+
+
+def bias_windows(bias_rows, ctx_index):
+    rev = jnp.concatenate([bias_rows[:, ::-1], jnp.full((16, 1152), NEG, F32)], axis=1)
+    cont = jnp.stack([rev[:, 7 - s : 7 - s + 1024] for s in range(8)], axis=1)
+    tail = lax.dynamic_slice_in_dim(rev, 704 - 64 * ctx_index, 1040, 1)
+    prompt = jnp.stack([tail[:, 7 - s : 7 - s + 1024] for s in range(8)], axis=1)
+    return jnp.stack([cont, prompt], axis=1)
+
+
+def bias_windows_back(grad, ctx_index):
+    def gather(part):
+        total = jnp.zeros((16, 1040), F32)
+        for s in range(8):
+            total = total + jnp.pad(part[:, s], ((0, 0), (7 - s, 9 + s)))
+        return total
+
+    wide = jnp.pad(gather(grad[:, 0]), ((0, 0), (0, 880)))
+    prompt = gather(grad[:, 1])
+    start = 704 - 64 * ctx_index
+    moved = lax.dynamic_update_slice_in_dim(jnp.zeros((16, 1920), F32), prompt, start, 1)
+    return (wide + moved)[:, :768][:, ::-1]
+
+
+ORDER = [(half, rc, ry, rx) for half in range(2) for rc in range(2) for ry in range(2) for rx in range(2)]
+
+
+def spread_plane(v):
+    half = v.shape[0] // 2
+    a, b = v[:half], v[half:]
+    ay, bx = move_y(a), move_x(b)
+    ax, by = move_x(a), move_y(b)
+    ayx, bxy = move_x(ay), move_y(bx)
+    near = {(0, 0, 0): a, (0, 1, 0): ay, (0, 0, 1): ax, (0, 1, 1): ayx, (1, 0, 0): b, (1, 0, 1): bx, (1, 1, 0): by, (1, 1, 1): bxy}
+    return [near[(h, ry, rx)] if rc == 0 else move_c(near[(h, ry, rx)]) for h, rc, ry, rx in ORDER]
+
+
+def add_low(a, b):
+    return (a.astype(F32) + b.astype(F32)).astype(BF)
+
+
+def collect_plane(v):
+    rows = v.shape[0] // 16
+    w = v.reshape(2, 2, 4, rows, v.shape[1])
+    sums = []
+    for h in range(2):
+        sums.append(add_low(w[h, 0], move_c(w[h, 1])))
+    a, b = sums
+    sy = add_low(a[2], move_x(a[3]))
+    sx = add_low(b[1], move_y(b[3]))
+    ax, by = move_x(a[1]), move_y(b[2])
+    ay, bx = move_y(sy), move_x(sx)
+    f = lambda t: t.astype(F32)
+    return jnp.concatenate([f(a[0]) + f(ax) + f(ay), f(b[0]) + f(by) + f(bx)], axis=0)
+
+
+def expert_kernel(expert, first, last, *refs):
+    refs = list(refs)
+    idx, x_ref, g_ref, m_ref = refs[:4]
+    srcs = refs[4:11]
+    at = 11
+    if not first:
+        out_prev, dx_prev = refs[at : at + 2]
+        at += 2
+    if last:
+        s0_ref, s1_ref = refs[at : at + 2]
+        at += 2
+    out_ref, dx_ref, dh_ref, win_ref, s_ref, w_scr, sem = refs[at:]
+    z = idx[0]
+
+    @pl.when(pl.program_id(0) == 0)
+    def _():
+        def copy(n, slot):
+            rows = pl.ds(pl.multiple_of(slot * 96, 96), 96)
+            return pltpu.make_async_copy(srcs[n], w_scr.at[:, rows, :], sem.at[n])
+
+        plan = [(0, z, None)]
+        for s in range(1, 4):
+            plan.append((s, z + s, z + s <= 3))
+            plan.append((3 + s, z - s, z - s >= 0))
+        for act in ("start", "wait"):
+            for n, slot, ok in plan:
+                if ok is None:
+                    getattr(copy(n, slot), act)()
+                else:
+
+                    @pl.when(ok)
+                    def _(n=n, slot=slot, act=act):
+                        getattr(copy(n, slot), act)()
+
+    x, g = x_ref[...], g_ref[...]
+    w_gu = w_scr[0:2].reshape(768, 1024)
+    w_d = w_scr[2]
+    gu = dot_nt(x, w_gu)
+    gi = dot_nt(g, w_d)
+    gate, up = gu[:, :384], gu[:, 384:]
+    l = [gate[:, 88 + n : 89 + n] for n in range(3)]
+    top = jnp.maximum(jnp.maximum(l[0], l[1]), l[2])
+    ex = [jnp.exp(v - top) for v in l]
+    inv = 1.0 / (ex[0] + ex[1] + ex[2])
+    p = [v * inv for v in ex]
+    m = m_ref[...]
+    keep = m[:, expert : expert + 1]
+    w = p[expert] * keep
+    sq = gate * gate
+    th = jnp.tanh(0.7978845608028654 * gate * (1.0 + 0.044715 * sq))
+    half1 = 0.5 + 0.5 * th
+    act = gate * half1
+    dact = half1 + (0.5 * gate) * (1.0 - th * th) * (0.7978845608028654 + 0.10703222440890037 * sq)
+    inner = (act * up).astype(BF).astype(F32)
+    s = jnp.sum(inner * gi, axis=-1, keepdims=True) * keep
+    gin = gi * w
+    dg = gin * up * dact
+    du = gin * act
+    if last:
+        ss = [s0_ref[...][:, 0:1], s1_ref[...][:, 0:1], s]
+        dot = p[0] * ss[0] + p[1] * ss[1] + p[2] * ss[2]
+        lane = lax.broadcasted_iota(jnp.int32, (1, 384), 1)
+        for n in range(3):
+            dg = jnp.where(lane == 88 + n, p[n] * (ss[n] - dot), dg)
+    win = (inner * w).astype(BF)
+    dh = jnp.concatenate([dg.astype(BF), du.astype(BF)], axis=1)
+    dh_ref[...] = dh
+    win_ref[...] = win
+    s_ref[...] = jnp.broadcast_to(s, s_ref.shape)
+    out = dot_nn(win, w_d)
+    dx = dot_nn(dh, w_gu)
+    if not first:
+        out = out + out_prev[...].astype(F32)
+        dx = dx + dx_prev[...].astype(F32)
+    out_ref[...] = out.astype(BF)
+    dx_ref[...] = dx.astype(BF)
+
+
+def expert_call(expert, idx, x, g, m, srcs, prev, s_prev, tile=512):
+    total = x.shape[0]
+    first, last = expert == 0, expert == 2
+    row = lambda n: pl.BlockSpec((tile, n), lambda i: (i, 0))
+    ins = [idx, x, g, m, *srcs]
+    specs = [SMEM, row(1024), row(1024), row(8)] + [ANY] * 7
+    if not first:
+        ins += list(prev)
+        specs += [row(1024), row(1024)]
+    if last:
+        ins += list(s_prev)
+        specs += [row(8), row(8)]
+    return pl.pallas_call(
+        functools.partial(expert_kernel, expert, first, last),
+        grid=(total // tile,),
+        out_shape=(
+            jax.ShapeDtypeStruct((total, 1024), BF),
+            jax.ShapeDtypeStruct((total, 1024), BF),
+            jax.ShapeDtypeStruct((total, 768), BF),
+            jax.ShapeDtypeStruct((total, 384), BF),
+            jax.ShapeDtypeStruct((total, 8), F32),
+        ),
+        in_specs=specs,
+        out_specs=(row(1024), row(1024), row(768), row(384), row(8)),
+        scratch_shapes=[pltpu.VMEM((3, 384, 1024), BF), pltpu.SemaphoreType.DMA((7,))],
+        compiler_params=params(),
+        cost_estimate=pl.CostEstimate(
+            flops=2 * total * 1024 * 384 * 6, bytes_accessed=total * 1024 * 16, transcendentals=total * 384
+        ),
+    )(*ins)
+
+
+def line_spread(v):
+    a1, b1 = down_z(v), up_z(v)
+    a2, b2 = down_z(a1), up_z(b1)
+    a3, b3 = down_z(a2), up_z(b2)
+    return [v, a1, a2, a3, b1, b2, b3]
+
+
+def line_collect(part_of, z):
+    at = lambda n: part_of(jnp.clip(z + n, 0, 3))
+    d = down_z(at(-3))
+    u = up_z(at(3))
+    d = down_z(add_low(at(-2), d))
+    u = up_z(add_low(at(2), u))
+    d = down_z(add_low(at(-1), d))
+    u = up_z(add_low(at(1), u))
+    return (at(0).astype(F32) + d.astype(F32) + u.astype(F32)).astype(BF)
+
+
+def trade_wt(v, wt_index):
+    at = lambda r: lax.dynamic_index_in_dim(v, wt_index ^ r, 0, keepdims=False)
+    got = [at(0), move_c(at(1)), move_x(at(2)), lax.ppermute(at(3), "wt", [(i, i ^ 3) for i in range(4)])]
+    return jnp.take(jnp.stack(got), jnp.arange(4, dtype=jnp.int32) ^ wt_index, axis=0)
+
+
+def sum_all(v):
+    v = v + move_c(v)
+    v = v + move_x(v)
+    v = v + move_y(v)
+    v = v + lax.ppermute(v, "ctx", [(i, i ^ 2) for i in range(8)])
+    return v + lax.ppermute(v, "ctx", [(i, i ^ 4) for i in range(8)])
+
+
+def norm_parts(values):
+    return values * lax.rsqrt(jnp.mean(values * values, axis=-1, keepdims=True) + epsilon)
+
+
+def local_fast(
+    tokens, cotangent, w_query, w_key, w_value, w_out, gain_attn, gain_ffn, w_router, rel_bias,
+    exp_gate, exp_up, exp_down, bucket_table, expert_ids, priority,
+):
+    ctx_index = lax.axis_index("ctx").astype(jnp.int32)
+    wt_index = lax.axis_index("wt").astype(jnp.int32)
+    z, y, x, c = ctx_index // 2, ctx_index % 2, wt_index // 2, wt_index % 2
+    idx = jnp.stack([z, y, x, c])
+    rows_own = tokens[0, 0]
+
+    packed = jnp.concatenate(
+        [gain_attn[None], gain_ffn[None], w_router.T, jnp.pad(rel_bias.reshape(1, 128), ((0, 0), (0, 128))),
+         jnp.zeros((2, 256), BF)], axis=0
+    )
+    small = lax.all_gather(packed, "wt", axis=0, tiled=False)
+    gain_attn_f = small[:, 0].reshape(1024).astype(F32)
+    gain_ffn_f = small[:, 1].reshape(1024).astype(F32)
+    bias_f = small[:, 5, :128].reshape(4, 32, 4).transpose(1, 0, 2).reshape(32, 16).astype(F32)
+
+    unit = jnp.stack([w_query, w_key, w_value, w_out])
+    w_kv, w_q, w_o = place_weights(idx, spread_all(unit))
+
+    prompt_own = rows_own[:64]
+    group = [prompt_own] + [shift_z(prompt_own, s) for s in (3, 2, 1)]
+    stack = jnp.stack([jnp.stack([v, move_y(v)]) for v in group])
+    stack = lax.dynamic_slice_in_dim(jnp.concatenate([stack, stack], axis=0), (4 - z) % 4, 4, 0)
+    stack = lax.dynamic_slice_in_dim(jnp.concatenate([stack, stack[:, :1]], axis=1), y, 2, 1)
+    prompts = stack.reshape(512, 1024)
+
+    ids, rank = expert_ids[0, 0], priority[0, 0]
+    expert = ids.T.reshape(-1)
+    rank_key = (jnp.arange(TOP, dtype=jnp.int32)[:, None] * 320 + rank[None, :]).reshape(-1)
+    earlier = (expert[:, None] == expert[None, :]) & (rank_key[None, :] < rank_key[:, None])
+    keep = (jnp.sum(earlier.astype(jnp.int32), axis=1) < CAP).reshape(TOP, 320)
+    hold = jnp.sum(
+        jnp.where((ids.T[:, :, None] == jnp.arange(EXPERTS, dtype=jnp.int32)) & keep[:, :, None], 1.0, 0.0), axis=0
+    )
+    marks = jnp.pad(hold.reshape(2, 1, 480), ((0, 0), (0, 15), (0, 544))).astype(BF)
+    cot = cotangent[0, 0]
+    cot_marked = jnp.concatenate([cot[:160], marks[0], cot[160:], marks[1]], axis=0)
+
+    def pieces(v):
+        return jnp.pad(v.reshape(3, 4, 88, 256), ((0, 0), (0, 0), (0, 8), (0, 0)))
+
+    gate_t, up_t = exp_gate.transpose(0, 2, 1), exp_up.transpose(0, 2, 1)
+    gate_p = pieces(gate_t)
+    router_rows = jnp.broadcast_to(
+        jnp.pad(w_router.T, ((0, 5), (0, 0)))[None, None], (3, 4, 8, 256)
+    )
+    gate_p = jnp.concatenate([gate_p[:, :, :88], router_rows], axis=2)
+    share = jnp.stack([gate_p, pieces(up_t), pieces(exp_down)], axis=1).transpose(2, 0, 1, 3, 4)
+    share = trade_wt(share, wt_index).transpose(1, 2, 3, 0, 4).reshape(3, 3, 96, 1024)
+    spread = [line_spread(share[e]) for e in range(3)]
+
+    source = rows_own.astype(F32)
+    own_low = (norm_parts(source) * gain_attn_f).astype(BF)
+    source_all = jnp.concatenate([prompts.astype(F32), source[64:]], axis=0)
+    unit_all = norm_parts(source_all)
+    all_low = (unit_all * gain_attn_f).astype(BF)
+    q = dot_nn(own_low, w_q).astype(BF)
+    k = dot_nn(all_low, w_kv[0]).astype(BF)
+    v = dot_nn(all_low, w_kv[1]).astype(BF)
+    onehot = jnp.where(bucket_table[:, None] == jnp.arange(BUCKETS, dtype=jnp.int32)[None, :], 1.0, 0.0)
+    bias_by_dist = lax.dot_general(bias_f, onehot, (((0,), (1,)), ((), ())), precision=precise)
+    windows = bias_windows(bias_by_dist, ctx_index)
+    probs, mixed = attend(windows, q, k, v)
+    hidden = source + dot_nn(mixed, w_o)
+    normed = (norm_parts(hidden) * gain_ffn_f).astype(BF)
+
+    cot_parts = spread_plane(after(cot_marked, w_q))
+    marks_all = jnp.stack([v[160] for v in cot_parts])[:, :480].reshape(2560, 3).astype(F32)
+    marks_all = jnp.pad(marks_all, ((0, 0), (0, 5)))
+    g_all = jnp.concatenate([v[:160] for v in cot_parts], axis=0)
+    x_all = jnp.concatenate(spread_plane(normed), axis=0)
+    prev, scores, dh, win = None, [], [], []
+    for e in range(3):
+        out, dx, dh_e, win_e, s_e = expert_call(e, idx, x_all, g_all, marks_all, spread[e], prev, scores)
+        prev = (out, dx)
+        scores.append(s_e)
+        dh.append(dh_e)
+        win.append(win_e)
+    out, dx = prev
+
+    grad_normed_ffn = collect_plane(dx)
+    bulk = []
+    for e in range(3):
+        gw = dot_tn(dh[e], x_all).astype(BF).reshape(2, 4, 96, 1024)
+        dw = dot_tn(win[e], g_all).astype(BF).reshape(1, 4, 96, 1024)
+        both = jnp.concatenate([gw, dw], axis=0)
+        if e == 2:
+            router_part = both[0, 0, 88:91].astype(F32)
+        bulk.append(line_collect(lambda n: lax.dynamic_index_in_dim(both, n, 1, keepdims=False), z))
+    combined = collect_plane(after(out, grad_normed_ffn))
+    output = (hidden + combined).astype(BF).reshape(1, 1, 320, 1024)
+
+    back = jnp.stack(bulk).reshape(3, 3, 96, 4, 256).transpose(3, 0, 1, 2, 4)
+    back = trade_wt(back, wt_index)[:, :, :, :88].transpose(1, 2, 0, 3, 4).reshape(3, 3, 352, 256).astype(F32)
+    res_gate, res_up, res_down = back[:, 0].transpose(0, 2, 1), back[:, 1].transpose(0, 2, 1), back[:, 2]
+
+    grad_final = cot.astype(F32)
+    unused, pull = jax.vjp(rms_norm, hidden, gain_ffn_f)
+    grad_part, gain_ffn_part = pull(grad_normed_ffn)
+    grad_hidden = grad_final + grad_part
+    grad_hidden_low = grad_hidden.astype(BF)
+    grad_mixed = dot_nt(grad_hidden_low, w_o).astype(BF)
+    dq, dk, dv, dbias = attend_back(probs, q, k, v, grad_mixed)
+
+    gn_all = dot_nt(dk, w_kv[0]) + dot_nt(dv, w_kv[1])
+    gn_q = dot_nt(dq, w_q)
+    gp = gn_all[:512].astype(BF).reshape(4, 2, 64, 1024)
+    gp_keep = lax.dynamic_index_in_dim(gp, y, 1, keepdims=False)
+    gp_sum = add_low(gp_keep, move_y(lax.dynamic_index_in_dim(gp, 1 - y, 1, keepdims=False)))
+    gp_at = lambda n: lax.dynamic_index_in_dim(gp_sum, (z + n) % 4, 0, keepdims=False)
+    gp_own = gp_at(0).astype(F32)
+    for s in (1, 2, 3):
+        gp_own = gp_own + shift_z(gp_at(s), s).astype(F32)
+    gn_own = gn_q + jnp.concatenate([gp_own, gn_all[512:]], axis=0)
+    unused, pull = jax.vjp(rms_norm, source, gain_attn_f)
+    grad_source, unused = pull(gn_own)
+    grad_tokens = (grad_hidden + grad_source).astype(BF).reshape(1, 1, 320, 1024)
+    gain_attn_part = jnp.sum(gn_all * unit_all, axis=0) + jnp.sum(gn_q * norm_parts(source), axis=0)
+
+    bias_rows = bias_windows_back(dbias, ctx_index)
+    bias_part = jnp.dot(bias_rows, onehot, precision=precise)
+    smalls = jnp.concatenate(
+        [gain_attn_part[None], gain_ffn_part[None], router_part, jnp.pad(bias_part.reshape(1, 512), ((0, 0), (0, 512))),
+         jnp.zeros((2, 1024), F32)], axis=0
+    )
+    smalls = sum_all(smalls)
+    mine = lax.dynamic_slice_in_dim(smalls, wt_index * 256, 256, 1)
+    res_gain_attn, res_gain_ffn, res_router = mine[0], mine[1], mine[2:5].T
+    res_bias = lax.dynamic_slice_in_dim(smalls[5, :512].reshape(16, 32), wt_index * 4, 4, 0).T
+
+    grads = jnp.stack(
+        [dot_tn(own_low, dq).astype(BF), dot_tn(all_low, dk).astype(BF), dot_tn(all_low, dv).astype(BF),
+         dot_tn(mixed, grad_hidden_low).astype(BF)]
+    ).reshape(4, 2, 2, 256, 1024)
+    pick = lambda v, n, d: lax.dynamic_index_in_dim(v, n, d, keepdims=False)
+    t = add_low(pick(grads, c, 2), move_c(pick(grads, 1 - c, 2)))
+    ta, tb = t[:2].reshape(2, 2, 256, 4, 2, 128), t[2:].reshape(2, 2, 256, 4, 2, 128)
+    ta = add_low(pick(ta, x, 1), move_x(pick(ta, 1 - x, 1)))
+    tb = add_low(pick(tb, y, 4), move_y(pick(tb, 1 - y, 4)))
+    ta = add_low(pick(ta, y, 3), move_y(pick(ta, 1 - y, 3)))
+    tb = add_low(pick(tb, x, 1), move_x(pick(tb, 1 - x, 1)))
+    tz = jnp.concatenate([ta, tb], axis=0)
+    tot = pick(tz, z, 2).astype(F32)
+    for s in (1, 2, 3):
+        tot = tot + shift_z(pick(tz, (z + s) % 4, 2), s).astype(F32)
+    return (
+        output, grad_tokens, tot[0], tot[1], tot[2], tot[3], res_gain_attn, res_gain_ffn, res_router, res_bias,
+        res_gate, res_up, res_down,
+    )
+
+
 def solution(mesh):
+    fast = mesh.shape["ctx"] == FAST_CTX and mesh.shape["wt"] == FAST_WT
     return jax.shard_map(
-        local,
+        local_fast if fast else local,
         mesh=mesh,
         in_specs=(
             P("wt", "ctx", None, None),

time: 2370 us -> 1030 us (0.43)
  waiting for transfers between devices: 1510 us -> 240 us
  Pallas kernels: 0 us -> 361 us
  local copies, waits for them, and re-layouts: 334 us -> 91.2 us
  starting transfers between devices: 1.2 us -> 187 us
  blocking collectives: 181 us -> 5.18 us
  matrix products: 239 us -> 73.2 us
    reduce_scatter x12 -> x0, waiting for transfers between devices: 721 us -> none  [the longest x1 157 us: local(): lax.psum_scatter(row_parts[6], 'ctx', scatter_dimension=1, tiled=True)]
    all_gather x12 -> x0, waiting for transfers between devices: 412 us -> none  [the longest x1 102 us: local(): lax.all_gather(cols_down, 'wt', axis=2, tiled=True)]
    unnamed x34 -> x0, waiting for transfers between devices: 382 us -> none
    pallas_call x0 -> x6, Pallas kernels: none -> 361 us  [the longest x1 257 us: place_weights(): pl.pallas_call(functools.partial(place_kernel, keys), out_shape=(jax.Shap...]
    ppermute x0 -> x141, waiting for transfers between devices: none -> 240 us  [the longest x23 70.7 us: move_x(): return lax.ppermute(v, 'wt', SWAP_X)]
    ppermute x0 -> x141, starting transfers between devices: none -> 187 us  [the longest x18 80.4 us: up_z(): return lax.ppermute(v, 'ctx', UP_Z)]
    dot_general x42 -> x20, matrix products: 239 us -> 73.2 us  [the longest x10 49.4 us: dot_tn(): lax.dot_general(a, b, (((0,), (0,)), ((), ())), preferred_element_type=F32)]
    all_gather x8 -> x1, blocking collectives: 140 us -> 5.18 us  [local_fast(): small = lax.all_gather(packed, 'wt', axis=0, tiled=False)]
  transfers between devices with their start and end apart: 29 -> 141, of which waited for: 22 -> 54; matrix products, arithmetic and copies ran while one was open for 21% -> 16% of each run, Pallas kernels for 0% -> 8%
where the time goes in v1:
time: 1030 us; the launch traced here: 1020 us
  Pallas kernels  361 us (35%)
  waiting for transfers between devices  240 us (23%)
  starting transfers between devices  187 us (18%)
  local copies, waits for them, and re-layouts  91.2 us (9%)
  matrix products  73.2 us (7%)
  other arithmetic  62.8 us (6%)
    pallas_call x1, Pallas kernels, place_weights(): pl.pallas_call(functools.partial(place_kernel, keys), out_shape=(jax.Shap...  257 us
    ppermute x18, starting transfers between devices, up_z(): return lax.ppermute(v, 'ctx', UP_Z)  80.4 us
    pallas_call x3, Pallas kernels, expert_call(): pl.pallas_call(functools.partial(expert_kernel, expert, first, last), gri...  70.9 us
    ppermute x23, waiting for transfers between devices, move_x(): return lax.ppermute(v, 'wt', SWAP_X)  70.7 us
    ppermute x26, waiting for transfers between devices, move_y(): return lax.ppermute(v, 'ctx', SWAP_Y)  68.3 us
    dot_general x10, matrix products, dot_tn(): lax.dot_general(a, b, (((0,), (0,)), ((), ())), preferred_element_type=F32)  49.4 us
    ppermute x18, waiting for transfers between devices, down_z(): return lax.ppermute(v, 'ctx', DOWN_Z)  39 us
    ppermute x18, waiting for transfers between devices, up_z(): return lax.ppermute(v, 'ctx', UP_Z)  29.5 us
  transfers between devices with their start and end apart: 141, of which 54 were waited for; matrix products, arithmetic and copies ran while one was open for 16% of the time, Pallas kernels for 8%

profile of v1, /device:TPU:0, one launch (start us, length us, event | category | flops | bytes accessed | tf_op | source)
XLA Modules:
  0.0 1024.3 jit_solution(942157438624010983)
XLA Ops:
  66.9 13.5 %collective-permute-done.1.refs_2_ = bf16[4,256,128]{2,1,0:T(8,128)(2,1)} collective-permute-done((bf16[4,256,128]{2,1,0:T(8,128)(2,1)}, bf16[4,256,128]{2,1,0:T(8,128)(2,1)}, u32[]{:S(2)}, u32[]{:S(2)}) %collective-permute-start.1) | collective-permute-done | bytes 262176 | tf_op jit(solution)/shard_map/ppermute | solution.py:509
  112.1 6.2 collective-permute-done.21.refs_22_
  123.3 256.9 %shard_map.255 = (bf16[2,1024,1024]{2,1,0:T(8,128)(2,1)}, bf16[1024,1024]{1,0:T(8,128)(2,1)}, bf16[1024,1024]{1,0:T(8,128)(2,1)}) custom-call(s32[4]{0:T(128)} %pad_add_fusion.1.idx.refs_0_, bf16[4,256,128]{2,1,0:T(8,128)(2,1)} %pad_maximum_fusion.8.refs_0_, bf16[4,256,128]{2,1,0:T(8,128)(2,1)} %copy-done.48, ...), custom_call_target="tpu_custom_call" | custom-call | tf_op jit(solution)/shard_map/pallas_call | solution.py:590
  391.0 15.6 %shard_map.256 = (bf16[16,320,768]{2,1,0:T(8,128)(2,1)}, bf16[320,1024]{1,0:T(8,128)(2,1)}) custom-call(f32[16,2,8,1024]{3,2,1,0:T(8,128)} %pad_maximum_fusion.6.w_ref, bf16[320,1024]{1,0:T(8,128)(2,1)} %convolution_convert_fusion.11.q_ref, bf16[768,1024]{1,0:T(8,128)(2,1)} %fusion.22.k_ref, bf16[768,1024]{1,0:T(8,128)(2,1)} %fusion.25.v_ref), custom_call_target="tpu_custom_call" | custom-call | flops 1006632960 | bytes 14680064 | tf_op jit(solution)/shard_map/pallas_call | solution.py:634
  413.7 7.3 collective-permute-done.38
  445.3 7.9 collective-permute-done.54
  465.6 8.5 collective-permute-done.46
  525.6 11.3 %collective-permute-done.85.refs_9_ = bf16[3,96,1024]{2,1,0:T(8,128)(2,1)} collective-permute-done((bf16[3,96,1024]{2,1,0:T(8,128)(2,1)}, bf16[3,96,1024]{2,1,0:T(8,128)(2,1)}, u32[]{:S(2)}, u32[]{:S(2)}) %collective-permute-start.85) | collective-permute-done | bytes 589856 | tf_op jit(solution)/shard_map/ppermute | solution.py:517
  568.3 21.1 %shard_map.257 = (bf16[2560,1024]{1,0:T(8,128)(2,1)}, bf16[2560,1024]{1,0:T(8,128)(2,1)}, bf16[2560,768]{1,0:T(8,128)(2,1)}, bf16[2560,384]{1,0:T(8,128)(2,1)}, f32[2560,8]{1,0:T(8,128)}) custom-call(s32[4]{0:T(128)} %pad_add_fusion.1.idx.refs_0_, bf16[2560,1024]{1,0:T(8,128)(2,1)} %copy-done.67, bf16[2560,1024]{1,0:T(8,128)(2,1)} %slice_dynamic-update-slice_fusion.refs_2_, ...), custom_call_target="tpu_custom_call" | custom-call | flops 12079595520 | bytes 41943040 | tf_op jit(solution)/shard_map/pallas_call | solution.py:859
  589.4 8.1 convolution_convert_fusion.5
  607.7 22.7 %shard_map.258 = (bf16[2560,1024]{1,0:T(8,128)(2,1)}, bf16[2560,1024]{1,0:T(8,128)(2,1)}, bf16[2560,768]{1,0:T(8,128)(2,1)}, bf16[2560,384]{1,0:T(8,128)(2,1)}, f32[2560,8]{1,0:T(8,128)}) custom-call(s32[4]{0:T(128)} %pad_add_fusion.1.idx.refs_0_, bf16[2560,1024]{1,0:T(8,128)(2,1)} %copy-done.67, bf16[2560,1024]{1,0:T(8,128)(2,1)} %slice_dynamic-update-slice_fusion.refs_2_, ...), custom_call_target="tpu_custom_call" | custom-call | flops 12079595520 | bytes 41943040 | tf_op jit(solution)/shard_map/pallas_call | solution.py:859
  635.8 27.1 %shard_map.259 = (bf16[2560,1024]{1,0:T(8,128)(2,1)}, bf16[2560,1024]{1,0:T(8,128)(2,1)}, bf16[2560,768]{1,0:T(8,128)(2,1)}, bf16[2560,384]{1,0:T(8,128)(2,1)}, f32[2560,8]{1,0:T(8,128)}) custom-call(s32[4]{0:T(128)} %pad_add_fusion.1.idx.refs_0_, bf16[2560,1024]{1,0:T(8,128)(2,1)} %copy-done.67, bf16[2560,1024]{1,0:T(8,128)(2,1)} %slice_dynamic-update-slice_fusion.refs_2_, ...), custom_call_target="tpu_custom_call" | custom-call | flops 12079595520 | bytes 41943040 | tf_op jit(solution)/shard_map/pallas_call | solution.py:859
  662.9 8.1 convolution_convert_fusion.6
  671.0 7.0 convolution_convert_fusion.4
  701.0 8.1 collective-permute-done.132
  714.7 7.1 collective-permute-done.121
  728.2 6.3 collective-permute-done.127
  737.0 6.3 collective-permute-done.133
  782.8 6.1 collective-permute-start.137
  833.0 17.2 %shard_map.260 = (bf16[320,1024]{1,0:T(8,128)(2,1)}, bf16[768,1024]{1,0:T(8,128)(2,1)}, bf16[768,1024]{1,0:T(8,128)(2,1)}, f32[16,2,8,1024]{3,2,1,0:T(8,128)}) custom-call(bf16[16,320,768]{2,1,0:T(8,128)(2,1)} %get-tuple-element.53.p_ref, bf16[320,1024]{1,0:T(8,128)(2,1)} %convolution_convert_fusion.11.q_ref, bf16[768,1024]{1,0:T(8,128)(2,1)} %fusion.22.k_ref, ...), custom_call_target="tpu_custom_call" | custom-call | flops 2516582400 | bytes 14680064 | tf_op jit(solution)/shard_map/pallas_call | solution.py:688
  907.5 6.5 collective-permute-done.103
  959.4 21.1 %collective-permute-done.117 = f32[8,1024]{1,0:T(8,128)S(1)} collective-permute-done((f32[8,1024]{1,0:T(8,128)S(1)}, f32[8,1024]{1,0:T(8,128)S(1)}, u32[]{:S(2)}, u32[]{:S(2)}) %collective-permute-start.117) | collective-permute-done | bytes 32800 | tf_op jit(solution)/shard_map/ppermute | solution.py:505
  993.1 7.1 collective-permute-done.109
  1013.6 7.4 collective-permute-done.113
  (759 shorter events, 506.1 us)
Async XLA Ops:
  2.4 43.4 %collective-permute-start.36 = (bf16[64,1024]{1,0:T(8,128)(2,1)}, bf16[64,1024]{1,0:T(8,128)(2,1)}, u32[]{:S(2)}, u32[]{:S(2)}) collective-permute-start(bf16[64,1024]{1,0:T(8,128)(2,1)} %get-tuple-element.174), channel_id=1, source_target_pairs={{0,8},{4,12},{8,16},{12,20},{16,24},{20,28},{24,0},{28,4},{1,9},{5... | collective-permute-start | bytes 393224 | tf_op jit(solution)/shard_map/ppermute | solution.py:525
  5.4 36.2 %collective-permute-start.34 = (bf16[64,1024]{1,0:T(8,128)(2,1)}, bf16[64,1024]{1,0:T(8,128)(2,1)}, u32[]{:S(2)}, u32[]{:S(2)}) collective-permute-start(bf16[64,1024]{1,0:T(8,128)(2,1)} %get-tuple-element.174), channel_id=1, source_target_pairs={{0,16},{4,20},{8,24},{12,28},{16,0},{20,4},{24,8},{28,12},{1,17},{... | collective-permute-start | bytes 393224 | tf_op jit(solution)/shard_map/ppermute | solution.py:525
  9.3 34.0 %collective-permute-start.31 = (bf16[64,1024]{1,0:T(8,128)(2,1)}, bf16[64,1024]{1,0:T(8,128)(2,1)}, u32[]{:S(2)}, u32[]{:S(2)}) collective-permute-start(bf16[64,1024]{1,0:T(8,128)(2,1)} %get-tuple-element.174), channel_id=1, source_target_pairs={{0,4},{4,0},{8,12},{12,8},{16,20},{20,16},{24,28},{28,24},{1,5},{5... | collective-permute-start | bytes 393224 | tf_op jit(solution)/shard_map/ppermute | solution.py:505
  12.5 42.1 %collective-permute-start.23 = (bf16[4,256,128]{2,1,0:T(8,128)(2,1)}, bf16[4,256,128]{2,1,0:T(8,128)(2,1)}, u32[]{:S(2)}, u32[]{:S(2)}) collective-permute-start(bf16[4,256,128]{2,1,0:T(8,128)(2,1)} %pad_maximum_fusion.8.refs_0_), channel_id=1, source_target_pairs={{0,24},{4,28},{8,0},{12,4},{16,8},{20,12},{24,16},{28,20},{1,25},{... | collective-permute-start | bytes 786440 | tf_op jit(solution)/shard_map/ppermute | solution.py:525
  380.3 43.6 %collective-permute-start.62 = (bf16[176,1024]{1,0:T(8,128)(2,1)S(1)}, bf16[176,1024]{1,0:T(8,128)(2,1)S(1)}, u32[]{:S(2)}, u32[]{:S(2)}) collective-permute-start(bf16[176,1024]{1,0:T(8,128)(2,1)S(1)} %get-tuple-element.166), channel_id=1, source_target_pairs={{0,1},{1,0},{2,3},{3,2},{4,5},{5,4},{6,7},{7,6},{8,9},{9,8},{10,11... | collective-permute-start | bytes 1081352 | tf_op jit(solution)/shard_map/ppermute | solution.py:513
  380.8 49.5 %collective-permute-start.60 = (bf16[176,1024]{1,0:T(8,128)(2,1)S(1)}, bf16[176,1024]{1,0:T(8,128)(2,1)S(1)}, u32[]{:S(2)}, u32[]{:S(2)}) collective-permute-start(bf16[176,1024]{1,0:T(8,128)(2,1)S(1)} %get-tuple-element.166), channel_id=1, source_target_pairs={{0,4},{4,0},{8,12},{12,8},{16,20},{20,16},{24,28},{28,24},{1,5},{5... | collective-permute-start | bytes 1081352 | tf_op jit(solution)/shard_map/ppermute | solution.py:505
  459.7 33.5 %collective-permute-start.69 = (bf16[3,96,1024]{2,1,0:T(8,128)(2,1)S(1)}, bf16[3,96,1024]{2,1,0:T(8,128)(2,1)}, u32[]{:S(2)}, u32[]{:S(2)}) collective-permute-start(bf16[3,96,1024]{2,1,0:T(8,128)(2,1)S(1)} %squeeze.273.refs_4_), channel_id=1, source_target_pairs={{8,0},{12,4},{16,8},{20,12},{24,16},{28,20},{9,1},{13,5},{17,9},{2... | collective-permute-start | bytes 1769480 | tf_op jit(solution)/shard_map/ppermute | solution.py:521
  507.4 34.0 %collective-permute-start.82 = (bf16[3,96,1024]{2,1,0:T(8,128)(2,1)}, bf16[3,96,1024]{2,1,0:T(8,128)(2,1)}, u32[]{:S(2)}, u32[]{:S(2)}) collective-permute-start(bf16[3,96,1024]{2,1,0:T(8,128)(2,1)} %collective-permute-done.81.refs_5_), channel_id=1, source_target_pairs={{8,0},{12,4},{16,8},{20,12},{24,16},{28,20},{9,1},{13,5},{17,9},{2... | collective-permute-start | bytes 1769480 | tf_op jit(solution)/shard_map/ppermute | solution.py:521
  517.0 33.3 %collective-permute-start.79 = (bf16[3,96,1024]{2,1,0:T(8,128)(2,1)}, bf16[3,96,1024]{2,1,0:T(8,128)(2,1)}, u32[]{:S(2)}, u32[]{:S(2)}) collective-permute-start(bf16[3,96,1024]{2,1,0:T(8,128)(2,1)} %collective-permute-done.78.refs_8_), channel_id=1, source_target_pairs={{0,8},{4,12},{8,16},{12,20},{16,24},{20,28},{1,9},{5,13},{9,17},{1... | collective-permute-start | bytes 1769480 | tf_op jit(solution)/shard_map/ppermute | solution.py:517
  544.6 91.1 %collective-permute-start.74 = (bf16[3,96,1024]{2,1,0:T(8,128)(2,1)}, bf16[3,96,1024]{2,1,0:T(8,128)(2,1)}, u32[]{:S(2)}, u32[]{:S(2)}) collective-permute-start(bf16[3,96,1024]{2,1,0:T(8,128)(2,1)} %copy-done.90), channel_id=1, source_target_pairs={{0,8},{4,12},{8,16},{12,20},{16,24},{20,28},{1,9},{5,13},{9,17},{1... | collective-permute-start | bytes 1769480 | tf_op jit(solution)/shard_map/ppermute | solution.py:517
  550.3 85.4 %collective-permute-start.71 = (bf16[3,96,1024]{2,1,0:T(8,128)(2,1)S(1)}, bf16[3,96,1024]{2,1,0:T(8,128)(2,1)}, u32[]{:S(2)}, u32[]{:S(2)}) collective-permute-start(bf16[3,96,1024]{2,1,0:T(8,128)(2,1)S(1)} %collective-permute-done.70.refs_6_), channel_id=1, source_target_pairs={{8,0},{12,4},{16,8},{20,12},{24,16},{28,20},{9,1},{13,5},{17,9},{2... | collective-permute-start | bytes 1769480 | tf_op jit(solution)/shard_map/ppermute | solution.py:521
  554.9 47.3 %collective-permute-start.80 = (bf16[3,96,1024]{2,1,0:T(8,128)(2,1)}, bf16[3,96,1024]{2,1,0:T(8,128)(2,1)}, u32[]{:S(2)}, u32[]{:S(2)}) collective-permute-start(bf16[3,96,1024]{2,1,0:T(8,128)(2,1)} %collective-permute-done.79.refs_9_), channel_id=1, source_target_pairs={{0,8},{4,12},{8,16},{12,20},{16,24},{20,28},{1,9},{5,13},{9,17},{1... | collective-permute-start | bytes 1769480 | tf_op jit(solution)/shard_map/ppermute | solution.py:517
  562.2 45.5 %collective-permute-start.77 = (bf16[3,96,1024]{2,1,0:T(8,128)(2,1)}, bf16[3,96,1024]{2,1,0:T(8,128)(2,1)}, u32[]{:S(2)}, u32[]{:S(2)}) collective-permute-start(bf16[3,96,1024]{2,1,0:T(8,128)(2,1)} %collective-permute-done.76.refs_6_), channel_id=1, source_target_pairs={{8,0},{12,4},{16,8},{20,12},{24,16},{28,20},{9,1},{13,5},{17,9},{2... | collective-permute-start | bytes 1769480 | tf_op jit(solution)/shard_map/ppermute | solution.py:521
  600.9 87.1 %collective-permute-start.120 = (bf16[3,96,1024]{2,1,0:T(8,128)(2,1)}, bf16[3,96,1024]{2,1,0:T(8,128)(2,1)S(1)}, u32[]{:S(2)}, u32[]{:S(2)}) collective-permute-start(bf16[3,96,1024]{2,1,0:T(8,128)(2,1)} %get-tuple-element.136), channel_id=1, source_target_pairs={{8,0},{12,4},{16,8},{20,12},{24,16},{28,20},{9,1},{13,5},{17,9},{2... | collective-permute-start | bytes 1769480 | tf_op jit(solution)/shard_map/ppermute | solution.py:521
  602.2 90.4 %collective-permute-start.123 = (bf16[3,96,1024]{2,1,0:T(8,128)(2,1)}, bf16[3,96,1024]{2,1,0:T(8,128)(2,1)}, u32[]{:S(2)}, u32[]{:S(2)}) collective-permute-start(bf16[3,96,1024]{2,1,0:T(8,128)(2,1)} %get-tuple-element.137), channel_id=1, source_target_pairs={{0,8},{4,12},{8,16},{12,20},{16,24},{20,28},{1,9},{5,13},{9,17},{1... | collective-permute-start | bytes 1769480 | tf_op jit(solution)/shard_map/ppermute | solution.py:517
  700.5 50.0 %collective-permute-start.95 = (bf16[4,160,1024]{2,1,0:T(8,128)(2,1)S(1)}, bf16[4,160,1024]{2,1,0:T(8,128)(2,1)S(1)}, u32[]{:S(2)}, u32[]{:S(2)}) collective-permute-start(bf16[4,160,1024]{2,1,0:T(8,128)(2,1)S(1)} %get-tuple-element.113), channel_id=1, source_target_pairs={{0,1},{1,0},{2,3},{3,2},{4,5},{5,4},{6,7},{7,6},{8,9},{9,8},{10,11... | collective-permute-start | bytes 3932168 | tf_op jit(solution)/shard_map/ppermute | solution.py:513
  709.2 46.4 %collective-permute-start.99 = (bf16[4,160,1024]{2,1,0:T(8,128)(2,1)S(1)}, bf16[4,160,1024]{2,1,0:T(8,128)(2,1)S(1)}, u32[]{:S(2)}, u32[]{:S(2)}) collective-permute-start(bf16[4,160,1024]{2,1,0:T(8,128)(2,1)S(1)} %get-tuple-element.114), channel_id=1, source_target_pairs={{0,1},{1,0},{2,3},{3,2},{4,5},{5,4},{6,7},{7,6},{8,9},{9,8},{10,11... | collective-permute-start | bytes 3932168 | tf_op jit(solution)/shard_map/ppermute | solution.py:513
  747.7 35.0 %collective-permute-start.122 = (bf16[3,96,1024]{2,1,0:T(8,128)(2,1)S(1)}, bf16[3,96,1024]{2,1,0:T(8,128)(2,1)S(1)}, u32[]{:S(2)}, u32[]{:S(2)}) collective-permute-start(bf16[3,96,1024]{2,1,0:T(8,128)(2,1)S(1)} %get-tuple-element.132), channel_id=1, source_target_pairs={{8,0},{12,4},{16,8},{20,12},{24,16},{28,20},{9,1},{13,5},{17,9},{2... | collective-permute-start | bytes 1769480 | tf_op jit(solution)/shard_map/ppermute | solution.py:521
  750.5 39.2 %collective-permute-start.125 = (bf16[3,96,1024]{2,1,0:T(8,128)(2,1)S(1)}, bf16[3,96,1024]{2,1,0:T(8,128)(2,1)S(1)}, u32[]{:S(2)}, u32[]{:S(2)}) collective-permute-start(bf16[3,96,1024]{2,1,0:T(8,128)(2,1)S(1)} %get-tuple-element.133), channel_id=1, source_target_pairs={{0,8},{4,12},{8,16},{12,20},{16,24},{20,28},{1,9},{5,13},{9,17},{1... | collective-permute-start | bytes 1769480 | tf_op jit(solution)/shard_map/ppermute | solution.py:517
  755.6 39.2 %collective-permute-start.128 = (bf16[3,96,1024]{2,1,0:T(8,128)(2,1)}, bf16[3,96,1024]{2,1,0:T(8,128)(2,1)}, u32[]{:S(2)}, u32[]{:S(2)}) collective-permute-start(bf16[3,96,1024]{2,1,0:T(8,128)(2,1)} %get-tuple-element.126), channel_id=1, source_target_pairs={{8,0},{12,4},{16,8},{20,12},{24,16},{28,20},{9,1},{13,5},{17,9},{2... | collective-permute-start | bytes 1769480 | tf_op jit(solution)/shard_map/ppermute | solution.py:521
  885.0 62.6 %collective-permute-start.107 = (bf16[4,2,256,1024]{2,3,1,0:T(8,128)(2,1)}, bf16[4,2,256,1024]{2,3,1,0:T(8,128)(2,1)}, u32[]{:S(2)}, u32[]{:S(2)}) collective-permute-start(bf16[4,2,256,1024]{2,3,1,0:T(8,128)(2,1)} %dynamic-slice_bitcast_fusion), channel_id=1, source_target_pairs={{0,1},{1,0},{2,3},{3,2},{4,5},{5,4},{6,7},{7,6},{8,9},{9,8},{10,11... | collective-permute-start | bytes 12582920 | tf_op jit(solution)/shard_map/ppermute | solution.py:513
  893.1 44.4 %collective-permute-start.138 = (bf16[3,3,96,256]{3,2,1,0:T(8,128)(2,1)}, bf16[3,3,96,256]{3,2,1,0:T(8,128)(2,1)}, u32[]{:S(2)}, u32[]{:S(2)}) collective-permute-start(bf16[3,3,96,256]{3,2,1,0:T(8,128)(2,1)} %bitcast.555), channel_id=1, source_target_pairs={{0,1},{1,0},{2,3},{3,2},{4,5},{5,4},{6,7},{7,6},{8,9},{9,8},{10,11... | collective-permute-start | bytes 1327112 | tf_op jit(solution)/shard_map/ppermute | solution.py:513
  952.5 35.6 %collective-permute-start.108 = (bf16[2,256,4,2,128]{1,4,3,2,0:T(8,128)(2,1)S(1)}, bf16[2,256,4,2,128]{1,4,3,2,0:T(8,128)(2,1)S(1)}, u32[]{:S(2)}, u32[]{:S(2)}) collective-permute-start(bf16[2,256,4,2,128]{1,4,3,2,0:T(8,128)(2,1)S(1)} %dynamic-slice_bitcast_fusion.1), channel_id=1, source_target_pairs={{0,2},{1,3},{2,0},{3,1},{4,6},{5,7},{6,4},{7,5},{8,10},{9,11},{10,... | collective-permute-start | bytes 3145736 | tf_op jit(solution)/shard_map/ppermute | solution.py:509
  954.6 35.3 %collective-permute-start.110 = (bf16[2,2,256,4,128]{2,4,3,0,1:T(8,128)(2,1)S(1)}, bf16[2,2,256,4,128]{2,4,3,0,1:T(8,128)(2,1)S(1)}, u32[]{:S(2)}, u32[]{:S(2)}) collective-permute-start(bf16[2,2,256,4,128]{2,4,3,0,1:T(8,128)(2,1)S(1)} %bitcast.611), channel_id=1, source_target_pairs={{0,4},{4,0},{8,12},{12,8},{16,20},{20,16},{24,28},{28,24},{1,5},{5... | collective-permute-start | bytes 3145736 | tf_op jit(solution)/shard_map/ppermute | solution.py:505
  (224 other events, 6399.0 us)

commit v2 on v1

--- a/solution.py
+++ b/solution.py
@@ -495,8 +495,8 @@
 NEG = -1e30
 
 SWAP_Y = [(i, i ^ 1) for i in range(8)]
-UP_Z = [(i, i + 2) for i in range(6)]
-DOWN_Z = [(i, i - 2) for i in range(2, 8)]
+PAIR_Z = [(i, i ^ 2) for i in range(8)]
+MID_Z = [(0, 0), (1, 1), (2, 4), (3, 5), (4, 2), (5, 3), (6, 6), (7, 7)]
 SWAP_C = [(i, i ^ 1) for i in range(4)]
 SWAP_X = [(i, i ^ 2) for i in range(4)]
 
@@ -513,12 +513,12 @@
     return lax.ppermute(v, "wt", SWAP_C)
 
 
-def up_z(v):
-    return lax.ppermute(v, "ctx", UP_Z)
-
-
-def down_z(v):
-    return lax.ppermute(v, "ctx", DOWN_Z)
+def pair_z(v):
+    return lax.ppermute(v, "ctx", PAIR_Z)
+
+
+def mid_z(v):
+    return lax.ppermute(v, "ctx", MID_Z)
 
 
 def shift_z(v, s):
@@ -569,24 +569,21 @@
 
 def place_kernel(keys, idx, *refs):
     count = len(keys)
-    ins, wkv, wq, wo, sem = refs[:count], refs[count], refs[count + 1], refs[count + 2], refs[count + 3]
+    ins, wkv, wq, wo = refs[:count], refs[count], refs[count + 1], refs[count + 2]
     z, y, x, c = idx[0], idx[1], idx[2], idx[3]
-    copies = []
     for n, (s, ry, rx, rc) in enumerate(keys):
         row = pl.multiple_of(((x ^ rx) * 2 + (c ^ rc)) * 256, 256)
         col = pl.multiple_of((lax.rem(z + 4 - s, 4) * 2 + (y ^ ry)) * 128, 128)
         rows, cols = pl.ds(row, 256), pl.ds(col, 128)
-        copies.append(pltpu.make_async_copy(ins[n].at[0], wq.at[rows, cols], sem.at[n, 0]))
-        copies.append(pltpu.make_async_copy(ins[n].at[pl.ds(1, 2)], wkv.at[:, rows, cols], sem.at[n, 1]))
-        copies.append(pltpu.make_async_copy(ins[n].at[3], wo.at[rows, cols], sem.at[n, 2]))
-    for copy in copies:
-        copy.start()
-    for copy in copies:
-        copy.wait()
+        wq[rows, cols] = ins[n][0]
+        wkv[0, rows, cols] = ins[n][1]
+        wkv[1, rows, cols] = ins[n][2]
+        wo[rows, cols] = ins[n][3]
 
 
 def place_weights(idx, pieces):
     keys = [k for k, _ in pieces]
+    whole = pl.BlockSpec(memory_space=pltpu.VMEM)
     return pl.pallas_call(
         functools.partial(place_kernel, keys),
         out_shape=(
@@ -594,9 +591,8 @@
             jax.ShapeDtypeStruct((1024, 1024), BF),
             jax.ShapeDtypeStruct((1024, 1024), BF),
         ),
-        in_specs=[SMEM] + [ANY] * len(keys),
-        out_specs=(ANY, ANY, ANY),
-        scratch_shapes=[pltpu.SemaphoreType.DMA((len(keys), 3))],
+        in_specs=[SMEM] + [whole] * len(keys),
+        out_specs=(whole, whole, whole),
         compiler_params=params(),
     )(idx, *[v for _, v in pieces])
 
@@ -769,8 +765,8 @@
 def expert_kernel(expert, first, last, *refs):
     refs = list(refs)
     idx, x_ref, g_ref, m_ref = refs[:4]
-    srcs = refs[4:11]
-    at = 11
+    srcs = refs[4:10]
+    at = 10
     if not first:
         out_prev, dx_prev = refs[at : at + 2]
         at += 2
@@ -786,10 +782,11 @@
             rows = pl.ds(pl.multiple_of(slot * 96, 96), 96)
             return pltpu.make_async_copy(srcs[n], w_scr.at[:, rows, :], sem.at[n])
 
-        plan = [(0, z, None)]
-        for s in range(1, 4):
-            plan.append((s, z + s, z + s <= 3))
-            plan.append((3 + s, z - s, z - s >= 0))
+        middle = (z == 1) | (z == 2)
+        other, far = jnp.where(z < 2, 2, 1), jnp.where(z < 2, 3, 0)
+        plan = [(0, z, None), (1, z ^ 1, None)]
+        for n, slot in ((2, other), (3, far)):
+            plan += [(n, slot, middle), (n + 2, slot, jnp.logical_not(middle))]
         for act in ("start", "wait"):
             for n, slot, ok in plan:
                 if ok is None:
@@ -849,7 +846,7 @@
     first, last = expert == 0, expert == 2
     row = lambda n: pl.BlockSpec((tile, n), lambda i: (i, 0))
     ins = [idx, x, g, m, *srcs]
-    specs = [SMEM, row(1024), row(1024), row(8)] + [ANY] * 7
+    specs = [SMEM, row(1024), row(1024), row(8)] + [ANY] * 6
     if not first:
         ins += list(prev)
         specs += [row(1024), row(1024)]
@@ -868,7 +865,7 @@
         ),
         in_specs=specs,
         out_specs=(row(1024), row(1024), row(768), row(384), row(8)),
-        scratch_shapes=[pltpu.VMEM((3, 384, 1024), BF), pltpu.SemaphoreType.DMA((7,))],
+        scratch_shapes=[pltpu.VMEM((3, 384, 1024), BF), pltpu.SemaphoreType.DMA((6,))],
         compiler_params=params(),
         cost_estimate=pl.CostEstimate(
             flops=2 * total * 1024 * 384 * 6, bytes_accessed=total * 1024 * 16, transcendentals=total * 384
@@ -877,21 +874,20 @@
 
 
 def line_spread(v):
-    a1, b1 = down_z(v), up_z(v)
-    a2, b2 = down_z(a1), up_z(b1)
-    a3, b3 = down_z(a2), up_z(b2)
-    return [v, a1, a2, a3, b1, b2, b3]
+    near = pair_z(v)
+    mid_own, mid_far = mid_z(v), mid_z(near)
+    return [v, near, mid_own, mid_far, pair_z(mid_own), pair_z(mid_far)]
 
 
 def line_collect(part_of, z):
-    at = lambda n: part_of(jnp.clip(z + n, 0, 3))
-    d = down_z(at(-3))
-    u = up_z(at(3))
-    d = down_z(add_low(at(-2), d))
-    u = up_z(add_low(at(2), u))
-    d = down_z(add_low(at(-1), d))
-    u = up_z(add_low(at(1), u))
-    return (at(0).astype(F32) + d.astype(F32) + u.astype(F32)).astype(BF)
+    low_half = z < 2
+    middle = (z == 1) | (z == 2)
+    far, other = part_of(jnp.where(low_half, 3, 0)), part_of(jnp.where(low_half, 2, 1))
+    from_far, from_other = pair_z(far), pair_z(other)
+    cross_far, cross_own = mid_z(add_low(far, from_far)), mid_z(add_low(other, from_other))
+    at_mid = lambda v: jnp.where(middle, v.astype(F32), 0.0)
+    near = (part_of(z ^ 1).astype(F32) + at_mid(cross_far)).astype(BF)
+    return (part_of(z).astype(F32) + pair_z(near).astype(F32) + at_mid(cross_own)).astype(BF)
 
 
 def trade_wt(v, wt_index):

time: 1030 us -> 781 us (0.76)
  Pallas kernels: 361 us -> 112 us
    pallas_call x1, Pallas kernels: 257 us -> 9.14 us  [place_weights(): pl.pallas_call(functools.partial(place_kernel, keys), out_shape=(jax.Shap...]
    ppermute x36 -> x30, starting transfers between devices: 104 us -> 101 us  [the longest x18 63.5 us: pair_z(): return lax.ppermute(v, 'ctx', PAIR_Z)]
    ppermute x36 -> x30, waiting for transfers between devices: 68.4 us -> 65.5 us  [the longest x18 65.5 us: pair_z(): return lax.ppermute(v, 'ctx', PAIR_Z)]
    unnamed x270 -> x266, local copies, waits for them, and re-layouts: 23.1 us -> 25 us
  transfers between devices with their start and end apart: 141 -> 135, of which waited for: 54 -> 45; matrix products, arithmetic and copies ran while one was open for 16% -> 22% of each run, Pallas kernels for 8% -> 11%
where the time goes in v2:
time: 781 us; the launch traced here: 769 us
  waiting for transfers between devices  243 us (31%)
  starting transfers between devices  177 us (23%)
  Pallas kernels  112 us (14%)
  local copies, waits for them, and re-layouts  94.1 us (12%)
  matrix products  70.2 us (9%)
  other arithmetic  64.3 us (8%)
    ppermute x23, waiting for transfers between devices, move_x(): return lax.ppermute(v, 'wt', SWAP_X)  73.2 us
    ppermute x26, waiting for transfers between devices, move_y(): return lax.ppermute(v, 'ctx', SWAP_Y)  70.9 us
    pallas_call x3, Pallas kernels, expert_call(): pl.pallas_call(functools.partial(expert_kernel, expert, first, last), gri...  70.3 us
    ppermute x18, waiting for transfers between devices, pair_z(): return lax.ppermute(v, 'ctx', PAIR_Z)  65.5 us
    ppermute x18, starting transfers between devices, pair_z(): return lax.ppermute(v, 'ctx', PAIR_Z)  63.5 us
    dot_general x10, matrix products, dot_tn(): lax.dot_general(a, b, (((0,), (0,)), ((), ())), preferred_element_type=F32)  45.8 us
    ppermute x12, starting transfers between devices, mid_z(): return lax.ppermute(v, 'ctx', MID_Z)  37.1 us
    ppermute x23, starting transfers between devices, move_x(): return lax.ppermute(v, 'wt', SWAP_X)  25.9 us
  transfers between devices with their start and end apart: 135, of which 45 were waited for; matrix products, arithmetic and copies ran while one was open for 22% of the time, Pallas kernels for 11%

profile of v2, /device:TPU:0, one launch (start us, length us, event | category | flops | bytes accessed | tf_op | source)
XLA Modules:
  0.0 769.4 jit_solution(3912914215276122221)
XLA Ops:
  56.2 6.0 collective-permute-done.15.refs_16_
  66.9 13.5 %collective-permute-done.1.refs_2_ = bf16[4,256,128]{2,1,0:T(8,128)(2,1)} collective-permute-done((bf16[4,256,128]{2,1,0:T(8,128)(2,1)}, bf16[4,256,128]{2,1,0:T(8,128)(2,1)}, u32[]{:S(2)}, u32[]{:S(2)}) %collective-permute-start.1) | collective-permute-done | bytes 262176 | tf_op jit(solution)/shard_map/ppermute | solution.py:509
  112.2 6.2 collective-permute-done.21.refs_22_
  123.3 9.1 %shard_map.255 = (bf16[2,1024,1024]{2,1,0:T(8,128)(2,1)}, bf16[1024,1024]{1,0:T(8,128)(2,1)}, bf16[1024,1024]{1,0:T(8,128)(2,1)}) custom-call(s32[4]{0:T(128)} %pad_add_fusion.1.idx.refs_0_, bf16[4,256,128]{2,1,0:T(8,128)(2,1)} %pad_maximum_fusion.8.refs_0_, bf16[4,256,128]{2,1,0:T(8,128)(2,1)} %copy-done.47, ...), custom_call_target="tpu_custom_call" | custom-call | tf_op jit(solution)/shard_map/pallas_call | solution.py:587
  143.8 15.0 %shard_map.256 = (bf16[16,320,768]{2,1,0:T(8,128)(2,1)}, bf16[320,1024]{1,0:T(8,128)(2,1)}) custom-call(f32[16,2,8,1024]{3,2,1,0:T(8,128)} %pad_maximum_fusion.6.w_ref, bf16[320,1024]{1,0:T(8,128)(2,1)} %convolution_convert_fusion.11.q_ref, bf16[768,1024]{1,0:T(8,128)(2,1)} %fusion.22.k_ref, bf16[768,1024]{1,0:T(8,128)(2,1)} %fusion.25.v_ref), custom_call_target="tpu_custom_call" | custom-call | flops 1006632960 | bytes 14680064 | tf_op jit(solution)/shard_map/pallas_call | solution.py:630
  166.0 7.3 collective-permute-done.38
  197.6 7.9 %collective-permute-done.54 = bf16[176,1024]{1,0:T(8,128)(2,1)S(1)} collective-permute-done((bf16[176,1024]{1,0:T(8,128)(2,1)S(1)}, bf16[176,1024]{1,0:T(8,128)(2,1)S(1)}, u32[]{:S(2)}, u32[]{:S(2)}) %collective-permute-start.54) | collective-permute-done | bytes 360480 | tf_op jit(solution)/shard_map/ppermute | solution.py:509
  217.9 8.5 %collective-permute-done.46 = bf16[160,1024]{1,0:T(8,128)(2,1)S(1)} collective-permute-done((bf16[160,1024]{1,0:T(8,128)(2,1)S(1)}, bf16[160,1024]{1,0:T(8,128)(2,1)S(1)}, u32[]{:S(2)}, u32[]{:S(2)}) %collective-permute-start.46) | collective-permute-done | bytes 327712 | tf_op jit(solution)/shard_map/ppermute | solution.py:505
  239.0 13.2 %collective-permute-done.79.refs_5_ = bf16[3,96,1024]{2,1,0:T(8,128)(2,1)} collective-permute-done((bf16[3,96,1024]{2,1,0:T(8,128)(2,1)S(1)}, bf16[3,96,1024]{2,1,0:T(8,128)(2,1)}, u32[]{:S(2)}, u32[]{:S(2)}) %collective-permute-start.79) | collective-permute-done | bytes 589856 | tf_op jit(solution)/shard_map/ppermute | solution.py:517
  285.3 12.6 %collective-permute-start.77 = (bf16[3,96,1024]{2,1,0:T(8,128)(2,1)}, bf16[3,96,1024]{2,1,0:T(8,128)(2,1)}, u32[]{:S(2)}, u32[]{:S(2)}) collective-permute-start(bf16[3,96,1024]{2,1,0:T(8,128)(2,1)} %collective-permute-done.75.refs_6_), channel_id=1, source_target_pairs={{0,8},{4,12},{8,0},{12,4},{16,24},{20,28},{24,16},{28,20},{1,9},{5... | collective-permute-start | bytes 1769480 | tf_op jit(solution)/shard_map/ppermute | solution.py:517
  297.9 10.6 %collective-permute-start.73 = (bf16[3,96,1024]{2,1,0:T(8,128)(2,1)}, bf16[3,96,1024]{2,1,0:T(8,128)(2,1)}, u32[]{:S(2)}, u32[]{:S(2)}) collective-permute-start(bf16[3,96,1024]{2,1,0:T(8,128)(2,1)} %collective-permute-done.71.refs_7_), channel_id=1, source_target_pairs={{0,8},{4,12},{8,0},{12,4},{16,24},{20,28},{24,16},{28,20},{1,9},{5... | collective-permute-start | bytes 1769480 | tf_op jit(solution)/shard_map/ppermute | solution.py:517
  310.2 21.1 %shard_map.257 = (bf16[2560,1024]{1,0:T(8,128)(2,1)}, bf16[2560,1024]{1,0:T(8,128)(2,1)}, bf16[2560,768]{1,0:T(8,128)(2,1)}, bf16[2560,384]{1,0:T(8,128)(2,1)}, f32[2560,8]{1,0:T(8,128)}) custom-call(s32[4]{0:T(128)} %pad_add_fusion.1.idx.refs_0_, bf16[2560,1024]{1,0:T(8,128)(2,1)} %copy-done.67, bf16[2560,1024]{1,0:T(8,128)(2,1)} %slice_dynamic-update-slice_fusion.refs_2_, ...), custom_call_target="tpu_custom_call" | custom-call | flops 12079595520 | bytes 41943040 | tf_op jit(solution)/shard_map/pallas_call | solution.py:856
  331.4 8.1 %convolution_convert_fusion.5 = bf16[768,1024]{1,0:T(8,128)(2,1)S(1)} fusion(bf16[2560,768]{1,0:T(8,128)(2,1)} %get-tuple-element.59, bf16[2560,1024]{1,0:T(8,128)(2,1)} %copy-done.67), kind=kOutput, calls=%fused_computation.74 | convolution fusion | flops 4027318272 | bytes 10747904 | tf_op jit(solution)/shard_map/dot_general | solution.py:537
  344.7 13.4 %collective-permute-done.78.refs_9_ = bf16[3,96,1024]{2,1,0:T(8,128)(2,1)} collective-permute-done((bf16[3,96,1024]{2,1,0:T(8,128)(2,1)}, bf16[3,96,1024]{2,1,0:T(8,128)(2,1)}, u32[]{:S(2)}, u32[]{:S(2)}) %collective-permute-start.78) | collective-permute-done | bytes 589856 | tf_op jit(solution)/shard_map/ppermute | solution.py:517
  358.2 22.4 %shard_map.258 = (bf16[2560,1024]{1,0:T(8,128)(2,1)}, bf16[2560,1024]{1,0:T(8,128)(2,1)}, bf16[2560,768]{1,0:T(8,128)(2,1)}, bf16[2560,384]{1,0:T(8,128)(2,1)}, f32[2560,8]{1,0:T(8,128)}) custom-call(s32[4]{0:T(128)} %pad_add_fusion.1.idx.refs_0_, bf16[2560,1024]{1,0:T(8,128)(2,1)} %copy-done.67, bf16[2560,1024]{1,0:T(8,128)(2,1)} %slice_dynamic-update-slice_fusion.refs_2_, ...), custom_call_target="tpu_custom_call" | custom-call | flops 12079595520 | bytes 41943040 | tf_op jit(solution)/shard_map/pallas_call | solution.py:856
  381.4 26.7 %shard_map.259 = (bf16[2560,1024]{1,0:T(8,128)(2,1)}, bf16[2560,1024]{1,0:T(8,128)(2,1)}, bf16[2560,768]{1,0:T(8,128)(2,1)}, bf16[2560,384]{1,0:T(8,128)(2,1)}, f32[2560,8]{1,0:T(8,128)}) custom-call(s32[4]{0:T(128)} %pad_add_fusion.1.idx.refs_0_, bf16[2560,1024]{1,0:T(8,128)(2,1)} %copy-done.67, bf16[2560,1024]{1,0:T(8,128)(2,1)} %slice_dynamic-update-slice_fusion.refs_2_, ...), custom_call_target="tpu_custom_call" | custom-call | flops 12079595520 | bytes 41943040 | tf_op jit(solution)/shard_map/pallas_call | solution.py:856
  435.8 7.9 %collective-permute-done.122 = bf16[3,96,1024]{2,1,0:T(8,128)(2,1)S(1)} collective-permute-done((bf16[3,96,1024]{2,1,0:T(8,128)(2,1)S(1)}, bf16[3,96,1024]{2,1,0:T(8,128)(2,1)S(1)}, u32[]{:S(2)}, u32[]{:S(2)}) %collective-permute-start.122) | collective-permute-done | bytes 589856 | tf_op jit(solution)/shard_map/ppermute | solution.py:517
  444.0 25.1 %collective-permute-done.127 = bf16[3,96,1024]{2,1,0:T(8,128)(2,1)S(1)} collective-permute-done((bf16[3,96,1024]{2,1,0:T(8,128)(2,1)S(1)}, bf16[3,96,1024]{2,1,0:T(8,128)(2,1)S(1)}, u32[]{:S(2)}, u32[]{:S(2)}) %collective-permute-start.127) | collective-permute-done | bytes 589856 | tf_op jit(solution)/shard_map/ppermute | solution.py:517
  487.5 21.3 %collective-permute-start.119 = (bf16[3,96,1024]{2,1,0:T(8,128)(2,1)S(1)}, bf16[3,96,1024]{2,1,0:T(8,128)(2,1)S(1)}, u32[]{:S(2)}, u32[]{:S(2)}) collective-permute-start(bf16[3,96,1024]{2,1,0:T(8,128)(2,1)S(1)} %fusion.45), channel_id=1, source_target_pairs={{0,8},{4,12},{8,0},{12,4},{16,24},{20,28},{24,16},{28,20},{1,9},{5... | collective-permute-start | bytes 1769480 | tf_op jit(solution)/shard_map/ppermute | solution.py:517
  581.0 17.2 %shard_map.260 = (bf16[320,1024]{1,0:T(8,128)(2,1)}, bf16[768,1024]{1,0:T(8,128)(2,1)}, bf16[768,1024]{1,0:T(8,128)(2,1)}, f32[16,2,8,1024]{3,2,1,0:T(8,128)}) custom-call(bf16[16,320,768]{2,1,0:T(8,128)(2,1)} %get-tuple-element.53.p_ref, bf16[320,1024]{1,0:T(8,128)(2,1)} %convolution_convert_fusion.11.q_ref, bf16[768,1024]{1,0:T(8,128)(2,1)} %fusion.22.k_ref, ...), custom_call_target="tpu_custom_call" | custom-call | flops 2516582400 | bytes 14680064 | tf_op jit(solution)/shard_map/pallas_call | solution.py:684
  654.7 7.3 collective-permute-done.100
  706.7 21.5 %collective-permute-done.114 = f32[8,1024]{1,0:T(8,128)S(1)} collective-permute-done((f32[8,1024]{1,0:T(8,128)S(1)}, f32[8,1024]{1,0:T(8,128)S(1)}, u32[]{:S(2)}, u32[]{:S(2)}) %collective-permute-start.114) | collective-permute-done | bytes 32800 | tf_op jit(solution)/shard_map/ppermute | solution.py:505
  738.8 7.9 %collective-permute-done.106 = bf16[2,256,4,128]{1,3,2,0:T(8,128)(2,1)S(1)} collective-permute-done((bf16[2,256,4,128]{1,3,2,0:T(8,128)(2,1)S(1)}, bf16[2,256,4,128]{1,3,2,0:T(8,128)(2,1)S(1)}, u32[]{:S(2)}, u32[]{:S(2)}) %collective-permute-start.106) | collective-permute-done | bytes 524320 | tf_op jit(solution)/shard_map/ppermute | solution.py:505
  759.0 7.1 collective-permute-done.110
  (745 shorter events, 448.9 us)
Async XLA Ops:
  2.4 43.4 %collective-permute-start.36 = (bf16[64,1024]{1,0:T(8,128)(2,1)}, bf16[64,1024]{1,0:T(8,128)(2,1)}, u32[]{:S(2)}, u32[]{:S(2)}) collective-permute-start(bf16[64,1024]{1,0:T(8,128)(2,1)} %get-tuple-element.162), channel_id=1, source_target_pairs={{0,8},{4,12},{8,16},{12,20},{16,24},{20,28},{24,0},{28,4},{1,9},{5... | collective-permute-start | bytes 393224 | tf_op jit(solution)/shard_map/ppermute | solution.py:525
  5.4 36.2 %collective-permute-start.34 = (bf16[64,1024]{1,0:T(8,128)(2,1)}, bf16[64,1024]{1,0:T(8,128)(2,1)}, u32[]{:S(2)}, u32[]{:S(2)}) collective-permute-start(bf16[64,1024]{1,0:T(8,128)(2,1)} %get-tuple-element.162), channel_id=1, source_target_pairs={{0,16},{4,20},{8,24},{12,28},{16,0},{20,4},{24,8},{28,12},{1,17},{... | collective-permute-start | bytes 393224 | tf_op jit(solution)/shard_map/ppermute | solution.py:525
  12.5 42.1 %collective-permute-start.23 = (bf16[4,256,128]{2,1,0:T(8,128)(2,1)}, bf16[4,256,128]{2,1,0:T(8,128)(2,1)}, u32[]{:S(2)}, u32[]{:S(2)}) collective-permute-start(bf16[4,256,128]{2,1,0:T(8,128)(2,1)} %pad_maximum_fusion.8.refs_0_), channel_id=1, source_target_pairs={{0,24},{4,28},{8,0},{12,4},{16,8},{20,12},{24,16},{28,20},{1,25},{... | collective-permute-start | bytes 786440 | tf_op jit(solution)/shard_map/ppermute | solution.py:525
  132.6 43.6 %collective-permute-start.62 = (bf16[176,1024]{1,0:T(8,128)(2,1)S(1)}, bf16[176,1024]{1,0:T(8,128)(2,1)S(1)}, u32[]{:S(2)}, u32[]{:S(2)}) collective-permute-start(bf16[176,1024]{1,0:T(8,128)(2,1)S(1)} %get-tuple-element.154), channel_id=1, source_target_pairs={{0,1},{1,0},{2,3},{3,2},{4,5},{5,4},{6,7},{7,6},{8,9},{9,8},{10,11... | collective-permute-start | bytes 1081352 | tf_op jit(solution)/shard_map/ppermute | solution.py:513
  133.0 49.5 %collective-permute-start.60 = (bf16[176,1024]{1,0:T(8,128)(2,1)S(1)}, bf16[176,1024]{1,0:T(8,128)(2,1)S(1)}, u32[]{:S(2)}, u32[]{:S(2)}) collective-permute-start(bf16[176,1024]{1,0:T(8,128)(2,1)S(1)} %get-tuple-element.154), channel_id=1, source_target_pairs={{0,4},{4,0},{8,12},{12,8},{16,20},{20,16},{24,28},{28,24},{1,5},{5... | collective-permute-start | bytes 1081352 | tf_op jit(solution)/shard_map/ppermute | solution.py:505
  207.4 57.6 %collective-permute-start.70 = (bf16[3,96,1024]{2,1,0:T(8,128)(2,1)S(1)}, bf16[3,96,1024]{2,1,0:T(8,128)(2,1)}, u32[]{:S(2)}, u32[]{:S(2)}) collective-permute-start(bf16[3,96,1024]{2,1,0:T(8,128)(2,1)S(1)} %squeeze.265.refs_4_), channel_id=1, source_target_pairs={{0,0},{4,4},{8,16},{12,20},{16,8},{20,12},{24,24},{28,28},{1,1},{5... | collective-permute-start | bytes 1769480 | tf_op jit(solution)/shard_map/ppermute | solution.py:521
  209.0 57.5 %collective-permute-start.69 = (bf16[3,96,1024]{2,1,0:T(8,128)(2,1)S(1)}, bf16[3,96,1024]{2,1,0:T(8,128)(2,1)}, u32[]{:S(2)}, u32[]{:S(2)}) collective-permute-start(bf16[3,96,1024]{2,1,0:T(8,128)(2,1)S(1)} %squeeze.265.refs_4_), channel_id=1, source_target_pairs={{0,8},{4,12},{8,0},{12,4},{16,24},{20,28},{24,16},{28,20},{1,9},{5... | collective-permute-start | bytes 1769480 | tf_op jit(solution)/shard_map/ppermute | solution.py:517
  233.9 44.5 %collective-permute-start.80 = (bf16[3,96,1024]{2,1,0:T(8,128)(2,1)S(1)}, bf16[3,96,1024]{2,1,0:T(8,128)(2,1)}, u32[]{:S(2)}, u32[]{:S(2)}) collective-permute-start(bf16[3,96,1024]{2,1,0:T(8,128)(2,1)S(1)} %squeeze.267.refs_4_), channel_id=1, source_target_pairs={{0,0},{4,4},{8,16},{12,20},{16,8},{20,12},{24,24},{28,28},{1,1},{5... | collective-permute-start | bytes 1769480 | tf_op jit(solution)/shard_map/ppermute | solution.py:521
  283.3 97.3 %collective-permute-start.72 = (bf16[3,96,1024]{2,1,0:T(8,128)(2,1)}, bf16[3,96,1024]{2,1,0:T(8,128)(2,1)S(1)}, u32[]{:S(2)}, u32[]{:S(2)}) collective-permute-start(bf16[3,96,1024]{2,1,0:T(8,128)(2,1)} %collective-permute-done.70.refs_6_), channel_id=1, source_target_pairs={{0,8},{4,12},{8,0},{12,4},{16,24},{20,28},{24,16},{28,20},{1,9},{5... | collective-permute-start | bytes 1769480 | tf_op jit(solution)/shard_map/ppermute | solution.py:517
  285.3 58.6 %collective-permute-start.77 = (bf16[3,96,1024]{2,1,0:T(8,128)(2,1)}, bf16[3,96,1024]{2,1,0:T(8,128)(2,1)}, u32[]{:S(2)}, u32[]{:S(2)}) collective-permute-start(bf16[3,96,1024]{2,1,0:T(8,128)(2,1)} %collective-permute-done.75.refs_6_), channel_id=1, source_target_pairs={{0,8},{4,12},{8,0},{12,4},{16,24},{20,28},{24,16},{28,20},{1,9},{5... | collective-permute-start | bytes 1769480 | tf_op jit(solution)/shard_map/ppermute | solution.py:517
  297.9 82.6 %collective-permute-start.73 = (bf16[3,96,1024]{2,1,0:T(8,128)(2,1)}, bf16[3,96,1024]{2,1,0:T(8,128)(2,1)}, u32[]{:S(2)}, u32[]{:S(2)}) collective-permute-start(bf16[3,96,1024]{2,1,0:T(8,128)(2,1)} %collective-permute-done.71.refs_7_), channel_id=1, source_target_pairs={{0,8},{4,12},{8,0},{12,4},{16,24},{20,28},{24,16},{28,20},{1,9},{5... | collective-permute-start | bytes 1769480 | tf_op jit(solution)/shard_map/ppermute | solution.py:517
  308.6 49.6 %collective-permute-start.78 = (bf16[3,96,1024]{2,1,0:T(8,128)(2,1)}, bf16[3,96,1024]{2,1,0:T(8,128)(2,1)}, u32[]{:S(2)}, u32[]{:S(2)}) collective-permute-start(bf16[3,96,1024]{2,1,0:T(8,128)(2,1)} %collective-permute-done.76.refs_7_), channel_id=1, source_target_pairs={{0,8},{4,12},{8,0},{12,4},{16,24},{20,28},{24,16},{28,20},{1,9},{5... | collective-permute-start | bytes 1769480 | tf_op jit(solution)/shard_map/ppermute | solution.py:517
  342.7 88.3 %collective-permute-start.117 = (bf16[3,96,1024]{2,1,0:T(8,128)(2,1)}, bf16[3,96,1024]{2,1,0:T(8,128)(2,1)}, u32[]{:S(2)}, u32[]{:S(2)}) collective-permute-start(bf16[3,96,1024]{2,1,0:T(8,128)(2,1)} %get-tuple-element.124), channel_id=1, source_target_pairs={{0,8},{4,12},{8,0},{12,4},{16,24},{20,28},{24,16},{28,20},{1,9},{5... | collective-permute-start | bytes 1769480 | tf_op jit(solution)/shard_map/ppermute | solution.py:517
  343.9 90.5 %collective-permute-start.120 = (bf16[3,96,1024]{2,1,0:T(8,128)(2,1)S(1)}, bf16[3,96,1024]{2,1,0:T(8,128)(2,1)}, u32[]{:S(2)}, u32[]{:S(2)}) collective-permute-start(bf16[3,96,1024]{2,1,0:T(8,128)(2,1)S(1)} %get-tuple-element.125), channel_id=1, source_target_pairs={{0,8},{4,12},{8,0},{12,4},{16,24},{20,28},{24,16},{28,20},{1,9},{5... | collective-permute-start | bytes 1769480 | tf_op jit(solution)/shard_map/ppermute | solution.py:517
  427.5 42.6 %collective-permute-start.125 = (bf16[3,96,1024]{2,1,0:T(8,128)(2,1)S(1)}, bf16[3,96,1024]{2,1,0:T(8,128)(2,1)S(1)}, u32[]{:S(2)}, u32[]{:S(2)}) collective-permute-start(bf16[3,96,1024]{2,1,0:T(8,128)(2,1)S(1)} %get-tuple-element.123), channel_id=1, source_target_pairs={{0,8},{4,12},{8,0},{12,4},{16,24},{20,28},{24,16},{28,20},{1,9},{5... | collective-permute-start | bytes 1769480 | tf_op jit(solution)/shard_map/ppermute | solution.py:517
  429.6 39.4 %collective-permute-start.127 = (bf16[3,96,1024]{2,1,0:T(8,128)(2,1)S(1)}, bf16[3,96,1024]{2,1,0:T(8,128)(2,1)S(1)}, u32[]{:S(2)}, u32[]{:S(2)}) collective-permute-start(bf16[3,96,1024]{2,1,0:T(8,128)(2,1)S(1)} %get-tuple-element.120), channel_id=1, source_target_pairs={{0,8},{4,12},{8,0},{12,4},{16,24},{20,28},{24,16},{28,20},{1,9},{5... | collective-permute-start | bytes 1769480 | tf_op jit(solution)/shard_map/ppermute | solution.py:517
  431.0 45.1 %collective-permute-start.130 = (bf16[3,96,1024]{2,1,0:T(8,128)(2,1)S(1)}, bf16[3,96,1024]{2,1,0:T(8,128)(2,1)S(1)}, u32[]{:S(2)}, u32[]{:S(2)}) collective-permute-start(bf16[3,96,1024]{2,1,0:T(8,128)(2,1)S(1)} %get-tuple-element.121), channel_id=1, source_target_pairs={{0,8},{4,12},{8,0},{12,4},{16,24},{20,28},{24,16},{28,20},{1,9},{5... | collective-permute-start | bytes 1769480 | tf_op jit(solution)/shard_map/ppermute | solution.py:517
  434.5 47.0 %collective-permute-start.92 = (bf16[4,160,1024]{2,1,0:T(8,128)(2,1)S(1)}, bf16[4,160,1024]{2,1,0:T(8,128)(2,1)S(1)}, u32[]{:S(2)}, u32[]{:S(2)}) collective-permute-start(bf16[4,160,1024]{2,1,0:T(8,128)(2,1)S(1)} %get-tuple-element.113), channel_id=1, source_target_pairs={{0,1},{1,0},{2,3},{3,2},{4,5},{5,4},{6,7},{7,6},{8,9},{9,8},{10,11... | collective-permute-start | bytes 3932168 | tf_op jit(solution)/shard_map/ppermute | solution.py:513
  443.8 43.7 %collective-permute-start.96 = (bf16[4,160,1024]{2,1,0:T(8,128)(2,1)S(1)}, bf16[4,160,1024]{2,1,0:T(8,128)(2,1)S(1)}, u32[]{:S(2)}, u32[]{:S(2)}) collective-permute-start(bf16[4,160,1024]{2,1,0:T(8,128)(2,1)S(1)} %get-tuple-element.114), channel_id=1, source_target_pairs={{0,1},{1,0},{2,3},{3,2},{4,5},{5,4},{6,7},{7,6},{8,9},{9,8},{10,11... | collective-permute-start | bytes 3932168 | tf_op jit(solution)/shard_map/ppermute | solution.py:513
  479.7 49.7 %collective-permute-start.121 = (bf16[3,96,1024]{2,1,0:T(8,128)(2,1)S(1)}, bf16[3,96,1024]{2,1,0:T(8,128)(2,1)S(1)}, u32[]{:S(2)}, u32[]{:S(2)}) collective-permute-start(bf16[3,96,1024]{2,1,0:T(8,128)(2,1)S(1)} %add_convert_fusion.4), channel_id=1, source_target_pairs={{0,0},{4,4},{8,16},{12,20},{16,8},{20,12},{24,24},{28,28},{1,1},{5... | collective-permute-start | bytes 1769480 | tf_op jit(solution)/shard_map/ppermute | solution.py:521
  481.5 59.8 %collective-permute-start.126 = (bf16[3,96,1024]{2,1,0:T(8,128)(2,1)}, bf16[3,96,1024]{2,1,0:T(8,128)(2,1)}, u32[]{:S(2)}, u32[]{:S(2)}) collective-permute-start(bf16[3,96,1024]{2,1,0:T(8,128)(2,1)} %add_convert_fusion.2), channel_id=1, source_target_pairs={{0,0},{4,4},{8,16},{12,20},{16,8},{20,12},{24,24},{28,28},{1,1},{5... | collective-permute-start | bytes 1769480 | tf_op jit(solution)/shard_map/ppermute | solution.py:521
  487.5 48.7 %collective-permute-start.119 = (bf16[3,96,1024]{2,1,0:T(8,128)(2,1)S(1)}, bf16[3,96,1024]{2,1,0:T(8,128)(2,1)S(1)}, u32[]{:S(2)}, u32[]{:S(2)}) collective-permute-start(bf16[3,96,1024]{2,1,0:T(8,128)(2,1)S(1)} %fusion.45), channel_id=1, source_target_pairs={{0,8},{4,12},{8,0},{12,4},{16,24},{20,28},{24,16},{28,20},{1,9},{5... | collective-permute-start | bytes 1769480 | tf_op jit(solution)/shard_map/ppermute | solution.py:517
  633.1 62.4 %collective-permute-start.104 = (bf16[4,2,256,1024]{2,3,1,0:T(8,128)(2,1)}, bf16[4,2,256,1024]{2,3,1,0:T(8,128)(2,1)}, u32[]{:S(2)}, u32[]{:S(2)}) collective-permute-start(bf16[4,2,256,1024]{2,3,1,0:T(8,128)(2,1)} %dynamic-slice_bitcast_fusion), channel_id=1, source_target_pairs={{0,1},{1,0},{2,3},{3,2},{4,5},{5,4},{6,7},{7,6},{8,9},{9,8},{10,11... | collective-permute-start | bytes 12582920 | tf_op jit(solution)/shard_map/ppermute | solution.py:513
  641.1 43.2 %collective-permute-start.132 = (bf16[3,3,96,256]{3,2,1,0:T(8,128)(2,1)}, bf16[3,3,96,256]{3,2,1,0:T(8,128)(2,1)}, u32[]{:S(2)}, u32[]{:S(2)}) collective-permute-start(bf16[3,3,96,256]{3,2,1,0:T(8,128)(2,1)} %bitcast.504), channel_id=1, source_target_pairs={{0,1},{1,0},{2,3},{3,2},{4,5},{5,4},{6,7},{7,6},{8,9},{9,8},{10,11... | collective-permute-start | bytes 1327112 | tf_op jit(solution)/shard_map/ppermute | solution.py:513
  (216 other events, 4164.7 us)

commit v3 on v0

--- a/solution.py
+++ b/solution.py
@@ -1,6 +1,10 @@
+import functools
+
 import jax
 import jax.numpy as jnp
 from jax import lax
+from jax.experimental import pallas as pl
+from jax.experimental.pallas import tpu as pltpu
 from jax.sharding import PartitionSpec as P
 
 HEADS = 16
@@ -484,9 +488,797 @@
     )
 
 
+BF = jnp.bfloat16
+F32 = jnp.float32
+FAST_CTX = 8
+FAST_WT = 4
+NEG = -1e30
+
+SWAP_Y = [(i, i ^ 1) for i in range(8)]
+LINES_Z = [[0, 2, 4, 6], [1, 3, 5, 7]]
+PAIR_Z = [(i, i ^ 2) for i in range(8)]
+FLIP_Z = [(i, i ^ 6) for i in range(8)]
+SWAP_C = [(i, i ^ 1) for i in range(4)]
+SWAP_X = [(i, i ^ 2) for i in range(4)]
+
+
+def move_y(v):
+    return lax.ppermute(v, "ctx", SWAP_Y)
+
+
+def move_x(v):
+    return lax.ppermute(v, "wt", SWAP_X)
+
+
+def move_c(v):
+    return lax.ppermute(v, "wt", SWAP_C)
+
+
+def pair_z(v):
+    return lax.ppermute(v, "ctx", PAIR_Z)
+
+
+def flip_z(v):
+    return lax.ppermute(v, "ctx", FLIP_Z)
+
+
+def phase(*vals):
+    return lax.optimization_barrier(vals)
+
+
+def dot_nt(a, b):
+    return lax.dot_general(a, b, (((1,), (1,)), ((), ())), preferred_element_type=F32)
+
+
+def dot_tn(a, b):
+    return lax.dot_general(a, b, (((0,), (0,)), ((), ())), preferred_element_type=F32)
+
+
+def dot_nn(a, b):
+    return jnp.dot(a, b, preferred_element_type=F32)
+
+
+def params(limit=56 * 2**20):
+    return pltpu.CompilerParams(vmem_limit_bytes=limit)
+
+
+COST_S = pl.CostEstimate(flops=10**6, bytes_accessed=10**6, transcendentals=0)
+COST_E = pl.CostEstimate(flops=10**6, bytes_accessed=10**6, transcendentals=0)
+ANY = pl.BlockSpec(memory_space=pl.ANY)
+SMEM = pl.BlockSpec(memory_space=pltpu.SMEM)
+
+
+def spread_z(v):
+    near, opp = pair_z(v), flip_z(v)
+    return {0: v, 1: near, 3: opp, 2: pair_z(opp)}
+
+
+def attend_kernel(sz, first, x_first, idx, n_ref, w_ref, *refs):
+    pieces, refs = refs[:2], refs[2:]
+    if not first:
+        refs = refs[4:]
+    p_ref, o_ref, qkv_ref, wt_ref, bc_ref, bp_ref, qs_ref = refs
+    z, y, x, c = idx[0], idx[1], idx[2], idx[3]
+    step = pl.program_id(0)
+    for ry in range(2):
+
+        @pl.when(step == ry)
+        def _(ry=ry):
+            for rx in range(2):
+                for rc in range(2):
+                    row = pl.multiple_of(((x ^ rx) * 2 + (c ^ rc)) * 256, 256)
+                    for t in range(3):
+                        block = pieces[rc][ry, rx, t] if x_first else pieces[rc][rx, ry, t]
+                        wt_ref[0, pl.ds(row, 256), 128 * t : 128 * t + 128] = block
+
+    qkv = dot_nn(n_ref[...], wt_ref[0]).astype(BF)
+    qkv_ref[0] = qkv
+    k, v = qkv[:, 128:256], qkv[:, 256:]
+    qs_ref[...] = qkv[:, :128]
+    q_c = qs_ref[512:, :]
+    q_p = qs_ref[pl.ds(pl.multiple_of((z * 2 + y) * 64, 64), 64), :]
+    lane = lax.broadcasted_iota(jnp.int32, (1, 128), 1)
+    outs = []
+    for h in range(2):
+        base_c, base_p = w_ref[h, 0], w_ref[h, 1]
+        for a in range(32):
+            bc_ref[8 * a : 8 * a + 8, :] = pltpu.roll(base_c, 1024 - (248 - 8 * a), 1)[:, :768]
+        for a in range(8):
+            shift = 56 - 8 * a
+            bp_ref[8 * a : 8 * a + 8, :] = (pltpu.roll(base_p, 1024 - shift, 1) if shift else base_p)[:, :512]
+        mine = (lane < 64) if h == 0 else (lane >= 64)
+        head = lambda t: jnp.where(mine, t, jnp.zeros_like(t))
+        sc = dot_nt(head(q_c), k) * 0.125 + bc_ref[...]
+        sp = dot_nt(head(q_p), k[:512]) * 0.125 + bp_ref[...]
+
+        def soft(t):
+            e = jnp.exp(t - jnp.max(t, axis=-1, keepdims=True))
+            return (e * (1.0 / jnp.sum(e, axis=-1, keepdims=True))).astype(BF)
+
+        pc, pp = soft(sc), soft(sp)
+        p_ref[h, 64:, :] = pc
+        p_ref[h, :64, :512] = pp
+        p_ref[h, :64, 512:] = jnp.zeros((64, 256), BF)
+        outs.append(jnp.concatenate([dot_nn(pp, v[:512]), dot_nn(pc, v)], axis=0))
+    o_ref[...] = jnp.where(lane < 64, outs[0], outs[1]).astype(BF)
+
+
+def attend(sz, x_first, idx, normed, windows, pieces, prev):
+    keys, rows = normed.shape[0], 320
+    at = lambda i, d: (d[0] ^ sz) * 2 + (d[1] ^ i)
+    whole = pl.BlockSpec(memory_space=pltpu.VMEM)
+    return pl.pallas_call(
+        functools.partial(attend_kernel, sz, prev is None, x_first),
+        grid_spec=pltpu.PrefetchScalarGridSpec(
+            num_scalar_prefetch=1,
+            grid=(2,),
+            in_specs=[whole, pl.BlockSpec((2, 2, 8, 1024), lambda i, d: (at(i, d), 0, 0, 0))]
+            + [whole] * 2
+            + ([] if prev is None else [ANY] * 4),
+            out_specs=(
+                pl.BlockSpec((2, rows, keys), lambda i, d: (at(i, d), 0, 0)),
+                pl.BlockSpec((rows, 128), lambda i, d: (0, at(i, d))),
+                pl.BlockSpec((1, keys, 384), lambda i, d: (at(i, d), 0, 0)),
+                pl.BlockSpec((1, 1024, 384), lambda i, d: (at(i, d), 0, 0)),
+            ),
+            scratch_shapes=[pltpu.VMEM((256, 768), F32), pltpu.VMEM((64, 512), F32), pltpu.VMEM((keys, 128), BF)],
+        ),
+        out_shape=(
+            jax.ShapeDtypeStruct((16, rows, keys), BF),
+            jax.ShapeDtypeStruct((rows, 1024), BF),
+            jax.ShapeDtypeStruct((8, keys, 384), BF),
+            jax.ShapeDtypeStruct((8, 1024, 384), BF),
+        ),
+        input_output_aliases={} if prev is None else {5 + n: n for n in range(4)},
+        compiler_params=params(),
+        cost_estimate=COST_S,
+    )(idx, normed, windows, *pieces, *([] if prev is None else prev))
+
+
+def attend_back_kernel(first, idx, n_ref, p_ref, qkv_ref, wt_ref, g_ref, m_ref, gl_ref, *refs):
+    if not first:
+        gn_prev, refs = refs[0], refs[2:]
+    keep_ref, send_ref, gn_ref, db_ref, dt_ref, qs_ref = refs
+    z, y, x, c = idx[0], idx[1], idx[2], idx[3]
+    own = pl.ds(pl.multiple_of((z * 2 + y) * 64, 64), 64)
+    qkv = qkv_ref[0]
+    k, v = qkv[:, 128:256], qkv[:, 256:]
+    qs_ref[...] = qkv[:, :128]
+    q = jnp.concatenate([qs_ref[own, :], qs_ref[512:, :]], axis=0)
+    g = g_ref[...]
+    lane = lax.broadcasted_iota(jnp.int32, (1, 128), 1)
+    parts = []
+    for h in range(2):
+        mine = (lane < 64) if h == 0 else (lane >= 64)
+        gh = jnp.where(mine, g, jnp.zeros_like(g))
+        p = p_ref[h]
+        pf = p.astype(F32)
+        dp = dot_nt(gh, v)
+        delta = jnp.sum(pf * dp, axis=-1, keepdims=True)
+        ds = pf * (dp - delta)
+        low = ds.astype(BF)
+        acc_c = jnp.zeros((8, 1024), F32)
+        for a in range(32):
+            part = jnp.concatenate([ds[64 + 8 * a : 72 + 8 * a], jnp.zeros((8, 256), F32)], axis=1)
+            acc_c = acc_c + pltpu.roll(part, 248 - 8 * a, 1) if a < 31 else acc_c + part
+        acc_p = jnp.zeros((8, 1024), F32)
+        for a in range(8):
+            part = jnp.concatenate([ds[8 * a : 8 * a + 8, :512], jnp.zeros((8, 512), F32)], axis=1)
+            acc_p = acc_p + (pltpu.roll(part, 56 - 8 * a, 1) if a < 7 else part)
+        db_ref[h, 0] = acc_c
+        db_ref[h, 1] = acc_p
+        parts.append((dot_nn(low, k) * 0.125, dot_tn(low, q) * 0.125, dot_tn(p, g)))
+    dq, dk, dv = [jnp.where(lane < 64, parts[0][n], parts[1][n]).astype(BF) for n in range(3)]
+    dt_ref[:512, :128] = jnp.zeros((512, 128), BF)
+    dt_ref[own, :128] = dq[:64]
+    dt_ref[512:, :128] = dq[64:]
+    dt_ref[:, 128:256] = dk
+    dt_ref[:, 256:] = dv
+    dt = dt_ref[...]
+    dw = jnp.concatenate([dot_tn(n_ref[...], dt).astype(BF), dot_tn(m_ref[...], gl_ref[...]).astype(BF)], axis=1)
+    for xx in range(2):
+        for cc in range(2):
+            block = dw[(xx * 2 + cc) * 256 : (xx * 2 + cc) * 256 + 256]
+
+            @pl.when(c == cc)
+            def _():
+                keep_ref[x ^ xx, 0] = block
+
+            @pl.when(c != cc)
+            def _():
+                send_ref[x ^ xx, 0] = block
+
+    gn = dot_nt(dt, wt_ref[0])
+
+    @pl.when(pl.program_id(0) == 0)
+    def _():
+        gn_ref[...] = gn if first else gn_prev[...] + gn
+
+    @pl.when(pl.program_id(0) != 0)
+    def _():
+        gn_ref[...] += gn
+
+
+def attend_back(base, count, idx, normed, p, qkv, wt, g, mixed, g_low, gn_prev, db_prev):
+    rows, keys = p.shape[1], p.shape[2]
+    at = lambda i, d: (i + base) ^ (d[0] * 2 + d[1])
+    whole = pl.BlockSpec((keys, 1024), lambda i, d: (0, 0))
+    return pl.pallas_call(
+        functools.partial(attend_back_kernel, gn_prev is None),
+        grid_spec=pltpu.PrefetchScalarGridSpec(
+            num_scalar_prefetch=1,
+            grid=(count,),
+            in_specs=[
+                whole,
+                pl.BlockSpec((2, rows, keys), lambda i, d: (at(i, d), 0, 0)),
+                pl.BlockSpec((1, keys, 384), lambda i, d: (at(i, d), 0, 0)),
+                pl.BlockSpec((1, 1024, 384), lambda i, d: (at(i, d), 0, 0)),
+                pl.BlockSpec((rows, 128), lambda i, d: (0, at(i, d))),
+                pl.BlockSpec((rows, 1024), lambda i, d: (0, 0)),
+                pl.BlockSpec((rows, 128), lambda i, d: (0, at(i, d))),
+            ]
+            + ([] if gn_prev is None else [whole, ANY]),
+            out_specs=(
+                pl.BlockSpec((2, 1, 256, 512), lambda i, d: (0, i, 0, 0)),
+                pl.BlockSpec((2, 1, 256, 512), lambda i, d: (0, i, 0, 0)),
+                whole,
+                pl.BlockSpec((2, 2, 8, 1024), lambda i, d: (at(i, d), 0, 0, 0)),
+            ),
+            scratch_shapes=[pltpu.VMEM((keys, 384), BF), pltpu.VMEM((keys, 128), BF)],
+        ),
+        out_shape=(
+            jax.ShapeDtypeStruct((2, count, 256, 512), BF),
+            jax.ShapeDtypeStruct((2, count, 256, 512), BF),
+            jax.ShapeDtypeStruct((keys, 1024), F32),
+            jax.ShapeDtypeStruct((16, 2, 8, 1024), F32),
+        ),
+        input_output_aliases={} if gn_prev is None else {9: 3},
+        compiler_params=params(),
+        cost_estimate=COST_E,
+    )(idx, normed, p, qkv, wt, g, mixed, g_low, *([] if gn_prev is None else [gn_prev, db_prev]))
+
+
+def cut_rows(t):
+    return t[:, :, :, :128], t[:, :, :, 128:]
+
+
+def out_back_kernel(a_ref, b_ref, c_ref, h_ref, gain_ref, cot_ref, w_ref, gh_ref, gl_ref, gm_ref, gg_ref):
+    f = lambda t: t.astype(F32)
+    dn = f(a_ref[...]) + f(b_ref[...]) + f(c_ref[...])
+    hidden, gain = h_ref[...], gain_ref[...]
+    scale = lax.rsqrt(jnp.mean(hidden * hidden, axis=-1, keepdims=True) + epsilon)
+    unit = hidden * scale
+    gg_ref[...] = jnp.broadcast_to(jnp.sum(dn * unit, axis=0, keepdims=True), gg_ref.shape)
+    du = dn * gain
+    grad = f(cot_ref[...]) + scale * (du - unit * jnp.mean(du * unit, axis=-1, keepdims=True))
+    gh_ref[...] = grad
+    low = grad.astype(BF)
+    gl_ref[...] = low
+    gm_ref[...] = dot_nt(low, w_ref[...]).astype(BF)
+
+
+def out_back(parts, hidden, gain, cot, w_o):
+    whole = pl.BlockSpec(memory_space=pltpu.VMEM)
+    return pl.pallas_call(
+        out_back_kernel,
+        in_specs=[whole] * 7,
+        out_specs=(whole,) * 4,
+        out_shape=(
+            jax.ShapeDtypeStruct((320, 1024), F32),
+            jax.ShapeDtypeStruct((320, 1024), BF),
+            jax.ShapeDtypeStruct((320, 1024), BF),
+            jax.ShapeDtypeStruct((8, 1024), F32),
+        ),
+        compiler_params=params(),
+        cost_estimate=COST_S,
+    )(*parts, hidden, gain[None], cot, w_o)
+
+
+def out_kernel(idx, m_ref, s_ref, g_ref, a_ref, b_ref, h_ref, l_ref, w_ref):
+    z, y, x, c = idx[0], idx[1], idx[2], idx[3]
+    for rx in range(2):
+        for ry in range(2):
+            for n, sz in enumerate((0, 1, 3, 2)):
+                col = pl.multiple_of(((z ^ sz) * 2 + (y ^ ry)) * 128, 128)
+                for rc, ref in ((0, a_ref), (1, b_ref)):
+                    row = pl.multiple_of(((x ^ rx) * 2 + (c ^ rc)) * 256, 256)
+                    w_ref[pl.ds(row, 256), pl.ds(col, 128)] = ref[rx, ry, n]
+    hidden = s_ref[...].astype(F32) + dot_nn(m_ref[...], w_ref[...])
+    h_ref[...] = hidden
+    scale = lax.rsqrt(jnp.mean(hidden * hidden, axis=-1, keepdims=True) + epsilon)
+    l_ref[...] = (hidden * scale * g_ref[...]).astype(BF)
+
+
+def project_out(idx, mixed, rows_own, gain, own, other):
+    whole = pl.BlockSpec(memory_space=pltpu.VMEM)
+    return pl.pallas_call(
+        out_kernel,
+        in_specs=[SMEM] + [whole] * 5,
+        out_specs=(whole,) * 3,
+        out_shape=(
+            jax.ShapeDtypeStruct((320, 1024), F32),
+            jax.ShapeDtypeStruct((320, 1024), BF),
+            jax.ShapeDtypeStruct((1024, 1024), BF),
+        ),
+        compiler_params=params(),
+        cost_estimate=COST_S,
+    )(idx, mixed, rows_own, gain[None], own, other)
+
+
+WIDE = 1920
+
+
+def window_kernel(idx, t_ref, b_ref, o_ref):
+    onehot = jnp.where(lax.broadcasted_iota(jnp.int32, (BUCKETS, WIDE), 0) == t_ref[...], 1.0, 0.0)
+    rev = lax.dot_general(b_ref[...], onehot, (((0,), (0,)), ((), ())), precision=precise, preferred_element_type=F32)
+    rev = jnp.where(lax.broadcasted_iota(jnp.int32, (16, WIDE), 1) < 768, rev, NEG)
+    tail = pltpu.roll(rev, WIDE - 704 + 64 * (idx[0] * 2 + idx[1]), 1)
+    for s in range(8):
+        o_ref[:, 0, s, :] = (pltpu.roll(rev, WIDE - 7 + s, 1) if s < 7 else rev)[:, :1024]
+        o_ref[:, 1, s, :] = (pltpu.roll(tail, WIDE - 7 + s, 1) if s < 7 else tail)[:, :1024]
+
+
+def bias_windows(idx, table_rev, bias_f):
+    whole = pl.BlockSpec(memory_space=pltpu.VMEM)
+    return pl.pallas_call(
+        window_kernel,
+        in_specs=[SMEM, whole, whole],
+        out_specs=whole,
+        out_shape=jax.ShapeDtypeStruct((16, 2, 8, 1024), F32),
+        compiler_params=params(),
+    )(idx, table_rev, bias_f)
+
+
+def pack_kernel(idx, t_ref, db_ref, gn_ref, src_ref, gf_ref, r_ref, small_ref, keep_ref, send_ref):
+    z, y = idx[0], idx[1]
+
+    def gather(n):
+        total = jnp.zeros((16, WIDE), F32)
+        for s in range(8):
+            part = jnp.concatenate([db_ref[:, n, s, :], jnp.zeros((16, WIDE - 1024), F32)], axis=1)
+            total = total + (pltpu.roll(part, 7 - s, 1) if s < 7 else part)
+        return total
+
+    rev = gather(0) + pltpu.roll(gather(1), 704 - 64 * (z * 2 + y), 1)
+    onehot = jnp.where(lax.broadcasted_iota(jnp.int32, (BUCKETS, 768), 0) == t_ref[:, :768], 1.0, 0.0)
+    bias = lax.dot_general(
+        rev[:, :768], onehot, (((1,), (1,)), ((), ())), precision=precise, preferred_element_type=F32
+    )
+    src = src_ref[...].astype(F32)
+    unit = src * lax.rsqrt(jnp.mean(src * src, axis=-1, keepdims=True) + epsilon)
+    small_ref[...] = jnp.zeros_like(small_ref)
+    small_ref[0:1, :] = jnp.sum(gn_ref[...] * unit, axis=0, keepdims=True)
+    small_ref[1:2, :] = gf_ref[0:1, :]
+    small_ref[2:5, :] = r_ref[0:3, :]
+    small_ref[8:24, 0:BUCKETS] = bias
+    for sz in range(4):
+        at = lambda yy: pl.ds(pl.multiple_of(((z ^ sz) * 2 + yy) * 64, 64), 64)
+        keep_ref[sz] = gn_ref[at(y), :].astype(BF)
+        send_ref[sz] = gn_ref[at(y ^ 1), :].astype(BF)
+
+
+def pack(idx, table_rev, dbias, gn, src, gain_ffn_part, router_part):
+    whole = pl.BlockSpec(memory_space=pltpu.VMEM)
+    return pl.pallas_call(
+        pack_kernel,
+        in_specs=[SMEM] + [whole] * 6,
+        out_specs=(whole,) * 3,
+        out_shape=(
+            jax.ShapeDtypeStruct((24, 1024), F32),
+            jax.ShapeDtypeStruct((4, 64, 1024), BF),
+            jax.ShapeDtypeStruct((4, 64, 1024), BF),
+        ),
+        compiler_params=params(),
+        cost_estimate=COST_S,
+    )(idx, table_rev, dbias, gn, src, gain_ffn_part, router_part)
+
+
+def final_kernel(p_ref, near_ref, opp_ref, gn_ref, src_ref, gain_ref, gh_ref, o_ref):
+    f = lambda t: t.astype(F32)
+    own = f(p_ref[0]) + f(near_ref[...]) + f(opp_ref[...])
+    grad = jnp.concatenate([own, gn_ref[512:, :]], axis=0) * gain_ref[...]
+    src = f(src_ref[...])
+    scale = lax.rsqrt(jnp.mean(src * src, axis=-1, keepdims=True) + epsilon)
+    unit = src * scale
+    back = scale * (grad - unit * jnp.mean(grad * unit, axis=-1, keepdims=True))
+    o_ref[...] = (gh_ref[...] + back).astype(BF)
+
+
+def finish(parts, near, opp, gn, src, gain, grad_hidden):
+    whole = pl.BlockSpec(memory_space=pltpu.VMEM)
+    return pl.pallas_call(
+        final_kernel,
+        in_specs=[whole] * 7,
+        out_specs=whole,
+        out_shape=jax.ShapeDtypeStruct((320, 1024), BF),
+        compiler_params=params(),
+        cost_estimate=COST_S,
+    )(parts, near, opp, gn, src, gain[None], grad_hidden)
+
+
+def add_low(a, b):
+    return (a.astype(F32) + b.astype(F32)).astype(BF)
+
+
+PIECES = [(0, 320), (320, 320), (640, 320), (960, 160), (1120, 160)]
+
+
+def fetch_pieces(want, x_parts, g_parts, x_scr, g_scr, sem):
+    copies = []
+    for rc in range(2):
+        for n, (row, size) in enumerate(PIECES):
+            at = rc * 1280 + row
+            tile = at // 640
+            if want not in (None, tile):
+                continue
+            k = rc * 5 + n
+            copies.append(pltpu.make_async_copy(x_parts[k], x_scr.at[pl.ds(at, size)], sem.at[k, 0]))
+            for h in range(size // 160):
+                src = g_parts[k].at[pl.ds(176 * h, 160)]
+                dst = g_scr.at[pl.ds(at + 160 * h, 160)]
+                copies.append(pltpu.make_async_copy(src, dst, sem.at[k, 1 + h]))
+    return copies
+
+
+def expert_kernel(expert, first, last, *refs):
+    refs = list(refs)
+    step = pl.program_id(0)
+    src, m_ref = refs[:2]
+    if first:
+        x_parts, g_parts = refs[2:12], refs[12:22]
+        at = 22
+    else:
+        x_ref, g_ref, out_prev, dx_prev = refs[2:6]
+        at = 6
+    if last:
+        s0_ref, s1_ref = refs[at : at + 2]
+        at += 2
+    if first:
+        out_ref, dx_ref, dh_ref, win_ref, s_ref, xo_ref, go_ref, w_scr, sem, x_scr, g_scr, psem = refs[at:]
+    elif last:
+        out_ref, out_c_ref, dx_ref, dx_c_ref, dh_ref, win_ref, w_scr, sem = refs[at:]
+    else:
+        out_ref, dx_ref, dh_ref, win_ref, s_ref, w_scr, sem = refs[at:]
+
+    @pl.when(step == 0)
+    def _():
+        copies = [
+            pltpu.make_async_copy(src.at[n], w_scr.at[:, pl.ds(96 * n, 96), :], sem.at[n]) for n in range(4)
+        ]
+        for copy in copies:
+            copy.start()
+        if first:
+            for copy in fetch_pieces(None, x_parts, g_parts, x_scr, g_scr, psem):
+                copy.start()
+        for copy in copies:
+            copy.wait()
+
+    if first:
+        for t in range(4):
+
+            @pl.when(step == t)
+            def _(t=t):
+                for copy in fetch_pieces(t, x_parts, g_parts, x_scr, g_scr, psem):
+                    copy.wait()
+
+        rows = pl.ds(pl.multiple_of(step * 640, 640), 640)
+        x, g = x_scr[rows, :], g_scr[rows, :]
+        xo_ref[...] = x
+        go_ref[...] = g
+    else:
+        x, g = x_ref[...], g_ref[...]
+    w_gu = w_scr[0:2].reshape(768, 1024)
+    w_d = w_scr[2]
+    gu = dot_nt(x, w_gu)
+    gi = dot_nt(g, w_d)
+    gate, up = gu[:, :384], gu[:, 384:]
+    l = [gate[:, 88 + n : 89 + n] for n in range(3)]
+    top = jnp.maximum(jnp.maximum(l[0], l[1]), l[2])
+    ex = [jnp.exp(v - top) for v in l]
+    inv = 1.0 / (ex[0] + ex[1] + ex[2])
+    p = [v * inv for v in ex]
+    m = m_ref[...]
+    keep = m[:, expert : expert + 1]
+    w = p[expert] * keep
+    sq = gate * gate
+    th = jnp.tanh(0.7978845608028654 * gate * (1.0 + 0.044715 * sq))
+    half1 = 0.5 + 0.5 * th
+    act = gate * half1
+    dact = half1 + (0.5 * gate) * (1.0 - th * th) * (0.7978845608028654 + 0.10703222440890037 * sq)
+    inner = (act * up).astype(BF).astype(F32)
+    s = jnp.sum(inner * gi, axis=-1, keepdims=True) * keep
+    gin = gi * w
+    dg = gin * up * dact
+    du = gin * act
+    if last:
+        ss = [s0_ref[...][:, 0:1], s1_ref[...][:, 0:1], s]
+        dot = p[0] * ss[0] + p[1] * ss[1] + p[2] * ss[2]
+        lane = lax.broadcasted_iota(jnp.int32, (1, 384), 1)
+        for n in range(3):
+            dg = jnp.where(lane == 88 + n, p[n] * (ss[n] - dot), dg)
+    win = (inner * w).astype(BF)
+    dh = jnp.concatenate([dg.astype(BF), du.astype(BF)], axis=1)
+    dh_ref[...] = dh
+    win_ref[...] = win
+    if not last:
+        s_ref[...] = jnp.broadcast_to(s, s_ref.shape)
+    out = dot_nn(win, w_d)
+    dx = dot_nn(dh, w_gu)
+    if not first:
+        out = out + out_prev[...].astype(F32)
+        dx = dx + dx_prev[...].astype(F32)
+    if last:
+
+        @pl.when(step < 2)
+        def _():
+            out_c_ref[...] = out.astype(BF)
+            dx_c_ref[...] = dx.astype(BF)
+
+        @pl.when(step >= 2)
+        def _():
+            out_ref[...] = out.astype(BF)
+            dx_ref[...] = dx.astype(BF)
+    else:
+        out_ref[...] = out.astype(BF)
+        dx_ref[...] = dx.astype(BF)
+
+
+def expert_call(expert, x, g, m, src, prev, s_prev, tile=640):
+    total = 2560
+    first, last = expert == 0, expert == 2
+    at = (lambda i: i ^ 2) if last else (lambda i: i)
+    row = lambda n: pl.BlockSpec((tile, n), lambda i: (at(i), 0))
+    shape = lambda n, t: jax.ShapeDtypeStruct((total, n), t)
+    outs = [(1024, BF), (1024, BF), (768, BF), (384, BF), (8, F32)]
+    scratch = [pltpu.VMEM((3, 384, 1024), BF), pltpu.SemaphoreType.DMA((4,))]
+    if first:
+        ins = [src, m, *x, *g]
+        specs = [ANY, row(8)] + [ANY] * 20
+        outs += [(1024, BF), (1024, BF)]
+        scratch += [pltpu.VMEM((total, 1024), BF), pltpu.VMEM((total, 1024), BF), pltpu.SemaphoreType.DMA((10, 3))]
+    else:
+        ins = [src, m, x, g, *prev]
+        specs = [ANY, row(8)] + [row(1024)] * 4
+    if last:
+        ins += list(s_prev)
+        specs += [row(8), row(8)]
+        half = jax.ShapeDtypeStruct((total // 2, 1024), BF)
+        mine = pl.BlockSpec((tile, 1024), lambda i: (jnp.maximum(i - 2, 0), 0))
+        other = pl.BlockSpec((tile, 1024), lambda i: (jnp.minimum(i, 1), 0))
+        out_shape = (half, half, half, half, shape(768, BF), shape(384, BF))
+        out_specs = (mine, other, mine, other, row(768), row(384))
+    else:
+        out_shape = tuple(shape(n, t) for n, t in outs)
+        out_specs = tuple(row(n) for n, t in outs)
+    return pl.pallas_call(
+        functools.partial(expert_kernel, expert, first, last),
+        grid=(total // tile,),
+        out_shape=out_shape,
+        in_specs=specs,
+        out_specs=out_specs,
+        scratch_shapes=scratch,
+        compiler_params=params(),
+        cost_estimate=COST_E,
+    )(*ins)
+
+
+def line_collect(part_of, z):
+    at = lambda n: part_of(z ^ n)
+    near = pair_z(at(1))
+    opp = flip_z(add_low(at(3), pair_z(at(2))))
+    return (at(0).astype(F32) + near.astype(F32) + opp.astype(F32)).astype(BF)
+
+
+def trade_wt(v):
+    return lax.all_to_all(v, "wt", 0, 0, tiled=True)
+
+
+def sum_all(v):
+    v = v + move_c(v)
+    v = v + move_x(v)
+    v = v + move_y(v)
+    v = v + lax.ppermute(v, "ctx", [(i, i ^ 2) for i in range(8)])
+    return v + lax.ppermute(v, "ctx", [(i, i ^ 4) for i in range(8)])
+
+
+def norm_parts(values):
+    return values * lax.rsqrt(jnp.mean(values * values, axis=-1, keepdims=True) + epsilon)
+
+
+def local_fast(
+    tokens, cotangent, w_query, w_key, w_value, w_out, gain_attn, gain_ffn, w_router, rel_bias,
+    exp_gate, exp_up, exp_down, bucket_table, expert_ids, priority,
+):
+    ctx_index = lax.axis_index("ctx").astype(jnp.int32)
+    wt_index = lax.axis_index("wt").astype(jnp.int32)
+    z, y, x, c = ctx_index // 2, ctx_index % 2, wt_index // 2, wt_index % 2
+    idx = jnp.stack([z, y, x, c])
+    rows_own = tokens[0, 0]
+
+    packed = jnp.concatenate(
+        [gain_attn[None], gain_ffn[None], w_router.T, jnp.pad(rel_bias.reshape(1, 128), ((0, 0), (0, 128))),
+         jnp.zeros((2, 256), BF)], axis=0
+    )
+    small = lax.all_gather(packed, "wt", axis=0, tiled=False)
+    gain_attn_f = small[:, 0].reshape(1024).astype(F32)
+    gain_ffn_f = small[:, 1].reshape(1024).astype(F32)
+    bias_f = small[:, 5, :128].reshape(4, 32, 4).transpose(1, 0, 2).reshape(32, 16).astype(F32)
+
+    ids, rank = expert_ids[0, 0], priority[0, 0]
+    expert = ids.T.reshape(-1)
+    rank_key = (jnp.arange(TOP, dtype=jnp.int32)[:, None] * 320 + rank[None, :]).reshape(-1)
+    earlier = (expert[:, None] == expert[None, :]) & (rank_key[None, :] < rank_key[:, None])
+    keep = (jnp.sum(earlier.astype(jnp.int32), axis=1) < CAP).reshape(TOP, 320)
+    hold = jnp.sum(
+        jnp.where((ids.T[:, :, None] == jnp.arange(EXPERTS, dtype=jnp.int32)) & keep[:, :, None], 1.0, 0.0), axis=0
+    )
+    marks = jnp.pad(hold.reshape(2, 1, 480), ((0, 0), (0, 15), (0, 544))).astype(BF)
+    cot = cotangent[0, 0]
+    cot_marked = jnp.concatenate([cot[:160], marks[0], cot[160:], marks[1]], axis=0)
+
+    def pieces(v):
+        return jnp.pad(v.reshape(3, 4, 88, 256), ((0, 0), (0, 0), (0, 8), (0, 0)))
+
+    gate_t, up_t = exp_gate.transpose(0, 2, 1), exp_up.transpose(0, 2, 1)
+    gate_p = pieces(gate_t)
+    router_rows = jnp.broadcast_to(
+        jnp.pad(w_router.T, ((0, 5), (0, 0)))[None, None], (3, 4, 8, 256)
+    )
+    gate_p = jnp.concatenate([gate_p[:, :, :88], router_rows], axis=2)
+    share = jnp.stack([gate_p, pieces(up_t), pieces(exp_down)], axis=1).transpose(2, 0, 1, 3, 4)
+    table_rev = jnp.pad(bucket_table[::-1], (0, WIDE - 768), constant_values=-1)[None]
+    windows = bias_windows(idx, table_rev, bias_f)
+
+    qkv_of = lambda u: u[:768].reshape(3, 256, 128)
+    prompt_own = rows_own[:64]
+    unit = jnp.stack([w_query, w_key, w_value, w_out]).reshape(1024, 128)
+    part_0 = qkv_of(unit)
+    share, small_first = phase(share, small)
+    near, opp, p_near, p_opp, y0 = phase(
+        pair_z(unit), flip_z(unit), pair_z(prompt_own), flip_z(prompt_own), move_y(part_0)
+    )
+    part_1, part_3 = qkv_of(near), qkv_of(opp)
+    s0 = jnp.stack([part_0, y0])
+    cross, p_cross, x0, x1, y3, share = phase(
+        pair_z(opp), pair_z(p_opp), move_x(s0), move_x(part_1), move_y(part_3), trade_wt(share)
+    )
+    share = share.transpose(1, 2, 3, 0, 4).reshape(3, 3, 96, 1024)
+    spread = [lax.all_gather(share[e], "ctx", axis=0, tiled=False, axis_index_groups=LINES_Z) for e in range(3)]
+    part_2 = qkv_of(cross)
+    t0, s1, s3 = jnp.stack([s0, x0]), jnp.stack([part_1, x1]), jnp.stack([part_3, y3])
+    prompt_z = jnp.stack([prompt_own, p_near, p_cross, p_opp])
+    prompt_y, c0, y1, x3, x2, windows, cot_marked = phase(
+        move_y(prompt_z), move_c(t0), move_y(s1), move_x(s3), move_x(part_2), windows, cot_marked
+    )
+    prompts = jnp.stack([prompt_z, prompt_y], axis=1).reshape(8, 64, 1024)
+    prompts = jnp.take(prompts, jnp.arange(8, dtype=jnp.int32) ^ ctx_index, axis=0).reshape(512, 1024)
+    source_all = jnp.concatenate([prompts, rows_own[64:]], axis=0)
+    all_low = (norm_parts(source_all.astype(F32)) * gain_attn_f).astype(BF)
+    t1, t3, s2 = jnp.stack([s1, y1]), jnp.stack([s3, x3]), jnp.stack([part_2, x2])
+    wo_z = jnp.stack([u[768:].reshape(256, 128) for u in (unit, near, opp, cross)])
+
+    state = attend(0, False, idx, all_low, windows, (t0, c0), None)
+    *state, c1, c3, y2, wo_y = phase(*state, move_c(t1), move_c(t3), move_y(s2), move_y(wo_z))
+    t2, wo_s = jnp.stack([s2, y2]), jnp.stack([wo_z, wo_y])
+    cot_marked, mixed_0 = phase(cot_marked, state[1])
+    state[1] = mixed_0
+    g_x, g_y = move_x(cot_marked), move_y(cot_marked)
+    state = attend(1, True, idx, all_low, windows, (t1, c1), state)
+    *state, c2, wo_x = phase(*state, move_c(t2), move_x(wo_s))
+    wo_t = jnp.stack([wo_s, wo_x])
+    state = attend(3, False, idx, all_low, windows, (t3, c3), state)
+    *state, wo_c, g_x, g_y = phase(*state, move_c(wo_t), g_x, g_y)
+    state = attend(2, True, idx, all_low, windows, (t2, c2), state)
+    *state, g_a, g_b, g_cx, g_cy, g_c = phase(
+        *state, move_x(g_y[:176]), move_y(g_x[176:]), move_c(g_x), move_c(g_y), move_c(cot_marked)
+    )
+    probs, mixed, qkv, w_qkv = state
+    hidden, normed, w_o = project_out(idx, mixed, rows_own, gain_ffn_f, wo_t, wo_c)
+
+    x_x, x_y, x_c, g_ca, g_cb = phase(move_x(normed), move_y(normed), move_c(normed), move_c(g_a), move_c(g_b))
+    x_a, x_b, x_cx, x_cy = phase(move_x(x_y[:160]), move_y(x_x[160:]), move_c(x_x), move_c(x_y))
+    x_parts = [normed, x_x, x_y, x_a, x_b, x_c, x_cx, x_cy, move_c(x_a), move_c(x_b)]
+    cot_parts = [cot_marked, g_x, g_y, g_a, g_b, g_c, g_cx, g_cy, g_ca, g_cb]
+    marks_of = lambda v: [v[n + 160] for n in range(0, v.shape[0], 176)]
+    marks_all = jnp.stack(sum([marks_of(v) for v in cot_parts], []))[:, :480].reshape(2560, 3).astype(F32)
+    marks_all = jnp.pad(marks_all, ((0, 0), (0, 5)))
+
+    def weight_grads(dh_e, win_e):
+        gw = dot_tn(dh_e, x_all).astype(BF).reshape(2, 4, 96, 1024)
+        dw = dot_tn(win_e, g_all).astype(BF).reshape(1, 4, 96, 1024)
+        return jnp.concatenate([gw, dw], axis=0).transpose(1, 0, 2, 3)
+
+    def along_z(both):
+        return lax.psum_scatter(both, "ctx", scatter_dimension=0, axis_index_groups=LINES_Z)
+
+    res = expert_call(0, x_parts, cot_parts, marks_all, spread[0], None, [])
+    x_all, g_all = res[5:]
+    both_0, s_0 = weight_grads(res[2], res[3]), res[4]
+    res = expert_call(1, x_all, g_all, marks_all, spread[1], res[:2], [])
+    both_1, s_1 = weight_grads(res[2], res[3]), res[4]
+    out, out_c, dx, dx_c, dh_2, win_2 = expert_call(
+        2, x_all, g_all, marks_all, spread[2], res[:2], [s_0, s_1]
+    )
+    bulk = [along_z(both_0), along_z(both_1)]
+
+    got, dh_2, win_2 = phase(move_c(dx_c), dh_2, win_2)
+    last, rest = add_low(dx[960:], got[960:]), add_low(dx[:960], got[:960])
+    g_w2 = dot_tn(dh_2, x_all).astype(BF)
+    d_a, d_b, rest, g_w2, win_2 = phase(move_x(last[:160]), move_y(last[160:]), rest, g_w2, win_2)
+
+    def mix_in(rest, a, b):
+        v_x = jnp.concatenate([rest[320:480], add_low(rest[480:640], b)], axis=0)
+        v_y = jnp.concatenate([add_low(rest[640:800], a), rest[800:]], axis=0)
+        return v_x, v_y
+
+    v_x, v_y = mix_in(rest, d_a, d_b)
+    g_d2 = dot_tn(win_2, g_all).astype(BF)
+    v_x, v_y, o_got, g_d2 = phase(move_x(v_x), move_y(v_y), move_c(out_c), g_d2)
+    both_2 = jnp.concatenate([g_w2.reshape(2, 4, 96, 1024), g_d2.reshape(1, 4, 96, 1024)], axis=0).transpose(1, 0, 2, 3)
+    router_part = both_2[0, 0, 88:96].astype(F32)
+    grad_hidden, grad_low, grad_mixed, gain_ffn_part = out_back(
+        (rest[:320], v_x, v_y), hidden, gain_ffn_f, cot, w_o
+    )
+    bulk.append(along_z(both_2))
+    o_last, o_rest = add_low(out[960:], o_got[960:]), add_low(out[:960], o_got[:960])
+    back_of = lambda base, count, *prev: attend_back(
+        base, count, idx, all_low, probs, qkv, w_qkv, grad_mixed, mixed, grad_low, *prev
+    )
+    keep_f, send_f, gn, dbias = back_of(4, 4, None, None)
+    o_a, o_b, gn = phase(move_x(o_last[:160]), move_y(o_last[160:]), gn)
+    o_x, o_y = mix_in(o_rest, o_a, o_b)
+    keep_n, send_n, gn, dbias = back_of(2, 2, gn, dbias)
+    o_x, o_y, got, gn = phase(move_x(o_x), move_y(o_y), move_c(send_f), gn)
+    combined = o_rest[:320].astype(F32) + o_x.astype(F32) + o_y.astype(F32)
+    output = (hidden + combined).astype(BF).reshape(1, 1, 320, 1024)
+
+    fa, fb = cut_rows(add_low(keep_f, got).reshape(2, 2, 2, 256, 512))
+    keep_h, send_h, gn_all, dbias = back_of(0, 2, gn, dbias)
+    fx, fy, got_n, gn_all = phase(move_x(fa[1]), move_y(fb[:, :, 1]), move_c(send_n), gn_all)
+    fa, fb = add_low(fa[0], fx), add_low(fb[:, :, 0], fy)
+    packed = pack(idx, table_rev, dbias, gn_all, source_all, gain_ffn_part, router_part)
+    got, fy, fx, smalls, gp_keep, gp_send = phase(move_c(send_h), move_y(fa[:, 1]), move_x(fb[1]), *packed)
+    far = jnp.concatenate([add_low(fa[:, 0], fy), add_low(fb[0], fx)], axis=1)
+    block = lambda t: t.reshape(2, 1, 2, 256, 512)
+    h = jnp.concatenate([add_low(block(keep_h), block(got)), add_low(block(keep_n), block(got_n))], axis=1)
+    ha, hb = cut_rows(h)
+    hx, hy, f_cross, gp_got, sm = phase(
+        move_x(ha[1]), move_y(hb[:, :, 1]), pair_z(far[0]), move_y(gp_send), move_c(smalls)
+    )
+    ha, hb = add_low(ha[0], hx), add_low(hb[:, :, 0], hy)
+    gp = add_low(gp_keep, gp_got)
+    smalls = smalls + sm
+    hy, hx, f_opp, gp_cross, sm = phase(
+        move_y(ha[:, 1]), move_x(hb[1]), flip_z(add_low(far[1], f_cross)), pair_z(gp[2]), move_x(smalls)
+    )
+    here = jnp.concatenate([add_low(ha[:, 0], hy), add_low(hb[0], hx)], axis=1)
+    smalls = smalls + sm
+    h_near, gp_opp, gp_near, sm = phase(
+        pair_z(here[1]), flip_z(add_low(gp[3], gp_cross)), pair_z(gp[1]), move_y(smalls)
+    )
+    smalls = smalls + sm
+    tot = here[0].astype(F32) + h_near.astype(F32) + f_opp.astype(F32)
+    grad_tokens = finish(gp, gp_near, gp_opp, gn_all, rows_own, gain_attn_f, grad_hidden).reshape(1, 1, 320, 1024)
+    smalls = smalls + pair_z(smalls)
+    smalls = smalls + lax.ppermute(smalls, "ctx", [(i, i ^ 4) for i in range(8)])
+    mine = lax.dynamic_slice_in_dim(smalls, wt_index * 256, 256, 1)
+    res_gain_attn, res_gain_ffn, res_router = mine[0], mine[1], mine[2:5].T
+    res_bias = lax.dynamic_slice_in_dim(smalls[8:24, :BUCKETS], wt_index * 4, 4, 0).T
+
+    back = jnp.stack(bulk).reshape(3, 3, 96, 4, 256).transpose(3, 0, 1, 2, 4)
+    back = trade_wt(back)[:, :, :, :88].transpose(1, 2, 0, 3, 4).reshape(3, 3, 352, 256).astype(F32)
+    res_gate, res_up, res_down = back[:, 0].transpose(0, 2, 1), back[:, 1].transpose(0, 2, 1), back[:, 2]
+
+    return (
+        output, grad_tokens, tot[:, :128], tot[:, 128:256], tot[:, 256:384], tot[:, 384:], res_gain_attn, res_gain_ffn, res_router, res_bias,
+        res_gate, res_up, res_down,
+    )
+
+
 def solution(mesh):
+    fast = mesh.shape["ctx"] == FAST_CTX and mesh.shape["wt"] == FAST_WT
     return jax.shard_map(
-        local,
+        local_fast if fast else local,
         mesh=mesh,
         in_specs=(
             P("wt", "ctx", None, None),

time: 2370 us -> 534 us (0.23)
  waiting for transfers between devices: 1510 us -> 120 us
  local copies, waits for them, and re-layouts: 334 us -> 44.3 us
  matrix products: 239 us -> 31.8 us
  Pallas kernels: 0 us -> 191 us
  blocking collectives: 181 us -> 6.18 us
  starting transfers between devices: 1.2 us -> 69.1 us
  other arithmetic: 76.4 us -> 49.7 us
    reduce_scatter x12 -> x3, waiting for transfers between devices: 721 us -> 0.06 us  [along_z(): lax.psum_scatter(both, 'ctx', scatter_dimension=0, axis_index_groups=LINE...]
    all_gather x12 -> x3, waiting for transfers between devices: 412 us -> 0.04 us  [local_fast(): lax.all_gather(share[e], 'ctx', axis=0, tiled=False, axis_index_groups=LI...]
    unnamed x34 -> x6, waiting for transfers between devices: 382 us -> 0.1 us
    dot_general x42 -> x6, matrix products: 239 us -> 31.8 us  [dot_tn(): lax.dot_general(a, b, (((0,), (0,)), ((), ())), preferred_element_type=F32)]
    pallas_call x0 -> x15, Pallas kernels: none -> 191 us  [the longest x3 77.6 us: expert_call(): pl.pallas_call(functools.partial(expert_kernel, expert, first, last), gri...]
    all_gather x8 -> x1, blocking collectives: 140 us -> 6.18 us  [local_fast(): small = lax.all_gather(packed, 'wt', axis=0, tiled=False)]
    ppermute x0 -> x73, waiting for transfers between devices: none -> 120 us  [the longest x18 49.1 us: move_x(): return lax.ppermute(v, 'wt', SWAP_X)]
    unnamed x225 -> x153, local copies, waits for them, and re-layouts: 112 us -> 9.43 us
  transfers between devices with their start and end apart: 29 -> 81, of which waited for: 22 -> 31; matrix products, arithmetic and copies ran while one was open for 21% -> 21% of each run, Pallas kernels for 0% -> 36%
where the time goes in v3:
time: 534 us; the launch traced here: 528 us
  Pallas kernels  191 us (36%)
  waiting for transfers between devices  120 us (22%)
  starting transfers between devices  69.1 us (13%)
  other arithmetic  49.7 us (9%)
  local copies, waits for them, and re-layouts  44.3 us (8%)
  matrix products  31.8 us (6%)
  between operations  15.9 us (3%)
  blocking collectives  6.18 us (1%)
    pallas_call x3, Pallas kernels, expert_call(): pl.pallas_call(functools.partial(expert_kernel, expert, first, last), gri...  77.6 us
    pallas_call x3, Pallas kernels, attend_back(): pl.pallas_call(functools.partial(attend_back_kernel, gn_prev is None), gr...  54.7 us
    ppermute x18, waiting for transfers between devices, move_x(): return lax.ppermute(v, 'wt', SWAP_X)  49.1 us
    ppermute x9, waiting for transfers between devices, pair_z(): return lax.ppermute(v, 'ctx', PAIR_Z)  38.9 us
    pallas_call x4, Pallas kernels, attend(): pl.pallas_call(functools.partial(attend_kernel, sz, prev is None, x_first...  36.3 us
    dot_general x6, matrix products, dot_tn(): lax.dot_general(a, b, (((0,), (0,)), ((), ())), preferred_element_type=F32)  31.8 us
    ppermute x20, starting transfers between devices, move_y(): return lax.ppermute(v, 'ctx', SWAP_Y)  23.5 us
    ppermute x20, waiting for transfers between devices, move_y(): return lax.ppermute(v, 'ctx', SWAP_Y)  22 us
  transfers between devices with their start and end apart: 81, of which 31 were waited for; matrix products, arithmetic and copies ran while one was open for 21% of the time, Pallas kernels for 36%

profile of v3, /device:TPU:0, one launch (start us, length us, event | category | flops | bytes accessed | tf_op | source)
XLA Modules:
  0.0 528.2 jit_solution(15301090004900309871)
XLA Ops:
  10.8 6.2 %all-gather = bf16[32,256]{1,0:T(8,128)(2,1)S(1)} all-gather(bf16[8,256]{1,0:T(8,128)(2,1)S(1)} %concatenate.44), channel_id=2, replica_groups=mesh['ctx'=8,'wt'=4] {'wt'}, dimensions={0}, use_global_device_ids=true | all-gather | bytes 20480 | tf_op jit(solution)/shard_map/all_gather | solution.py:1102
  33.3 9.0 %collective-permute-done.2 = bf16[64,1024]{1,0:T(8,128)(2,1)S(1)} collective-permute-done((bf16[64,1024]{1,0:T(8,128)(2,1)S(1)}, bf16[64,1024]{1,0:T(8,128)(2,1)S(1)}, u32[]{:S(2)}, u32[]{:S(2)}) %collective-permute-start.2) | collective-permute-done | bytes 131104 | tf_op jit(solution)/shard_map/ppermute | solution.py:518
  54.7 5.3 %collective-permute-done.6 = bf16[64,1024]{1,0:T(8,128)(2,1)S(1)} collective-permute-done((bf16[64,1024]{1,0:T(8,128)(2,1)S(1)}, bf16[64,1024]{1,0:T(8,128)(2,1)S(1)}, u32[]{:S(2)}, u32[]{:S(2)}) %collective-permute-start.6) | collective-permute-done | bytes 131104 | tf_op jit(solution)/shard_map/ppermute | solution.py:518
  87.3 9.7 %collective-permute-done.14 = bf16[3,256,128]{2,1,0:T(8,128)(2,1)} collective-permute-done((bf16[3,256,128]{2,1,0:T(8,128)(2,1)S(1)}, bf16[3,256,128]{2,1,0:T(8,128)(2,1)}, u32[]{:S(2)}, u32[]{:S(2)}) %collective-permute-start.14) | collective-permute-done | bytes 196640 | tf_op jit(solution)/shard_map/ppermute | solution.py:510
  111.0 9.1 %shard_map.256 = (bf16[16,320,768]{2,1,0:T(8,128)(2,1)}, bf16[320,1024]{1,0:T(8,128)(2,1)}, bf16[8,768,384]{2,1,0:T(8,128)(2,1)}, bf16[8,1024,384]{2,1,0:T(8,128)(2,1)}) custom-call(s32[4]{0:T(128)} %pad_add_fusion.idx, bf16[768,1024]{1,0:T(8,128)(2,1)} %fusion.2.n_ref, f32[16,2,8,1024]{3,2,1,0:T(8,128)} %shard_map.255.w_ref, ...), custom_call_target="tpu_custom_call" | custom-call | flops 1000000 | bytes 1000000 | tf_op jit(solution)/shard_map/pallas_call | solution.py:610
  123.4 9.2 %shard_map.257 = (bf16[16,320,768]{2,1,0:T(8,128)(2,1)}, bf16[320,1024]{1,0:T(8,128)(2,1)}, bf16[8,768,384]{2,1,0:T(8,128)(2,1)}, bf16[8,1024,384]{2,1,0:T(8,128)(2,1)}) custom-call(s32[4]{0:T(128)} %pad_add_fusion.idx, bf16[768,1024]{1,0:T(8,128)(2,1)} %fusion.2.n_ref, ...), custom_call_target="tpu_custom_call", output_to_operand_aliasing={{0}: (5, {}), {1}: (6, {}), {2}: (7, {}), {3}: (8, {})} | custom-call | flops 1000000 | bytes 1000000 | tf_op jit(solution)/shard_map/pallas_call | solution.py:610
  138.8 9.0 %shard_map.258 = (bf16[16,320,768]{2,1,0:T(8,128)(2,1)}, bf16[320,1024]{1,0:T(8,128)(2,1)}, bf16[8,768,384]{2,1,0:T(8,128)(2,1)}, bf16[8,1024,384]{2,1,0:T(8,128)(2,1)}) custom-call(s32[4]{0:T(128)} %pad_add_fusion.idx, bf16[768,1024]{1,0:T(8,128)(2,1)} %fusion.2.n_ref, ...), custom_call_target="tpu_custom_call", output_to_operand_aliasing={{0}: (5, {}), {1}: (6, {}), {2}: (7, {}), {3}: (8, {})} | custom-call | flops 1000000 | bytes 1000000 | tf_op jit(solution)/shard_map/pallas_call | solution.py:610
  147.8 8.8 %collective-permute-done.22.refs_13_ = bf16[352,1024]{1,0:T(8,128)(2,1)S(1)} collective-permute-done((bf16[352,1024]{1,0:T(8,128)(2,1)}, bf16[352,1024]{1,0:T(8,128)(2,1)S(1)}, u32[]{:S(2)}, u32[]{:S(2)}) %collective-permute-start.22) | collective-permute-done | bytes 720928 | tf_op jit(solution)/shard_map/ppermute | solution.py:510
  163.7 9.0 %shard_map.259 = (bf16[16,320,768]{2,1,0:T(8,128)(2,1)}, bf16[320,1024]{1,0:T(8,128)(2,1)}, bf16[8,768,384]{2,1,0:T(8,128)(2,1)}, bf16[8,1024,384]{2,1,0:T(8,128)(2,1)}) custom-call(s32[4]{0:T(128)} %pad_add_fusion.idx, bf16[768,1024]{1,0:T(8,128)(2,1)} %fusion.2.n_ref, ...), custom_call_target="tpu_custom_call", output_to_operand_aliasing={{0}: (5, {}), {1}: (6, {}), {2}: (7, {}), {3}: (8, {})} | custom-call | flops 1000000 | bytes 1000000 | tf_op jit(solution)/shard_map/pallas_call | solution.py:610
  172.7 5.9 %shard_map.260 = (f32[320,1024]{1,0:T(8,128)}, bf16[320,1024]{1,0:T(8,128)(2,1)}, bf16[1024,1024]{1,0:T(8,128)(2,1)}) custom-call(s32[4]{0:T(128)} %pad_add_fusion.idx, bf16[320,1024]{1,0:T(8,128)(2,1)} %get-tuple-element.228.m_ref, bf16[320,1024]{1,0:T(8,128)(2,1)} %bitcast.282, f32[1,1024]{1,0:T(1,128)} %bitcast.328, ...), custom_call_target="tpu_custom_call" | custom-call | flops 1000000 | bytes 1000000 | tf_op jit(solution)/shard_map/pallas_call | solution.py:794
  184.2 10.7 %collective-permute-done.29.refs_3_ = bf16[320,1024]{1,0:T(8,128)(2,1)} collective-permute-done((bf16[320,1024]{1,0:T(8,128)(2,1)}, bf16[320,1024]{1,0:T(8,128)(2,1)}, u32[]{:S(2)}, u32[]{:S(2)}) %collective-permute-start.29) | collective-permute-done | bytes 655392 | tf_op jit(solution)/shard_map/ppermute | solution.py:510
  212.8 24.5 %shard_map.261 = (bf16[2560,1024]{1,0:T(8,128)(2,1)}, bf16[2560,1024]{1,0:T(8,128)(2,1)}, bf16[2560,768]{1,0:T(8,128)(2,1)}, bf16[2560,384]{1,0:T(8,128)(2,1)}, ...) custom-call(bf16[4,3,96,1024]{3,2,1,0:T(8,128)(2,1)} %all-gather.7.cloned.1.call-done.refs_0_, ...), custom_call_target="tpu_custom_call" | custom-call | flops 1000000 | bytes 1000000 | tf_op jit(solution)/shard_map/pallas_call | solution.py:1053
  237.4 5.4 %convolution_convert_fusion.4 = bf16[384,1024]{1,0:T(8,128)(2,1)S(1)} fusion(bf16[2560,384]{1,0:T(8,128)(2,1)} %get-tuple-element.328, bf16[2560,1024]{1,0:T(8,128)(2,1)} %get-tuple-element.248.refs_3_), kind=kOutput, calls=%fused_computation.30 | convolution fusion | flops 2013659136 | bytes 7995392 | tf_op jit(solution)/shard_map/dot_general | solution.py:534
  249.3 23.4 %shard_map.262 = (bf16[2560,1024]{1,0:T(8,128)(2,1)}, bf16[2560,1024]{1,0:T(8,128)(2,1)}, bf16[2560,768]{1,0:T(8,128)(2,1)}, bf16[2560,384]{1,0:T(8,128)(2,1)}, f32[2560,8]{1,0:T(8,128)}) custom-call(bf16[4,3,96,1024]{3,2,1,0:T(8,128)(2,1)} %all-gather.9.cloned.1.call-done.refs_0_, f32[2560,8]{1,0:T(8,128)} %pad_convert_fusion.refs_1_, ...), custom_call_target="tpu_custom_call" | custom-call | flops 1000000 | bytes 1000000 | tf_op jit(solution)/shard_map/pallas_call | solution.py:1053
  272.7 29.7 %shard_map.263 = (bf16[1280,1024]{1,0:T(8,128)(2,1)}, bf16[1280,1024]{1,0:T(8,128)(2,1)}, bf16[1280,1024]{1,0:T(8,128)(2,1)}, bf16[1280,1024]{1,0:T(8,128)(2,1)}...) custom-call(bf16[4,3,96,1024]{3,2,1,0:T(8,128)(2,1)} %all-gather.5.cloned.1.call-done.refs_0_, ...), custom_call_target="tpu_custom_call" | custom-call | flops 1000000 | bytes 1000000 | tf_op jit(solution)/shard_map/pallas_call | solution.py:1053
  306.9 6.8 %convolution_convert_fusion = bf16[768,1024]{1,0:T(8,128)(2,1)S(1)} fusion(bf16[2560,768]{1,0:T(8,128)(2,1)S(1)} %copy-done.65, bf16[2560,1024]{1,0:T(8,128)(2,1)} %get-tuple-element.247.refs_2_), kind=kOutput, calls=%fused_computation.23 | convolution fusion | flops 4027318272 | bytes 10747904 | tf_op jit(solution)/shard_map/dot_general | solution.py:534
  319.9 9.1 %convolution_convert_fusion.2 = bf16[768,1024]{1,0:T(8,128)(2,1)} fusion(bf16[2560,768]{1,0:T(8,128)(2,1)} %get-tuple-element.261, bf16[2560,1024]{1,0:T(8,128)(2,1)} %get-tuple-element.247.refs_2_), kind=kOutput, calls=%fused_computation.25 | convolution fusion | flops 4027318272 | bytes 10747904 | tf_op jit(solution)/shard_map/dot_general | solution.py:534
  337.6 10.6 %collective-permute-done.44.c_ref = bf16[320,1024]{1,0:T(8,128)(2,1)S(1)} collective-permute-done((bf16[320,1024]{1,0:T(8,128)(2,1)S(1)}, bf16[320,1024]{1,0:T(8,128)(2,1)S(1)}, u32[]{:S(2)}, u32[]{:S(2)}) %collective-permute-start.44) | collective-permute-done | bytes 655392 | tf_op jit(solution)/shard_map/ppermute | solution.py:506
  349.7 5.4 %shard_map.264 = (f32[320,1024]{1,0:T(8,128)}, bf16[320,1024]{1,0:T(8,128)(2,1)}, bf16[320,1024]{1,0:T(8,128)(2,1)}, f32[8,1024]{1,0:T(8,128)}) custom-call(bf16[320,1024]{1,0:T(8,128)(2,1)} %slice.395.a_ref, bf16[320,1024]{1,0:T(8,128)(2,1)} %copy-done.31, bf16[320,1024]{1,0:T(8,128)(2,1)} %copy-done.30, f32[320,1024]{1,0:T(8,128)} %get-tuple-element.230.h_ref, ...), custom_call_target="tpu_custom_call" | custom-call | flops 1000000 | bytes 1000000 | tf_op jit(solution)/shard_map/pallas_call | solution.py:762
  355.2 23.7 %shard_map.265 = (bf16[2,4,256,512]{3,2,1,0:T(8,128)(2,1)}, bf16[2,4,256,512]{3,2,1,0:T(8,128)(2,1)}, f32[768,1024]{1,0:T(8,128)}, f32[16,2,8,1024]{3,2,1,0:T(8,128)}) custom-call(s32[4]{0:T(128)} %pad_add_fusion.idx, bf16[768,1024]{1,0:T(8,128)(2,1)} %fusion.2.n_ref, bf16[16,320,768]{2,1,0:T(8,128)(2,1)} %get-tuple-element.269.p_ref, ...), custom_call_target="tpu_custom_call" | custom-call | flops 1000000 | bytes 1000000 | tf_op jit(solution)/shard_map/pallas_call | solution.py:706
  395.1 15.5 %shard_map.266 = (bf16[2,2,256,512]{3,2,1,0:T(8,128)(2,1)}, bf16[2,2,256,512]{3,2,1,0:T(8,128)(2,1)}, f32[768,1024]{1,0:T(8,128)}, f32[16,2,8,1024]{3,2,1,0:T(8,128)}) custom-call(s32[4]{0:T(128)} %pad_add_fusion.idx, bf16[768,1024]{1,0:T(8,128)(2,1)} %fusion.2.n_ref, ...), custom_call_target="tpu_custom_call", output_to_operand_aliasing={{3}: (9, {})} | custom-call | flops 1000000 | bytes 1000000 | tf_op jit(solution)/shard_map/pallas_call | solution.py:706
  420.8 15.6 %shard_map.267 = (bf16[2,2,256,512]{3,2,1,0:T(8,128)(2,1)}, bf16[2,2,256,512]{3,2,1,0:T(8,128)(2,1)}, f32[768,1024]{1,0:T(8,128)}, f32[16,2,8,1024]{3,2,1,0:T(8,128)}) custom-call(s32[4]{0:T(128)} %pad_add_fusion.idx, bf16[768,1024]{1,0:T(8,128)(2,1)} %fusion.2.n_ref, ...), custom_call_target="tpu_custom_call", output_to_operand_aliasing={{3}: (9, {})} | custom-call | flops 1000000 | bytes 1000000 | tf_op jit(solution)/shard_map/pallas_call | solution.py:706
  452.8 13.9 %collective-permute-done.59 = bf16[256,512]{1,0:T(8,128)(2,1)S(1)} collective-permute-done((bf16[256,512]{1,0:T(8,128)(2,1)S(1)}, bf16[256,512]{1,0:T(8,128)(2,1)S(1)}, u32[]{:S(2)}, u32[]{:S(2)}) %collective-permute-start.59) | collective-permute-done | bytes 262176 | tf_op jit(solution)/shard_map/ppermute | solution.py:518
  500.0 5.9 %collective-permute-done.67 = bf16[256,512]{1,0:T(8,128)(2,1)S(1)} collective-permute-done((bf16[256,512]{1,0:T(8,128)(2,1)S(1)}, bf16[256,512]{1,0:T(8,128)(2,1)S(1)}, u32[]{:S(2)}, u32[]{:S(2)}) %collective-permute-start.67) | collective-permute-done | bytes 262176 | tf_op jit(solution)/shard_map/ppermute | solution.py:518
  (472 shorter events, 230.9 us)
Async XLA Ops:
  21.0 42.8 %all-to-all-start = ((bf16[4,3,3,96,256]{4,3,2,1,0:T(8,128)(2,1)}), bf16[4,3,3,96,256]{4,3,2,1,0:T(8,128)(2,1)S(1)}, u32[]{:S(2)}, u32[]{:S(2)}) async-start(bf16[4,3,3,96,256]{4,3,2,1,0:T(8,128)(2,1)} %copy.124), calls=%async_computation | async-start | bytes 3538944 | tf_op jit(solution)/shard_map/all_to_all | solution.py:1073
  24.7 187.2 %all-gather.7.cloned.1.call-start = ((), (), s32[]{:S(2)}) async-start(), calls=%async_computation.6 | async-start | bytes 2949120 | tf_op jit(solution)/shard_map/all_gather | solution.py:1146
  24.9 22.5 %collective-permute-start = (bf16[1024,128]{1,0:T(8,128)(2,1)S(1)}, bf16[1024,128]{1,0:T(8,128)(2,1)S(1)}, u32[]{:S(2)}, u32[]{:S(2)}) collective-permute-start(bf16[1024,128]{1,0:T(8,128)(2,1)S(1)} %bitcast.309), channel_id=1, source_target_pairs={{0,8},{4,12},{8,0},{12,4},{16,24},{20,28},{24,16},{28,20},{1,9},{5... | collective-permute-start | bytes 786440 | tf_op jit(solution)/shard_map/ppermute | solution.py:518
  27.0 20.5 %collective-permute-start.1 = (bf16[1024,128]{1,0:T(8,128)(2,1)S(1)}, bf16[1024,128]{1,0:T(8,128)(2,1)S(1)}, u32[]{:S(2)}, u32[]{:S(2)}) collective-permute-start(bf16[1024,128]{1,0:T(8,128)(2,1)S(1)} %bitcast.310), channel_id=1, source_target_pairs={{0,24},{4,28},{8,16},{12,20},{16,8},{20,12},{24,0},{28,4},{1,25},{... | collective-permute-start | bytes 786440 | tf_op jit(solution)/shard_map/ppermute | solution.py:522
  66.7 182.6 %all-gather.9.cloned.1.call-start = ((), (), s32[]{:S(2)}) async-start(), calls=%async_computation.7 | async-start | bytes 2949120 | tf_op jit(solution)/shard_map/all_gather | solution.py:1146
  78.4 21.7 %collective-permute-start.10 = (bf16[4,64,1024]{2,1,0:T(8,128)(2,1)}, bf16[4,64,1024]{2,1,0:T(8,128)(2,1)}, u32[]{:S(2)}, u32[]{:S(2)}) collective-permute-start(bf16[4,64,1024]{2,1,0:T(8,128)(2,1)} %get-tuple-element.378), channel_id=1, source_target_pairs={{0,4},{4,0},{8,12},{12,8},{16,20},{20,16},{24,28},{28,24},{1,5},{5... | collective-permute-start | bytes 1572872 | tf_op jit(solution)/shard_map/ppermute | solution.py:506
  80.0 20.1 %collective-permute-start.11 = (bf16[2,2,3,256,128]{4,3,2,1,0:T(8,128)(2,1)S(1)}, bf16[2,2,3,256,128]{4,3,2,1,0:T(8,128)(2,1)}, u32[]{:S(2)}, u32[]{:S(2)}) collective-permute-start(bf16[2,2,3,256,128]{4,3,2,1,0:T(8,128)(2,1)S(1)} %pad_maximum_fusion.4.refs_0_), channel_id=1, source_target_pairs={{0,1},{1,0},{2,3},{3,2},{4,5},{5,4},{6,7},{7,6},{8,9},{9,8},{10,11... | collective-permute-start | bytes 2359304 | tf_op jit(solution)/shard_map/ppermute | solution.py:514
  86.2 186.5 %all-gather.5.cloned.1.call-start = ((), (), s32[]{:S(2)}) async-start(), calls=%async_computation.5 | async-start | bytes 2949120 | tf_op jit(solution)/shard_map/all_gather | solution.py:1146
  97.0 23.2 %collective-permute-start.18 = (bf16[4,256,128]{2,1,0:T(8,128)(2,1)}, bf16[4,256,128]{2,1,0:T(8,128)(2,1)}, u32[]{:S(2)}, u32[]{:S(2)}) collective-permute-start(bf16[4,256,128]{2,1,0:T(8,128)(2,1)} %get-tuple-element.388), channel_id=1, source_target_pairs={{0,4},{4,0},{8,12},{12,8},{16,20},{20,16},{24,28},{28,24},{1,5},{5... | collective-permute-start | bytes 786440 | tf_op jit(solution)/shard_map/ppermute | solution.py:506
  101.1 19.1 %collective-permute-start.15 = (bf16[2,2,3,256,128]{4,3,2,1,0:T(8,128)(2,1)}, bf16[2,2,3,256,128]{4,3,2,1,0:T(8,128)(2,1)}, u32[]{:S(2)}, u32[]{:S(2)}) collective-permute-start(bf16[2,2,3,256,128]{4,3,2,1,0:T(8,128)(2,1)} %pad_maximum_fusion.5.refs_0_), channel_id=1, source_target_pairs={{0,1},{1,0},{2,3},{3,2},{4,5},{5,4},{6,7},{7,6},{8,9},{9,8},{10,11... | collective-permute-start | bytes 2359304 | tf_op jit(solution)/shard_map/ppermute | solution.py:514
  137.8 19.4 %collective-permute-start.21 = (bf16[2,2,4,256,128]{4,3,2,1,0:T(8,128)(2,1)S(1)}, bf16[2,2,4,256,128]{4,3,2,1,0:T(8,128)(2,1)S(1)}, u32[]{:S(2)}, u32[]{:S(2)}) collective-permute-start(bf16[2,2,4,256,128]{4,3,2,1,0:T(8,128)(2,1)S(1)} %pad_maximum_fusion.3.a_ref), channel_id=1, source_target_pairs={{0,1},{1,0},{2,3},{3,2},{4,5},{5,4},{6,7},{7,6},{8,9},{9,8},{10,11... | collective-permute-start | bytes 3145736 | tf_op jit(solution)/shard_map/ppermute | solution.py:514
  137.9 18.8 %collective-permute-start.22 = (bf16[352,1024]{1,0:T(8,128)(2,1)}, bf16[352,1024]{1,0:T(8,128)(2,1)S(1)}, u32[]{:S(2)}, u32[]{:S(2)}) collective-permute-start(bf16[352,1024]{1,0:T(8,128)(2,1)} %pad_maximum_fusion.8.refs_12_), channel_id=1, source_target_pairs={{0,2},{1,3},{2,0},{3,1},{4,6},{5,7},{6,4},{7,5},{8,10},{9,11},{10,... | collective-permute-start | bytes 2162696 | tf_op jit(solution)/shard_map/ppermute | solution.py:510
  138.7 34.0 %collective-permute-start.28 = (bf16[352,1024]{1,0:T(8,128)(2,1)}, bf16[352,1024]{1,0:T(8,128)(2,1)}, u32[]{:S(2)}, u32[]{:S(2)}) collective-permute-start(bf16[352,1024]{1,0:T(8,128)(2,1)} %pad_maximum_fusion.8.refs_12_), channel_id=1, source_target_pairs={{0,1},{1,0},{2,3},{3,2},{4,5},{5,4},{6,7},{7,6},{8,9},{9,8},{10,11... | collective-permute-start | bytes 2162696 | tf_op jit(solution)/shard_map/ppermute | solution.py:514
  163.4 325.8 %reduce-scatter.4.cloned.1.call-start = ((), (), s32[]{:S(2)}) async-start(), calls=%async_computation.8 | async-start | bytes 2949120 | tf_op jit(solution)/shard_map/reduce_scatter | solution.py:1192
  249.2 240.0 %reduce-scatter.6.cloned.1.call-start = ((), (), s32[]{:S(2)}) async-start(), calls=%async_computation.9 | async-start | bytes 2949120 | tf_op jit(solution)/shard_map/reduce_scatter | solution.py:1192
  302.6 35.0 %collective-permute-start.45 = (bf16[1280,1024]{1,0:T(8,128)(2,1)}, bf16[1280,1024]{1,0:T(8,128)(2,1)}, u32[]{:S(2)}, u32[]{:S(2)}) collective-permute-start(bf16[1280,1024]{1,0:T(8,128)(2,1)} %get-tuple-element.266), channel_id=1, source_target_pairs={{0,1},{1,0},{2,3},{3,2},{4,5},{5,4},{6,7},{7,6},{8,9},{9,8},{10,11... | collective-permute-start | bytes 7864328 | tf_op jit(solution)/shard_map/ppermute | solution.py:514
  315.5 173.7 %reduce-scatter.8.cloned.1.call-start = ((), (), s32[]{:S(2)}) async-start(), calls=%async_computation.10 | async-start | bytes 2949120 | tf_op jit(solution)/shard_map/reduce_scatter | solution.py:1192
  378.8 31.8 %collective-permute-start.50 = (bf16[2,4,256,512]{3,2,1,0:T(8,128)(2,1)}, bf16[2,4,256,512]{3,2,1,0:T(8,128)(2,1)}, u32[]{:S(2)}, u32[]{:S(2)}) collective-permute-start(bf16[2,4,256,512]{3,2,1,0:T(8,128)(2,1)} %get-tuple-element.280), channel_id=1, source_target_pairs={{0,1},{1,0},{2,3},{3,2},{4,5},{5,4},{6,7},{7,6},{8,9},{9,8},{10,11... | collective-permute-start | bytes 6291464 | tf_op jit(solution)/shard_map/ppermute | solution.py:514
  410.5 25.9 %collective-permute-start.54 = (bf16[2,2,256,512]{3,2,1,0:T(8,128)(2,1)}, bf16[2,2,256,512]{3,2,1,0:T(8,128)(2,1)}, u32[]{:S(2)}, u32[]{:S(2)}) collective-permute-start(bf16[2,2,256,512]{3,2,1,0:T(8,128)(2,1)} %get-tuple-element.291), channel_id=1, source_target_pairs={{0,1},{1,0},{2,3},{3,2},{4,5},{5,4},{6,7},{7,6},{8,9},{9,8},{10,11... | collective-permute-start | bytes 3145736 | tf_op jit(solution)/shard_map/ppermute | solution.py:514
  414.7 21.8 %collective-permute-start.52 = (bf16[2,2,128,512]{3,2,0,1:T(8,128)(2,1)}, bf16[2,2,128,512]{3,2,0,1:T(8,128)(2,1)S(1)}, u32[]{:S(2)}, u32[]{:S(2)}) collective-permute-start(bf16[2,2,128,512]{3,2,0,1:T(8,128)(2,1)} %bitcast.271), channel_id=1, source_target_pairs={{0,2},{1,3},{2,0},{3,1},{4,6},{5,7},{6,4},{7,5},{8,10},{9,11},{10,... | collective-permute-start | bytes 1572872 | tf_op jit(solution)/shard_map/ppermute | solution.py:510
  417.0 19.5 %collective-permute-start.53 = (bf16[2,2,128,512]{3,2,1,0:T(8,128)(2,1)}, bf16[2,2,128,512]{3,2,1,0:T(8,128)(2,1)}, u32[]{:S(2)}, u32[]{:S(2)}) collective-permute-start(bf16[2,2,128,512]{3,2,1,0:T(8,128)(2,1)} %slice_bitcast_fusion.7), channel_id=1, source_target_pairs={{0,4},{4,0},{8,12},{12,8},{16,20},{20,16},{24,28},{28,24},{1,5},{5... | collective-permute-start | bytes 1572872 | tf_op jit(solution)/shard_map/ppermute | solution.py:506
  447.3 19.4 %collective-permute-start.58 = (bf16[2,2,128,512]{3,2,0,1:T(8,128)(2,1)S(1)}, bf16[2,2,128,512]{3,2,0,1:T(8,128)(2,1)S(1)}, u32[]{:S(2)}, u32[]{:S(2)}) collective-permute-start(bf16[2,2,128,512]{3,2,0,1:T(8,128)(2,1)S(1)} %fusion.13), channel_id=1, source_target_pairs={{0,4},{4,0},{8,12},{12,8},{16,20},{20,16},{24,28},{28,24},{1,5},{5... | collective-permute-start | bytes 1572872 | tf_op jit(solution)/shard_map/ppermute | solution.py:506
  450.3 21.6 %collective-permute-start.60 = (bf16[4,64,1024]{2,1,0:T(8,128)(2,1)S(1)}, bf16[4,64,1024]{2,1,0:T(8,128)(2,1)S(1)}, u32[]{:S(2)}, u32[]{:S(2)}) collective-permute-start(bf16[4,64,1024]{2,1,0:T(8,128)(2,1)S(1)} %copy-done.68), channel_id=1, source_target_pairs={{0,4},{4,0},{8,12},{12,8},{16,20},{20,16},{24,28},{28,24},{1,5},{5... | collective-permute-start | bytes 1572872 | tf_op jit(solution)/shard_map/ppermute | solution.py:506
  492.3 26.8 %all-to-all-start.1 = ((bf16[4,3,3,96,256]{4,3,2,1,0:T(8,128)(2,1)}), bf16[4,3,3,96,256]{4,3,2,1,0:T(8,128)(2,1)S(1)}, u32[]{:S(2)}, u32[]{:S(2)}) async-start(bf16[4,3,3,96,256]{4,3,2,1,0:T(8,128)(2,1)} %bitcast.269), calls=%async_computation.4 | async-start | bytes 3538944 | tf_op jit(solution)/shard_map/all_to_all | solution.py:1073
  (130 other events, 1316.0 us)
Sparse Core Ops, SparseCore 0:
  66.8 49.4 all-gather.6
  117.9 49.3 all-gather.8
  168.8 49.2 all-gather.4
  249.3 45.8 reduce-scatter.3
  315.6 45.5 reduce-scatter.5
  419.6 50.6 reduce-scatter.7

commit v4 on v3

--- a/solution.py
+++ b/solution.py
@@ -542,8 +542,8 @@
     return pltpu.CompilerParams(vmem_limit_bytes=limit)
 
 
-COST_S = pl.CostEstimate(flops=10**6, bytes_accessed=10**6, transcendentals=0)
-COST_E = pl.CostEstimate(flops=10**6, bytes_accessed=10**6, transcendentals=0)
+COST_S = pl.CostEstimate(flops=10**10, bytes_accessed=10**6, transcendentals=0)
+COST_E = pl.CostEstimate(flops=25 * 10**9, bytes_accessed=10**6, transcendentals=0)
 ANY = pl.BlockSpec(memory_space=pl.ANY)
 SMEM = pl.BlockSpec(memory_space=pltpu.SMEM)
 
@@ -553,25 +553,28 @@
     return {0: v, 1: near, 3: opp, 2: pair_z(opp)}
 
 
-def attend_kernel(sz, first, x_first, idx, n_ref, w_ref, *refs):
-    pieces, refs = refs[:2], refs[2:]
+def attend_kernel(groups, first, idx, n_ref, w_ref, *refs):
+    pieces, refs = refs[: 2 * len(groups)], refs[2 * len(groups) :]
     if not first:
         refs = refs[4:]
     p_ref, o_ref, qkv_ref, wt_ref, bc_ref, bp_ref, qs_ref = refs
     z, y, x, c = idx[0], idx[1], idx[2], idx[3]
     step = pl.program_id(0)
-    for ry in range(2):
-
-        @pl.when(step == ry)
-        def _(ry=ry):
-            for rx in range(2):
-                for rc in range(2):
-                    row = pl.multiple_of(((x ^ rx) * 2 + (c ^ rc)) * 256, 256)
-                    for t in range(3):
-                        block = pieces[rc][ry, rx, t] if x_first else pieces[rc][rx, ry, t]
-                        wt_ref[0, pl.ds(row, 256), 128 * t : 128 * t + 128] = block
-
-    qkv = dot_nn(n_ref[...], wt_ref[0]).astype(BF)
+    for n, (sz, x_first) in enumerate(groups):
+        for ry in range(2):
+
+            @pl.when(step == 2 * n + ry)
+            def _(n=n, ry=ry, x_first=x_first):
+                for rx in range(2):
+                    for rc in range(2):
+                        row = pl.multiple_of(((x ^ rx) * 2 + (c ^ rc)) * 256, 256)
+                        src = pieces[2 * n + rc]
+                        for t in range(4):
+                            rows = slice(256 * t, 256 * t + 256)
+                            block = src[ry, rx, rows] if x_first else src[rx, ry, rows]
+                            wt_ref[0, pl.ds(row, 256), 128 * t : 128 * t + 128] = block
+
+    qkv = dot_nn(n_ref[...], wt_ref[0, :, :384]).astype(BF)
     qkv_ref[0] = qkv
     k, v = qkv[:, 128:256], qkv[:, 256:]
     qs_ref[...] = qkv[:, :128]
@@ -603,23 +606,52 @@
     o_ref[...] = jnp.where(lane < 64, outs[0], outs[1]).astype(BF)
 
 
-def attend(sz, x_first, idx, normed, windows, pieces, prev):
+def norm_kernel(idx, a_ref, b_ref, own_ref, gain_ref, src_ref, low_ref):
+    z, y = idx[0], idx[1]
+    for sz in range(4):
+        at = lambda yy: pl.ds(pl.multiple_of(((z ^ sz) * 2 + yy) * 64, 64), 64)
+        src_ref[at(y), :] = a_ref[sz]
+        src_ref[at(y ^ 1), :] = b_ref[sz]
+    src_ref[512:, :] = own_ref[64:, :]
+    values = src_ref[...].astype(F32)
+    low_ref[...] = (norm_parts(values) * gain_ref[...]).astype(BF)
+
+
+def norm_rows(idx, prompt_z, prompt_y, rows_own, gain):
+    whole = pl.BlockSpec(memory_space=pltpu.VMEM)
+    out = jax.ShapeDtypeStruct((768, 1024), BF)
+    return pl.pallas_call(
+        norm_kernel,
+        in_specs=[SMEM] + [whole] * 4,
+        out_specs=(whole, whole),
+        out_shape=(out, out),
+        compiler_params=params(),
+    )(idx, prompt_z, prompt_y, rows_own, gain[None])
+
+
+def attend(groups, idx, normed, windows, pieces, prev):
     keys, rows = normed.shape[0], 320
-    at = lambda i, d: (d[0] ^ sz) * 2 + (d[1] ^ i)
+
+    def at(i, d):
+        sz = groups[0][0]
+        for n, (other, unused) in enumerate(groups):
+            sz = jnp.where(i // 2 == n, other, sz)
+        return (d[0] ^ sz) * 2 + (d[1] ^ (i % 2))
+
     whole = pl.BlockSpec(memory_space=pltpu.VMEM)
     return pl.pallas_call(
-        functools.partial(attend_kernel, sz, prev is None, x_first),
+        functools.partial(attend_kernel, groups, prev is None),
         grid_spec=pltpu.PrefetchScalarGridSpec(
             num_scalar_prefetch=1,
-            grid=(2,),
+            grid=(2 * len(groups),),
             in_specs=[whole, pl.BlockSpec((2, 2, 8, 1024), lambda i, d: (at(i, d), 0, 0, 0))]
-            + [whole] * 2
+            + [whole] * len(pieces)
             + ([] if prev is None else [ANY] * 4),
             out_specs=(
                 pl.BlockSpec((2, rows, keys), lambda i, d: (at(i, d), 0, 0)),
                 pl.BlockSpec((rows, 128), lambda i, d: (0, at(i, d))),
                 pl.BlockSpec((1, keys, 384), lambda i, d: (at(i, d), 0, 0)),
-                pl.BlockSpec((1, 1024, 384), lambda i, d: (at(i, d), 0, 0)),
+                pl.BlockSpec((1, 1024, 512), lambda i, d: (at(i, d), 0, 0)),
             ),
             scratch_shapes=[pltpu.VMEM((256, 768), F32), pltpu.VMEM((64, 512), F32), pltpu.VMEM((keys, 128), BF)],
         ),
@@ -627,9 +659,9 @@
             jax.ShapeDtypeStruct((16, rows, keys), BF),
             jax.ShapeDtypeStruct((rows, 1024), BF),
             jax.ShapeDtypeStruct((8, keys, 384), BF),
-            jax.ShapeDtypeStruct((8, 1024, 384), BF),
+            jax.ShapeDtypeStruct((8, 1024, 512), BF),
         ),
-        input_output_aliases={} if prev is None else {5 + n: n for n in range(4)},
+        input_output_aliases={} if prev is None else {3 + len(pieces) + n: n for n in range(4)},
         compiler_params=params(),
         cost_estimate=COST_S,
     )(idx, normed, windows, *pieces, *([] if prev is None else prev))
@@ -688,7 +720,7 @@
             def _():
                 send_ref[x ^ xx, 0] = block
 
-    gn = dot_nt(dt, wt_ref[0])
+    gn = dot_nt(dt, wt_ref[0, :, :384])
 
     @pl.when(pl.program_id(0) == 0)
     def _():
@@ -712,7 +744,7 @@
                 whole,
                 pl.BlockSpec((2, rows, keys), lambda i, d: (at(i, d), 0, 0)),
                 pl.BlockSpec((1, keys, 384), lambda i, d: (at(i, d), 0, 0)),
-                pl.BlockSpec((1, 1024, 384), lambda i, d: (at(i, d), 0, 0)),
+                pl.BlockSpec((1, 1024, 512), lambda i, d: (at(i, d), 0, 0)),
                 pl.BlockSpec((rows, 128), lambda i, d: (0, at(i, d))),
                 pl.BlockSpec((rows, 1024), lambda i, d: (0, 0)),
                 pl.BlockSpec((rows, 128), lambda i, d: (0, at(i, d))),
@@ -754,7 +786,10 @@
     gh_ref[...] = grad
     low = grad.astype(BF)
     gl_ref[...] = low
-    gm_ref[...] = dot_nt(low, w_ref[...]).astype(BF)
+    total = dot_nt(low[:, :128], w_ref[0, :, 384:])
+    for n in range(1, 8):
+        total = total + dot_nt(low[:, 128 * n : 128 * n + 128], w_ref[n, :, 384:])
+    gm_ref[...] = total.astype(BF)
 
 
 def out_back(parts, hidden, gain, cot, w_o):
@@ -774,35 +809,26 @@
     )(*parts, hidden, gain[None], cot, w_o)
 
 
-def out_kernel(idx, m_ref, s_ref, g_ref, a_ref, b_ref, h_ref, l_ref, w_ref):
-    z, y, x, c = idx[0], idx[1], idx[2], idx[3]
-    for rx in range(2):
-        for ry in range(2):
-            for n, sz in enumerate((0, 1, 3, 2)):
-                col = pl.multiple_of(((z ^ sz) * 2 + (y ^ ry)) * 128, 128)
-                for rc, ref in ((0, a_ref), (1, b_ref)):
-                    row = pl.multiple_of(((x ^ rx) * 2 + (c ^ rc)) * 256, 256)
-                    w_ref[pl.ds(row, 256), pl.ds(col, 128)] = ref[rx, ry, n]
-    hidden = s_ref[...].astype(F32) + dot_nn(m_ref[...], w_ref[...])
-    h_ref[...] = hidden
+def out_kernel(m_ref, s_ref, g_ref, w_ref, h_ref, l_ref):
+    m = m_ref[...]
+    for n in range(8):
+        cols = slice(128 * n, 128 * n + 128)
+        h_ref[:, cols] = s_ref[:, cols].astype(F32) + dot_nn(m, w_ref[n, :, 384:])
+    hidden = h_ref[...]
     scale = lax.rsqrt(jnp.mean(hidden * hidden, axis=-1, keepdims=True) + epsilon)
     l_ref[...] = (hidden * scale * g_ref[...]).astype(BF)
 
 
-def project_out(idx, mixed, rows_own, gain, own, other):
+def project_out(mixed, rows_own, gain, wt):
     whole = pl.BlockSpec(memory_space=pltpu.VMEM)
     return pl.pallas_call(
         out_kernel,
-        in_specs=[SMEM] + [whole] * 5,
-        out_specs=(whole,) * 3,
-        out_shape=(
-            jax.ShapeDtypeStruct((320, 1024), F32),
-            jax.ShapeDtypeStruct((320, 1024), BF),
-            jax.ShapeDtypeStruct((1024, 1024), BF),
-        ),
+        in_specs=[whole] * 4,
+        out_specs=(whole,) * 2,
+        out_shape=(jax.ShapeDtypeStruct((320, 1024), F32), jax.ShapeDtypeStruct((320, 1024), BF)),
         compiler_params=params(),
         cost_estimate=COST_S,
-    )(idx, mixed, rows_own, gain[None], own, other)
+    )(mixed, rows_own, gain[None], wt)
 
 
 WIDE = 1920
@@ -913,47 +939,45 @@
                 continue
             k = rc * 5 + n
             copies.append(pltpu.make_async_copy(x_parts[k], x_scr.at[pl.ds(at, size)], sem.at[k, 0]))
-            for h in range(size // 160):
-                src = g_parts[k].at[pl.ds(176 * h, 160)]
-                dst = g_scr.at[pl.ds(at + 160 * h, 160)]
-                copies.append(pltpu.make_async_copy(src, dst, sem.at[k, 1 + h]))
+            copies.append(pltpu.make_async_copy(g_parts[k], g_scr.at[pl.ds(at, size)], sem.at[k, 1]))
     return copies
 
 
-def expert_kernel(expert, first, last, *refs):
+def expert_kernel(group, last, *refs):
     refs = list(refs)
     step = pl.program_id(0)
+    count = len(group)
+    idx, refs = refs[0], refs[1:]
+    w_at = idx[2] * 2 + idx[3]
     src, m_ref = refs[:2]
-    if first:
+    if not last:
         x_parts, g_parts = refs[2:12], refs[12:22]
-        at = 22
+        out_ref, dx_ref, dh_ref, win_ref, s_ref, xo_ref, go_ref, w_scr, sem, x_scr, g_scr, psem = refs[22:]
     else:
-        x_ref, g_ref, out_prev, dx_prev = refs[2:6]
-        at = 6
-    if last:
-        s0_ref, s1_ref = refs[at : at + 2]
-        at += 2
-    if first:
-        out_ref, dx_ref, dh_ref, win_ref, s_ref, xo_ref, go_ref, w_scr, sem, x_scr, g_scr, psem = refs[at:]
-    elif last:
-        out_ref, out_c_ref, dx_ref, dx_c_ref, dh_ref, win_ref, w_scr, sem = refs[at:]
-    else:
-        out_ref, dx_ref, dh_ref, win_ref, s_ref, w_scr, sem = refs[at:]
+        x_ref, g_ref, out_prev, dx_prev, s_prev = refs[2:7]
+        out_ref, out_c_ref, dx_ref, dx_c_ref, dh_ref, win_ref, w_scr, sem = refs[7:]
 
     @pl.when(step == 0)
     def _():
         copies = [
-            pltpu.make_async_copy(src.at[n], w_scr.at[:, pl.ds(96 * n, 96), :], sem.at[n]) for n in range(4)
+            pltpu.make_async_copy(
+                src.at[n, r, e],
+                w_scr.at[e, :, pl.ds(96 * n, 96), pl.ds(pl.multiple_of((w_at ^ r) * 256, 256), 256)],
+                sem.at[n, 4 * e + r],
+            )
+            for e in range(count)
+            for n in range(4)
+            for r in range(4)
         ]
         for copy in copies:
             copy.start()
-        if first:
+        if not last:
             for copy in fetch_pieces(None, x_parts, g_parts, x_scr, g_scr, psem):
                 copy.start()
         for copy in copies:
             copy.wait()
 
-    if first:
+    if not last:
         for t in range(4):
 
             @pl.when(step == t)
@@ -967,91 +991,88 @@
         go_ref[...] = g
     else:
         x, g = x_ref[...], g_ref[...]
-    w_gu = w_scr[0:2].reshape(768, 1024)
-    w_d = w_scr[2]
-    gu = dot_nt(x, w_gu)
-    gi = dot_nt(g, w_d)
-    gate, up = gu[:, :384], gu[:, 384:]
-    l = [gate[:, 88 + n : 89 + n] for n in range(3)]
-    top = jnp.maximum(jnp.maximum(l[0], l[1]), l[2])
-    ex = [jnp.exp(v - top) for v in l]
-    inv = 1.0 / (ex[0] + ex[1] + ex[2])
-    p = [v * inv for v in ex]
     m = m_ref[...]
-    keep = m[:, expert : expert + 1]
-    w = p[expert] * keep
-    sq = gate * gate
-    th = jnp.tanh(0.7978845608028654 * gate * (1.0 + 0.044715 * sq))
-    half1 = 0.5 + 0.5 * th
-    act = gate * half1
-    dact = half1 + (0.5 * gate) * (1.0 - th * th) * (0.7978845608028654 + 0.10703222440890037 * sq)
-    inner = (act * up).astype(BF).astype(F32)
-    s = jnp.sum(inner * gi, axis=-1, keepdims=True) * keep
-    gin = gi * w
-    dg = gin * up * dact
-    du = gin * act
+    lane = lax.broadcasted_iota(jnp.int32, (1, 384), 1)
+    scores = []
+    for k, expert in enumerate(group):
+        w_gu = w_scr[k, 0:2].reshape(768, 1024)
+        w_d = w_scr[k, 2]
+        gu = dot_nt(x, w_gu)
+        gi = dot_nt(g, w_d)
+        gate, up = gu[:, :384], gu[:, 384:]
+        if k == 0:
+            l = [gate[:, 88 + n : 89 + n] for n in range(3)]
+            top = jnp.maximum(jnp.maximum(l[0], l[1]), l[2])
+            ex = [jnp.exp(v - top) for v in l]
+            inv = 1.0 / (ex[0] + ex[1] + ex[2])
+            p = [v * inv for v in ex]
+        keep = m[:, expert : expert + 1]
+        w = p[expert] * keep
+        sq = gate * gate
+        th = jnp.tanh(0.7978845608028654 * gate * (1.0 + 0.044715 * sq))
+        half1 = 0.5 + 0.5 * th
+        act = gate * half1
+        dact = half1 + (0.5 * gate) * (1.0 - th * th) * (0.7978845608028654 + 0.10703222440890037 * sq)
+        inner = (act * up).astype(BF).astype(F32)
+        s = jnp.sum(inner * gi, axis=-1, keepdims=True) * keep
+        scores.append(s)
+        gin = gi * w
+        dg = gin * up * dact
+        du = gin * act
+        if last:
+            ss = [s_prev[...][:, 0:1], s_prev[...][:, 1:2], s]
+            dot = p[0] * ss[0] + p[1] * ss[1] + p[2] * ss[2]
+            for n in range(3):
+                dg = jnp.where(lane == 88 + n, p[n] * (ss[n] - dot), dg)
+        win = (inner * w).astype(BF)
+        dh = jnp.concatenate([dg.astype(BF), du.astype(BF)], axis=1)
+        dh_ref[:, 768 * k : 768 * k + 768] = dh
+        win_ref[:, 384 * k : 384 * k + 384] = win
+        o_k, dx_k = dot_nn(win, w_d), dot_nn(dh, w_gu)
+        out, dx = (o_k, dx_k) if k == 0 else (out + o_k, dx + dx_k)
     if last:
-        ss = [s0_ref[...][:, 0:1], s1_ref[...][:, 0:1], s]
-        dot = p[0] * ss[0] + p[1] * ss[1] + p[2] * ss[2]
-        lane = lax.broadcasted_iota(jnp.int32, (1, 384), 1)
-        for n in range(3):
-            dg = jnp.where(lane == 88 + n, p[n] * (ss[n] - dot), dg)
-    win = (inner * w).astype(BF)
-    dh = jnp.concatenate([dg.astype(BF), du.astype(BF)], axis=1)
-    dh_ref[...] = dh
-    win_ref[...] = win
-    if not last:
-        s_ref[...] = jnp.broadcast_to(s, s_ref.shape)
-    out = dot_nn(win, w_d)
-    dx = dot_nn(dh, w_gu)
-    if not first:
-        out = out + out_prev[...].astype(F32)
-        dx = dx + dx_prev[...].astype(F32)
-    if last:
+        out = (out + out_prev[...].astype(F32)).astype(BF)
+        dx = (dx + dx_prev[...].astype(F32)).astype(BF)
 
         @pl.when(step < 2)
         def _():
-            out_c_ref[...] = out.astype(BF)
-            dx_c_ref[...] = dx.astype(BF)
+            out_c_ref[...] = out
+            dx_c_ref[...] = dx
 
         @pl.when(step >= 2)
         def _():
-            out_ref[...] = out.astype(BF)
-            dx_ref[...] = dx.astype(BF)
+            out_ref[...] = out
+            dx_ref[...] = dx
     else:
         out_ref[...] = out.astype(BF)
         dx_ref[...] = dx.astype(BF)
-
-
-def expert_call(expert, x, g, m, src, prev, s_prev, tile=640):
-    total = 2560
-    first, last = expert == 0, expert == 2
+        s_ref[...] = jnp.where(lane[:, :128] == 0, scores[0], scores[1])
+
+
+def expert_call(group, idx, x, g, m, src, prev, tile=640):
+    total, count = 2560, len(group)
+    last = prev is not None
     at = (lambda i: i ^ 2) if last else (lambda i: i)
     row = lambda n: pl.BlockSpec((tile, n), lambda i: (at(i), 0))
     shape = lambda n, t: jax.ShapeDtypeStruct((total, n), t)
-    outs = [(1024, BF), (1024, BF), (768, BF), (384, BF), (8, F32)]
-    scratch = [pltpu.VMEM((3, 384, 1024), BF), pltpu.SemaphoreType.DMA((4,))]
-    if first:
-        ins = [src, m, *x, *g]
-        specs = [ANY, row(8)] + [ANY] * 20
-        outs += [(1024, BF), (1024, BF)]
-        scratch += [pltpu.VMEM((total, 1024), BF), pltpu.VMEM((total, 1024), BF), pltpu.SemaphoreType.DMA((10, 3))]
+    scratch = [pltpu.VMEM((count, 3, 384, 1024), BF), pltpu.SemaphoreType.DMA((4, 4 * count))]
+    if not last:
+        ins = [idx, src, m, *x, *g]
+        specs = [SMEM, ANY, row(128)] + [ANY] * 20
+        outs = [(1024, BF), (1024, BF), (768 * count, BF), (384 * count, BF), (128, F32), (1024, BF), (1024, BF)]
+        out_shape = tuple(shape(n, t) for n, t in outs)
+        out_specs = tuple(row(n) for n, t in outs)
+        scratch += [pltpu.VMEM((total, 1024), BF), pltpu.VMEM((total, 1024), BF), pltpu.SemaphoreType.DMA((10, 2))]
     else:
-        ins = [src, m, x, g, *prev]
-        specs = [ANY, row(8)] + [row(1024)] * 4
-    if last:
-        ins += list(s_prev)
-        specs += [row(8), row(8)]
+        ins = [idx, src, m, x, g, *prev]
+        specs = [SMEM, ANY, row(128)] + [row(1024)] * 4 + [row(128)]
         half = jax.ShapeDtypeStruct((total // 2, 1024), BF)
         mine = pl.BlockSpec((tile, 1024), lambda i: (jnp.maximum(i - 2, 0), 0))
         other = pl.BlockSpec((tile, 1024), lambda i: (jnp.minimum(i, 1), 0))
-        out_shape = (half, half, half, half, shape(768, BF), shape(384, BF))
-        out_specs = (mine, other, mine, other, row(768), row(384))
-    else:
-        out_shape = tuple(shape(n, t) for n, t in outs)
-        out_specs = tuple(row(n) for n, t in outs)
+        out_shape = (half, half, half, half, shape(768 * count, BF), shape(384 * count, BF))
+        out_specs = (mine, other, mine, other, row(768 * count), row(384 * count))
     return pl.pallas_call(
-        functools.partial(expert_kernel, expert, first, last),
+        functools.partial(expert_kernel, group, last),
         grid=(total // tile,),
         out_shape=out_shape,
         in_specs=specs,
@@ -1099,11 +1120,6 @@
         [gain_attn[None], gain_ffn[None], w_router.T, jnp.pad(rel_bias.reshape(1, 128), ((0, 0), (0, 128))),
          jnp.zeros((2, 256), BF)], axis=0
     )
-    small = lax.all_gather(packed, "wt", axis=0, tiled=False)
-    gain_attn_f = small[:, 0].reshape(1024).astype(F32)
-    gain_ffn_f = small[:, 1].reshape(1024).astype(F32)
-    bias_f = small[:, 5, :128].reshape(4, 32, 4).transpose(1, 0, 2).reshape(32, 16).astype(F32)
-
     ids, rank = expert_ids[0, 0], priority[0, 0]
     expert = ids.T.reshape(-1)
     rank_key = (jnp.arange(TOP, dtype=jnp.int32)[:, None] * 320 + rank[None, :]).reshape(-1)
@@ -1112,9 +1128,8 @@
     hold = jnp.sum(
         jnp.where((ids.T[:, :, None] == jnp.arange(EXPERTS, dtype=jnp.int32)) & keep[:, :, None], 1.0, 0.0), axis=0
     )
-    marks = jnp.pad(hold.reshape(2, 1, 480), ((0, 0), (0, 15), (0, 544))).astype(BF)
+    marks = jnp.pad(hold.reshape(960), (0, 1088)).astype(BF).reshape(16, 128)
     cot = cotangent[0, 0]
-    cot_marked = jnp.concatenate([cot[:160], marks[0], cot[160:], marks[1]], axis=0)
 
     def pieces(v):
         return jnp.pad(v.reshape(3, 4, 88, 256), ((0, 0), (0, 0), (0, 8), (0, 0)))
@@ -1126,118 +1141,126 @@
     )
     gate_p = jnp.concatenate([gate_p[:, :, :88], router_rows], axis=2)
     share = jnp.stack([gate_p, pieces(up_t), pieces(exp_down)], axis=1).transpose(2, 0, 1, 3, 4)
+    pick = lambda v, n, d: lax.dynamic_index_in_dim(v, n, d, keepdims=False)
+    unit = jnp.stack([w_query, w_key, w_value, w_out]).reshape(1024, 128)
+    prompt_own = rows_own[:64]
+    along = jnp.concatenate([unit, prompt_own.reshape(512, 128)], axis=0)
+    weights_in = lambda v: v[:1024]
+    rows_in = lambda v: v[1024:].reshape(64, 1024)
+    share = share.reshape(2, 2, 3, 3, 96, 256)
+    share_x, share_own = pick(share, 1 - x, 0), pick(share, x, 0)
+    packed_c, packed_x, packed_xc, along, share_x = phase(
+        move_c(packed), move_x(packed), lax.ppermute(packed, "wt", [(i, i ^ 3) for i in range(4)]), along, share_x
+    )
+    unit_0 = jnp.concatenate([unit, marks], axis=0)
+    near, opp, p_cross, y0, share_x, g_y, share_own = phase(
+        pair_z(along), flip_z(along), lax.ppermute(prompt_own, "ctx", [(i, i ^ 4) for i in range(8)]),
+        move_y(unit_0), move_x(share_x), move_y(cot), share_own
+    )
+    s0 = jnp.stack([unit_0, y0])
+    unit_1, unit_3 = weights_in(near), weights_in(opp)
+    prompt_z = jnp.stack([prompt_own, rows_in(near), p_cross, rows_in(opp)])
+    share = jnp.stack([share_own, share_x])
+    share_own, share_c = pick(share, c, 1), pick(share, 1 - c, 1)
+    s0, unit_1, unit_3, prompt_z, share_c, share_own, small = phase(
+        s0, unit_1, unit_3, prompt_z, share_c, share_own, jnp.stack([packed, packed_c, packed_x, packed_xc])
+    )
+    small = jnp.take(small, jnp.arange(4, dtype=jnp.int32) ^ wt_index, axis=0)
+    gain_attn_f = small[:, 0].reshape(1024).astype(F32)
+    gain_ffn_f = small[:, 1].reshape(1024).astype(F32)
+    bias_f = small[:, 5, :128].reshape(4, 32, 4).transpose(1, 0, 2).reshape(32, 16).astype(F32)
     table_rev = jnp.pad(bucket_table[::-1], (0, WIDE - 768), constant_values=-1)[None]
     windows = bias_windows(idx, table_rev, bias_f)
-
-    qkv_of = lambda u: u[:768].reshape(3, 256, 128)
-    prompt_own = rows_own[:64]
-    unit = jnp.stack([w_query, w_key, w_value, w_out]).reshape(1024, 128)
-    part_0 = qkv_of(unit)
-    share, small_first = phase(share, small)
-    near, opp, p_near, p_opp, y0 = phase(
-        pair_z(unit), flip_z(unit), pair_z(prompt_own), flip_z(prompt_own), move_y(part_0)
-    )
-    part_1, part_3 = qkv_of(near), qkv_of(opp)
-    s0 = jnp.stack([part_0, y0])
-    cross, p_cross, x0, x1, y3, share = phase(
-        pair_z(opp), pair_z(p_opp), move_x(s0), move_x(part_1), move_y(part_3), trade_wt(share)
-    )
-    share = share.transpose(1, 2, 3, 0, 4).reshape(3, 3, 96, 1024)
-    spread = [lax.all_gather(share[e], "ctx", axis=0, tiled=False, axis_index_groups=LINES_Z) for e in range(3)]
-    part_2 = qkv_of(cross)
-    t0, s1, s3 = jnp.stack([s0, x0]), jnp.stack([part_1, x1]), jnp.stack([part_3, y3])
-    prompt_z = jnp.stack([prompt_own, p_near, p_cross, p_opp])
-    prompt_y, c0, y1, x3, x2, windows, cot_marked = phase(
-        move_y(prompt_z), move_c(t0), move_y(s1), move_x(s3), move_x(part_2), windows, cot_marked
-    )
-    prompts = jnp.stack([prompt_z, prompt_y], axis=1).reshape(8, 64, 1024)
-    prompts = jnp.take(prompts, jnp.arange(8, dtype=jnp.int32) ^ ctx_index, axis=0).reshape(512, 1024)
-    source_all = jnp.concatenate([prompts, rows_own[64:]], axis=0)
-    all_low = (norm_parts(source_all.astype(F32)) * gain_attn_f).astype(BF)
-    t1, t3, s2 = jnp.stack([s1, y1]), jnp.stack([s3, x3]), jnp.stack([part_2, x2])
-    wo_z = jnp.stack([u[768:].reshape(256, 128) for u in (unit, near, opp, cross)])
-
-    state = attend(0, False, idx, all_low, windows, (t0, c0), None)
-    *state, c1, c3, y2, wo_y = phase(*state, move_c(t1), move_c(t3), move_y(s2), move_y(wo_z))
-    t2, wo_s = jnp.stack([s2, y2]), jnp.stack([wo_z, wo_y])
-    cot_marked, mixed_0 = phase(cot_marked, state[1])
-    state[1] = mixed_0
-    g_x, g_y = move_x(cot_marked), move_y(cot_marked)
-    state = attend(1, True, idx, all_low, windows, (t1, c1), state)
-    *state, c2, wo_x = phase(*state, move_c(t2), move_x(wo_s))
-    wo_t = jnp.stack([wo_s, wo_x])
-    state = attend(3, False, idx, all_low, windows, (t3, c3), state)
-    *state, wo_c, g_x, g_y = phase(*state, move_c(wo_t), g_x, g_y)
-    state = attend(2, True, idx, all_low, windows, (t2, c2), state)
-    *state, g_a, g_b, g_cx, g_cy, g_c = phase(
-        *state, move_x(g_y[:176]), move_y(g_x[176:]), move_c(g_x), move_c(g_y), move_c(cot_marked)
-    )
-    probs, mixed, qkv, w_qkv = state
-    hidden, normed, w_o = project_out(idx, mixed, rows_own, gain_ffn_f, wo_t, wo_c)
-
-    x_x, x_y, x_c, g_ca, g_cb = phase(move_x(normed), move_y(normed), move_c(normed), move_c(g_a), move_c(g_b))
+    cross, prompt_y, x0, x1, y3, windows, gain_attn_f = phase(
+        pair_z(unit_3), move_y(prompt_z), move_x(s0), move_x(unit_1), move_y(unit_3), windows, gain_attn_f
+    )
+    t0, s1, s3 = jnp.stack([s0, x0]), jnp.stack([unit_1, x1]), jnp.stack([unit_3, y3])
+    t0, s1, s3 = phase(t0, s1, s3)
+    c0, share_c, s1, s3 = phase(move_c(t0), move_c(share_c), s1, s3)
+    share = jnp.stack([share_own, share_c], axis=1).reshape(4, 3, 3, 96, 256)
+    spread = [
+        lax.all_gather(t, "ctx", axis=0, tiled=False, axis_index_groups=LINES_Z) for t in (share[:, :2], share[:, 2:])
+    ]
+    source_all, all_low = norm_rows(idx, prompt_z, prompt_y, rows_own, gain_attn_f)
+    state = attend(((0, False),), idx, all_low, windows, (t0, c0), None)
+    *state, y1, x3, x2, g_cy = phase(*state, move_y(s1), move_x(s3), move_x(cross), move_c(g_y))
+    t1, t3, s2, *state = phase(jnp.stack([s1, y1]), jnp.stack([s3, x3]), jnp.stack([cross, x2]), *state)
+    c1, c3, *state = phase(move_c(t1), move_c(t3), *state)
+    state = attend(((1, True), (3, False)), idx, all_low, windows, (t1, c1, t3, c3), state)
+    *state, y2, g_x, g_c = phase(*state, move_y(s2), move_x(cot), move_c(cot))
+    t2, g_ya, g_xb, *state = phase(jnp.stack([s2, y2]), g_y[:160], g_x[160:], *state)
+    c2, *state = phase(move_c(t2), *state)
+    state = attend(((2, True),), idx, all_low, windows, (t2, c2), state)
+    marks_all = jnp.stack([t0[:, :, 1024:], c0[:, :, 1024:]]).reshape(2, 2, 2, 2048)[..., :960]
+    marks_all = marks_all.transpose(0, 2, 1, 3).reshape(2560, 3).astype(F32)
+    marks_all = jnp.pad(marks_all, ((0, 0), (0, 125)))
+    *state, g_a, g_b, g_cx, marks_all = phase(*state, move_x(g_ya), move_y(g_xb), move_c(g_x), marks_all)
+    probs, mixed, qkv, w_all = state
+    hidden, normed = project_out(mixed, rows_own, gain_ffn_f, w_all)
+    hidden, normed, g_ca, g_cb = phase(hidden, normed, move_c(g_a), move_c(g_b))
+
+    x_x, x_y, x_c = phase(move_x(normed), move_y(normed), move_c(normed))
     x_a, x_b, x_cx, x_cy = phase(move_x(x_y[:160]), move_y(x_x[160:]), move_c(x_x), move_c(x_y))
     x_parts = [normed, x_x, x_y, x_a, x_b, x_c, x_cx, x_cy, move_c(x_a), move_c(x_b)]
-    cot_parts = [cot_marked, g_x, g_y, g_a, g_b, g_c, g_cx, g_cy, g_ca, g_cb]
-    marks_of = lambda v: [v[n + 160] for n in range(0, v.shape[0], 176)]
-    marks_all = jnp.stack(sum([marks_of(v) for v in cot_parts], []))[:, :480].reshape(2560, 3).astype(F32)
-    marks_all = jnp.pad(marks_all, ((0, 0), (0, 5)))
-
-    def weight_grads(dh_e, win_e):
-        gw = dot_tn(dh_e, x_all).astype(BF).reshape(2, 4, 96, 1024)
-        dw = dot_tn(win_e, g_all).astype(BF).reshape(1, 4, 96, 1024)
-        return jnp.concatenate([gw, dw], axis=0).transpose(1, 0, 2, 3)
-
-    def along_z(both):
-        return lax.psum_scatter(both, "ctx", scatter_dimension=0, axis_index_groups=LINES_Z)
-
-    res = expert_call(0, x_parts, cot_parts, marks_all, spread[0], None, [])
-    x_all, g_all = res[5:]
-    both_0, s_0 = weight_grads(res[2], res[3]), res[4]
-    res = expert_call(1, x_all, g_all, marks_all, spread[1], res[:2], [])
-    both_1, s_1 = weight_grads(res[2], res[3]), res[4]
+    cot_parts = [cot, g_x, g_y, g_a, g_b, g_c, g_cx, g_cy, g_ca, g_cb]
+
+    def along_z(gw, dw):
+        gw, dw = gw.astype(BF).reshape(-1, 2, 4, 96, 1024), dw.astype(BF).reshape(-1, 1, 4, 96, 1024)
+        return jnp.concatenate([gw, dw], axis=1).transpose(2, 0, 1, 3, 4)
+
+    def reduce_z(both):
+        flat = both.reshape(4, -1, 1024)
+        got = lax.psum_scatter(flat, "ctx", scatter_dimension=0, axis_index_groups=LINES_Z)
+        return got.reshape(both.shape[1:])
+
+    out, dx, dh, win, s_01, x_all, g_all = expert_call((0, 1), idx, x_parts, cot_parts, marks_all, spread[0], None)
+    both_01 = along_z(dot_tn(dh, x_all), dot_tn(win, g_all))
+    both_01, out = phase(both_01, out)
+    bulk = [reduce_z(both_01)]
     out, out_c, dx, dx_c, dh_2, win_2 = expert_call(
-        2, x_all, g_all, marks_all, spread[2], res[:2], [s_0, s_1]
-    )
-    bulk = [along_z(both_0), along_z(both_1)]
-
-    got, dh_2, win_2 = phase(move_c(dx_c), dh_2, win_2)
+        (2,), idx, x_all, g_all, marks_all, spread[1], (out, dx, s_01)
+    )
+
+    got, g_d2, dh_2 = phase(move_c(dx_c), dot_tn(win_2, g_all), dh_2)
     last, rest = add_low(dx[960:], got[960:]), add_low(dx[:960], got[:960])
-    g_w2 = dot_tn(dh_2, x_all).astype(BF)
-    d_a, d_b, rest, g_w2, win_2 = phase(move_x(last[:160]), move_y(last[160:]), rest, g_w2, win_2)
+    last_a, last_b, dh_2, rest = phase(last[:160], last[160:], dh_2, rest)
+    both_2 = along_z(dot_tn(dh_2, x_all), g_d2)
+    d_a, d_b, rest, both_2, o_got = phase(move_x(last_a), move_y(last_b), rest, both_2, move_c(out_c))
 
     def mix_in(rest, a, b):
         v_x = jnp.concatenate([rest[320:480], add_low(rest[480:640], b)], axis=0)
         v_y = jnp.concatenate([add_low(rest[640:800], a), rest[800:]], axis=0)
         return v_x, v_y
 
+    bulk.append(reduce_z(both_2))
     v_x, v_y = mix_in(rest, d_a, d_b)
-    g_d2 = dot_tn(win_2, g_all).astype(BF)
-    v_x, v_y, o_got, g_d2 = phase(move_x(v_x), move_y(v_y), move_c(out_c), g_d2)
-    both_2 = jnp.concatenate([g_w2.reshape(2, 4, 96, 1024), g_d2.reshape(1, 4, 96, 1024)], axis=0).transpose(1, 0, 2, 3)
-    router_part = both_2[0, 0, 88:96].astype(F32)
+    v_x, v_y, out, o_got = phase(v_x, v_y, out, o_got)
+    o_last, o_rest = add_low(out[960:], o_got[960:]), add_low(out[:960], o_got[:960])
+    v_x, v_y, o_la, o_lb, o_rest = phase(move_x(v_x), move_y(v_y), o_last[:160], o_last[160:], o_rest)
+    router_part = both_2[0, 0, 0, 88:96].astype(F32)
     grad_hidden, grad_low, grad_mixed, gain_ffn_part = out_back(
-        (rest[:320], v_x, v_y), hidden, gain_ffn_f, cot, w_o
-    )
-    bulk.append(along_z(both_2))
-    o_last, o_rest = add_low(out[960:], o_got[960:]), add_low(out[:960], o_got[:960])
+        (rest[:320], v_x, v_y), hidden, gain_ffn_f, cot, w_all
+    )
     back_of = lambda base, count, *prev: attend_back(
-        base, count, idx, all_low, probs, qkv, w_qkv, grad_mixed, mixed, grad_low, *prev
+        base, count, idx, all_low, probs, qkv, w_all, grad_mixed, mixed, grad_low, *prev
     )
     keep_f, send_f, gn, dbias = back_of(4, 4, None, None)
-    o_a, o_b, gn = phase(move_x(o_last[:160]), move_y(o_last[160:]), gn)
-    o_x, o_y = mix_in(o_rest, o_a, o_b)
+    o_a, o_b, gn = phase(move_x(o_la), move_y(o_lb), gn)
+    o_x, o_y, gn = phase(*mix_in(o_rest, o_a, o_b), gn)
+    o_x, o_y, gn, bulk[0] = phase(o_x, o_y, gn, bulk[0])
     keep_n, send_n, gn, dbias = back_of(2, 2, gn, dbias)
     o_x, o_y, got, gn = phase(move_x(o_x), move_y(o_y), move_c(send_f), gn)
     combined = o_rest[:320].astype(F32) + o_x.astype(F32) + o_y.astype(F32)
     output = (hidden + combined).astype(BF).reshape(1, 1, 320, 1024)
 
     fa, fb = cut_rows(add_low(keep_f, got).reshape(2, 2, 2, 256, 512))
+    fa0, fa1, fb0, fb1, gn = phase(fa[0], fa[1], fb[:, :, 0], fb[:, :, 1], gn)
     keep_h, send_h, gn_all, dbias = back_of(0, 2, gn, dbias)
-    fx, fy, got_n, gn_all = phase(move_x(fa[1]), move_y(fb[:, :, 1]), move_c(send_n), gn_all)
-    fa, fb = add_low(fa[0], fx), add_low(fb[:, :, 0], fy)
+    fx, fy, got_n, gn_all = phase(move_x(fa1), move_y(fb1), move_c(send_n), gn_all)
+    fa, fb = add_low(fa0, fx), add_low(fb0, fy)
     packed = pack(idx, table_rev, dbias, gn_all, source_all, gain_ffn_part, router_part)
     got, fy, fx, smalls, gp_keep, gp_send = phase(move_c(send_h), move_y(fa[:, 1]), move_x(fb[1]), *packed)
+    fy, bulk[1] = phase(fy, bulk[1])
     far = jnp.concatenate([add_low(fa[:, 0], fy), add_low(fb[0], fx)], axis=1)
     block = lambda t: t.reshape(2, 1, 2, 256, 512)
     h = jnp.concatenate([add_low(block(keep_h), block(got)), add_low(block(keep_n), block(got_n))], axis=1)
@@ -1265,7 +1288,7 @@
     res_gain_attn, res_gain_ffn, res_router = mine[0], mine[1], mine[2:5].T
     res_bias = lax.dynamic_slice_in_dim(smalls[8:24, :BUCKETS], wt_index * 4, 4, 0).T
 
-    back = jnp.stack(bulk).reshape(3, 3, 96, 4, 256).transpose(3, 0, 1, 2, 4)
+    back = jnp.concatenate(bulk).reshape(3, 3, 96, 4, 256).transpose(3, 0, 1, 2, 4)
     back = trade_wt(back)[:, :, :, :88].transpose(1, 2, 0, 3, 4).reshape(3, 3, 352, 256).astype(F32)
     res_gate, res_up, res_down = back[:, 0].transpose(0, 2, 1), back[:, 1].transpose(0, 2, 1), back[:, 2]
 

time: 534 us -> 482 us (0.903)
  waiting for transfers between devices: 120 us -> 97 us
  other arithmetic: 49.7 us -> 43.4 us
  blocking collectives: 6.18 us -> 0 us
    ppermute x9 -> x7, waiting for transfers between devices: 38.9 us -> 16.7 us  [pair_z(): return lax.ppermute(v, 'ctx', PAIR_Z)]
    pallas_call x8 -> x7, Pallas kernels: 120 us -> 112 us  [the longest x2 68 us: expert_call(): pl.pallas_call(functools.partial(expert_kernel, group, last), grid=(total...]
    all_gather x1 -> x0, blocking collectives: 6.18 us -> none  [local_fast(): small = lax.all_gather(packed, 'wt', axis=0, tiled=False)]
    ppermute x18 -> x19, waiting for transfers between devices: 49.1 us -> 43.7 us  [move_x(): return lax.ppermute(v, 'wt', SWAP_X)]
    dot_general x6 -> x4, matrix products: 31.8 us -> 28 us  [dot_tn(): lax.dot_general(a, b, (((0,), (0,)), ((), ())), preferred_element_type=F32)]
    unnamed x153 -> x140, local copies, waits for them, and re-layouts: 9.43 us -> 12.5 us
    ppermute x20 -> x19, starting transfers between devices: 23.5 us -> 21.6 us  [move_y(): return lax.ppermute(v, 'ctx', SWAP_Y)]
    ppermute x18 -> x19, starting transfers between devices: 19.5 us -> 21.3 us  [move_x(): return lax.ppermute(v, 'wt', SWAP_X)]
  transfers between devices with their start and end apart: 81 -> 78, of which waited for: 31 -> 27; matrix products, arithmetic and copies ran while one was open for 21% -> 18% of each run, Pallas kernels for 36% -> 39%
where the time goes in v4:
time: 482 us; the launch traced here: 476 us
  Pallas kernels  186 us (39%)
  waiting for transfers between devices  97 us (20%)
  starting transfers between devices  64.5 us (13%)
  other arithmetic  43.4 us (9%)
  local copies, waits for them, and re-layouts  41.8 us (9%)
  matrix products  28 us (6%)
  between operations  15.7 us (3%)
    pallas_call x2, Pallas kernels, expert_call(): pl.pallas_call(functools.partial(expert_kernel, group, last), grid=(total...  68 us
    pallas_call x3, Pallas kernels, attend_back(): pl.pallas_call(functools.partial(attend_back_kernel, gn_prev is None), gr...  54.3 us
    ppermute x19, waiting for transfers between devices, move_x(): return lax.ppermute(v, 'wt', SWAP_X)  43.7 us
    pallas_call x3, Pallas kernels, attend(): pl.pallas_call(functools.partial(attend_kernel, groups, prev is None), gr...  33.9 us
    dot_general x4, matrix products, dot_tn(): lax.dot_general(a, b, (((0,), (0,)), ((), ())), preferred_element_type=F32)  28 us
    ppermute x19, waiting for transfers between devices, move_y(): return lax.ppermute(v, 'ctx', SWAP_Y)  22.1 us
    ppermute x19, starting transfers between devices, move_y(): return lax.ppermute(v, 'ctx', SWAP_Y)  21.6 us
    ppermute x19, starting transfers between devices, move_x(): return lax.ppermute(v, 'wt', SWAP_X)  21.3 us
  transfers between devices with their start and end apart: 78, of which 27 were waited for; matrix products, arithmetic and copies ran while one was open for 18% of the time, Pallas kernels for 39%

profile of v4, /device:TPU:0, one launch (start us, length us, event | category | flops | bytes accessed | tf_op | source)
XLA Modules:
  0.0 476.1 jit_solution(1259830247811091103)
XLA Ops:
  31.2 5.6 %collective-permute-done.6 = bf16[1040,128]{1,0:T(8,128)(2,1)} collective-permute-done((bf16[1040,128]{1,0:T(8,128)(2,1)S(1)}, bf16[1040,128]{1,0:T(8,128)(2,1)}, u32[]{:S(2)}, u32[]{:S(2)}) %collective-permute-start.6) | collective-permute-done | bytes 266272 | tf_op jit(solution)/shard_map/ppermute | solution.py:506
  36.8 9.9 %collective-permute-done.3 = bf16[1536,128]{1,0:T(8,128)(2,1)} collective-permute-done((bf16[1536,128]{1,0:T(8,128)(2,1)}, bf16[1536,128]{1,0:T(8,128)(2,1)}, u32[]{:S(2)}, u32[]{:S(2)}) %collective-permute-start.3) | collective-permute-done | bytes 393248 | tf_op jit(solution)/shard_map/ppermute | solution.py:518
  66.7 10.0 %collective-permute-done.12 = bf16[1024,128]{1,0:T(8,128)(2,1)} collective-permute-done((bf16[1024,128]{1,0:T(8,128)(2,1)S(1)}, bf16[1024,128]{1,0:T(8,128)(2,1)}, u32[]{:S(2)}, u32[]{:S(2)}) %collective-permute-start.12) | collective-permute-done | bytes 262176 | tf_op jit(solution)/shard_map/ppermute | solution.py:510
  90.3 9.3 %shard_map.257 = (bf16[16,320,768]{2,1,0:T(8,128)(2,1)}, bf16[320,1024]{1,0:T(8,128)(2,1)}, bf16[8,768,384]{2,1,0:T(8,128)(2,1)}, bf16[8,1024,512]{2,1,0:T(8,128)(2,1)}) custom-call(s32[4]{0:T(128)} %pad_add_fusion.idx.refs_0_, bf16[768,1024]{1,0:T(8,128)(2,1)} %get-tuple-element.239.n_ref, f32[16,2,8,1024]{3,2,1,0:T(8,128)} %shard_map.255.w_ref, ...), custom_call_target="tpu_custom_call" | custom-call | flops 10000000000 | bytes 1000000 | tf_op jit(solution)/shard_map/pallas_call | solution.py:642
  110.3 15.2 %shard_map.258 = (bf16[16,320,768]{2,1,0:T(8,128)(2,1)}, bf16[320,1024]{1,0:T(8,128)(2,1)}, bf16[8,768,384]{2,1,0:T(8,128)(2,1)}, bf16[8,1024,512]{2,1,0:T(8,128)(2,1)}) custom-call(s32[4]{0:T(128)} %pad_add_fusion.idx.refs_0_, bf16[768,1024]{1,0:T(8,128)(2,1)} %get-tuple-element.239.n_ref, ...), custom_call_target="tpu_custom_call", output_to_operand_aliasing={{0}: (7, {}), {1}: (8, {}), {2}: (9, {}), {3}: (10, {})} | custom-call | flops 10000000000 | bytes 1000000 | tf_op jit(solution)/shard_map/pallas_call | solution.py:642
  132.3 9.4 %shard_map.259 = (bf16[16,320,768]{2,1,0:T(8,128)(2,1)}, bf16[320,1024]{1,0:T(8,128)(2,1)}, bf16[8,768,384]{2,1,0:T(8,128)(2,1)}, bf16[8,1024,512]{2,1,0:T(8,128)(2,1)}) custom-call(s32[4]{0:T(128)} %pad_add_fusion.idx.refs_0_, bf16[768,1024]{1,0:T(8,128)(2,1)} %get-tuple-element.239.n_ref, ...), custom_call_target="tpu_custom_call", output_to_operand_aliasing={{0}: (5, {}), {1}: (6, {}), {2}: (7, {}), {3}: (8, {})} | custom-call | flops 10000000000 | bytes 1000000 | tf_op jit(solution)/shard_map/pallas_call | solution.py:642
  142.3 6.6 %shard_map.260 = (f32[320,1024]{1,0:T(8,128)}, bf16[320,1024]{1,0:T(8,128)(2,1)}) custom-call(bf16[320,1024]{1,0:T(8,128)(2,1)} %get-tuple-element.303.m_ref, bf16[320,1024]{1,0:T(8,128)(2,1)} %bitcast.252, f32[1,1024]{1,0:T(1,128)} %convert.27.g_ref.gain_ref, bf16[8,1024,512]{2,1,0:T(8,128)(2,1)} %get-tuple-element.304.w_ref.wt_ref), custom_call_target="tpu_custom_call" | custom-call | flops 10000000000 | bytes 1000000 | tf_op jit(solution)/shard_map/pallas_call | solution.py:824
  152.5 14.2 %collective-permute-done.31.refs_4_ = bf16[320,1024]{1,0:T(8,128)(2,1)S(1)} collective-permute-done((bf16[320,1024]{1,0:T(8,128)(2,1)}, bf16[320,1024]{1,0:T(8,128)(2,1)S(1)}, u32[]{:S(2)}, u32[]{:S(2)}) %collective-permute-start.31) | collective-permute-done | bytes 655392 | tf_op jit(solution)/shard_map/ppermute | solution.py:510
  170.8 8.0 %collective-permute-done.34.refs_6_ = bf16[160,1024]{1,0:T(8,128)(2,1)S(1)} collective-permute-done((bf16[160,1024]{1,0:T(8,128)(2,1)S(1)}, bf16[160,1024]{1,0:T(8,128)(2,1)S(1)}, u32[]{:S(2)}, u32[]{:S(2)}) %collective-permute-start.34) | collective-permute-done | bytes 327712 | tf_op jit(solution)/shard_map/ppermute | solution.py:510
  183.1 37.4 %shard_map.261 = (bf16[2560,1024]{1,0:T(8,128)(2,1)}, bf16[2560,1024]{1,0:T(8,128)(2,1)}, bf16[2560,1536]{1,0:T(8,128)(2,1)}, bf16[2560,768]{1,0:T(8,128)(2,1)},...) custom-call(s32[4]{0:T(128)} %pad_add_fusion.idx.refs_0_, ...), custom_call_target="tpu_custom_call" | custom-call | flops 24999999488 | bytes 1000000 | tf_op jit(solution)/shard_map/pallas_call | solution.py:1074
  220.5 8.1 %convolution_convert_fusion.2 = bf16[768,1024]{1,0:T(8,128)(2,1)S(1)} fusion(bf16[2560,768]{1,0:T(8,128)(2,1)} %get-tuple-element.329, bf16[2560,1024]{1,0:T(8,128)(2,1)} %get-tuple-element.327.refs_4_), kind=kOutput, calls=%fused_computation.23 | convolution fusion | flops 4027318272 | bytes 10747904 | tf_op jit(solution)/shard_map/dot_general | solution.py:534
  228.7 9.3 %convolution_convert_fusion = bf16[1536,1024]{1,0:T(8,128)(2,1)S(1)} fusion(bf16[2560,1536]{1,0:T(8,128)(2,1)S(1)} %copy-done.65, bf16[2560,1024]{1,0:T(8,128)(2,1)S(1)} %copy-done.63), kind=kOutput, calls=%fused_computation.5 | convolution fusion | flops 8054636544 | bytes 16252928 | tf_op jit(solution)/shard_map/dot_general | solution.py:534
  240.8 30.7 %shard_map.262 = (bf16[1280,1024]{1,0:T(8,128)(2,1)}, bf16[1280,1024]{1,0:T(8,128)(2,1)}, bf16[1280,1024]{1,0:T(8,128)(2,1)}, bf16[1280,1024]{1,0:T(8,128)(2,1)}...) custom-call(s32[4]{0:T(128)} %pad_add_fusion.idx.refs_0_, bf16[4,4,1,3,96,256]{5,4,3,2,1,0:T(8,128)(2,1)} %bitcast.284, ...), custom_call_target="tpu_custom_call" | custom-call | flops 24999999488 | bytes 1000000 | tf_op jit(solution)/shard_map/pallas_call | solution.py:1074
  280.4 6.8 %convolution_convert_fusion.1 = bf16[768,1024]{1,0:T(8,128)(2,1)S(1)} fusion(bf16[2560,768]{1,0:T(8,128)(2,1)S(1)} %copy-done.64, bf16[2560,1024]{1,0:T(8,128)(2,1)} %get-tuple-element.326.refs_3_), kind=kOutput, calls=%fused_computation.22 | convolution fusion | flops 4027318272 | bytes 10747904 | tf_op jit(solution)/shard_map/dot_general | solution.py:534
  299.7 7.2 %collective-permute-done.44.b_ref = bf16[320,1024]{1,0:T(8,128)(2,1)} collective-permute-done((bf16[320,1024]{1,0:T(8,128)(2,1)}, bf16[320,1024]{1,0:T(8,128)(2,1)}, u32[]{:S(2)}, u32[]{:S(2)}) %collective-permute-start.44) | collective-permute-done | bytes 655392 | tf_op jit(solution)/shard_map/ppermute | solution.py:510
  309.7 7.9 %shard_map.263 = (f32[320,1024]{1,0:T(8,128)}, bf16[320,1024]{1,0:T(8,128)(2,1)}, bf16[320,1024]{1,0:T(8,128)(2,1)}, f32[8,1024]{1,0:T(8,128)}) custom-call(bf16[320,1024]{1,0:T(8,128)(2,1)} %slice.278.a_ref, bf16[320,1024]{1,0:T(8,128)(2,1)} %collective-permute-done.44.b_ref, bf16[320,1024]{1,0:T(8,128)(2,1)} %collective-permute-done.45.c_ref, ...), custom_call_target="tpu_custom_call" | custom-call | flops 10000000000 | bytes 1000000 | tf_op jit(solution)/shard_map/pallas_call | solution.py:797
  317.5 23.3 %shard_map.264 = (bf16[2,4,256,512]{3,2,1,0:T(8,128)(2,1)}, bf16[2,4,256,512]{3,2,1,0:T(8,128)(2,1)}, f32[768,1024]{1,0:T(8,128)}, f32[16,2,8,1024]{3,2,1,0:T(8,128)}) custom-call(s32[4]{0:T(128)} %pad_add_fusion.idx.refs_0_, bf16[768,1024]{1,0:T(8,128)(2,1)} %get-tuple-element.239.n_ref, bf16[16,320,768]{2,1,0:T(8,128)(2,1)} %get-tuple-element.358.p_ref, ...), custom_call_target="tpu_custom_call" | custom-call | flops 24999999488 | bytes 1000000 | tf_op jit(solution)/shard_map/pallas_call | solution.py:738
  343.6 15.4 %shard_map.265 = (bf16[2,2,256,512]{3,2,1,0:T(8,128)(2,1)}, bf16[2,2,256,512]{3,2,1,0:T(8,128)(2,1)}, f32[768,1024]{1,0:T(8,128)}, f32[16,2,8,1024]{3,2,1,0:T(8,128)}) custom-call(s32[4]{0:T(128)} %pad_add_fusion.idx.refs_0_, bf16[768,1024]{1,0:T(8,128)(2,1)} %get-tuple-element.239.n_ref, ...), custom_call_target="tpu_custom_call", output_to_operand_aliasing={{3}: (9, {})} | custom-call | flops 24999999488 | bytes 1000000 | tf_op jit(solution)/shard_map/pallas_call | solution.py:738
  362.7 15.6 %shard_map.266 = (bf16[2,2,256,512]{3,2,1,0:T(8,128)(2,1)}, bf16[2,2,256,512]{3,2,1,0:T(8,128)(2,1)}, f32[768,1024]{1,0:T(8,128)}, f32[16,2,8,1024]{3,2,1,0:T(8,128)}) custom-call(s32[4]{0:T(128)} %pad_add_fusion.idx.refs_0_, bf16[768,1024]{1,0:T(8,128)(2,1)} %get-tuple-element.239.n_ref, ...), custom_call_target="tpu_custom_call", output_to_operand_aliasing={{3}: (9, {})} | custom-call | flops 24999999488 | bytes 1000000 | tf_op jit(solution)/shard_map/pallas_call | solution.py:738
  381.9 4.8 %shard_map.267 = (f32[24,1024]{1,0:T(8,128)}, bf16[4,64,1024]{2,1,0:T(8,128)(2,1)}, bf16[4,64,1024]{2,1,0:T(8,128)(2,1)}) custom-call(s32[4]{0:T(128)} %pad_add_fusion.idx.refs_0_, s32[1,1920]{1,0:T(1,128)} %broadcast_in_dim.51.t_ref, f32[16,2,8,1024]{3,2,1,0:T(8,128)} %get-tuple-element.394.db_ref, f32[768,1024]{1,0:T(8,128)} %get-tuple-element.395.gn_ref, ...), custom_call_target="tpu_custom_call" | custom-call | flops 10000000000 | bytes 1000000 | tf_op jit(solution)/shard_map/pallas_call | solution.py:888
  400.0 5.4 %collective-permute-done.59 = bf16[256,512]{1,0:T(8,128)(2,1)S(1)} collective-permute-done((bf16[256,512]{1,0:T(8,128)(2,1)S(1)}, bf16[256,512]{1,0:T(8,128)(2,1)S(1)}, u32[]{:S(2)}, u32[]{:S(2)}) %collective-permute-start.59) | collective-permute-done | bytes 262176 | tf_op jit(solution)/shard_map/ppermute | solution.py:518
  408.8 8.7 %collective-permute-done.60 = bf16[4,64,1024]{2,1,0:T(8,128)(2,1)} collective-permute-done((bf16[4,64,1024]{2,1,0:T(8,128)(2,1)}, bf16[4,64,1024]{2,1,0:T(8,128)(2,1)}, u32[]{:S(2)}, u32[]{:S(2)}) %collective-permute-start.60) | collective-permute-done | bytes 524320 | tf_op jit(solution)/shard_map/ppermute | solution.py:506
  453.8 6.4 %collective-permute-done.72 = f32[24,1024]{1,0:T(8,128)S(1)} collective-permute-done((f32[24,1024]{1,0:T(8,128)S(1)}, f32[24,1024]{1,0:T(8,128)S(1)}, u32[]{:S(2)}, u32[]{:S(2)}) %collective-permute-start.72) | collective-permute-done | bytes 98336 | tf_op jit(solution)/shard_map/ppermute | solution.py:1286
  462.1 5.0 %all-to-all-done = bf16[4,3,3,96,256]{4,3,2,1,0:T(8,128)(2,1)S(1)} async-done(((bf16[4,3,3,96,256]{4,3,2,1,0:T(8,128)(2,1)}), bf16[4,3,3,96,256]{4,3,2,1,0:T(8,128)(2,1)S(1)}, u32[]{:S(2)}, u32[]{:S(2)}) %all-to-all-start) | async-done | bytes 1769504 | tf_op jit(solution)/shard_map/all_to_all | solution.py:1094
  (434 shorter events, 180.3 us)
Async XLA Ops:
  7.2 175.9 %all-gather.7.cloned.1.call-start = ((), (), s32[]{:S(2)}) async-start(), calls=%async_computation.6 | async-start | bytes 5898240 | tf_op jit(solution)/shard_map/all_gather | solution.py:1182
  13.5 33.3 %collective-permute-start.8 = (bf16[320,1024]{1,0:T(8,128)(2,1)}, bf16[320,1024]{1,0:T(8,128)(2,1)}, u32[]{:S(2)}, u32[]{:S(2)}) collective-permute-start(bf16[320,1024]{1,0:T(8,128)(2,1)} %bitcast.285), channel_id=1, source_target_pairs={{0,4},{4,0},{8,12},{12,8},{16,20},{20,16},{24,28},{28,24},{1,5},{5... | collective-permute-start | bytes 1966088 | tf_op jit(solution)/shard_map/ppermute | solution.py:506
  25.8 21.4 %collective-permute-start.7 = (bf16[2,3,3,96,256]{4,3,2,1,0:T(8,128)(2,1)S(1)}, bf16[2,3,3,96,256]{4,3,2,1,0:T(8,128)(2,1)S(1)}, u32[]{:S(2)}, u32[]{:S(2)}) collective-permute-start(bf16[2,3,3,96,256]{4,3,2,1,0:T(8,128)(2,1)S(1)} %get-tuple-element.222), channel_id=1, source_target_pairs={{0,2},{1,3},{2,0},{3,1},{4,6},{5,7},{6,4},{7,5},{8,10},{9,11},{10,... | collective-permute-start | bytes 2654216 | tf_op jit(solution)/shard_map/ppermute | solution.py:510
  27.4 19.3 %collective-permute-start.3 = (bf16[1536,128]{1,0:T(8,128)(2,1)}, bf16[1536,128]{1,0:T(8,128)(2,1)}, u32[]{:S(2)}, u32[]{:S(2)}) collective-permute-start(bf16[1536,128]{1,0:T(8,128)(2,1)} %pad_maximum_fusion.17), channel_id=1, source_target_pairs={{0,8},{4,12},{8,0},{12,4},{16,24},{20,28},{24,16},{28,20},{1,9},{5... | collective-permute-start | bytes 1179656 | tf_op jit(solution)/shard_map/ppermute | solution.py:518
  29.1 17.7 %collective-permute-start.4 = (bf16[1536,128]{1,0:T(8,128)(2,1)}, bf16[1536,128]{1,0:T(8,128)(2,1)}, u32[]{:S(2)}, u32[]{:S(2)}) collective-permute-start(bf16[1536,128]{1,0:T(8,128)(2,1)} %pad_maximum_fusion.17), channel_id=1, source_target_pairs={{0,24},{4,28},{8,16},{12,20},{16,8},{20,12},{24,0},{28,4},{1,25},{... | collective-permute-start | bytes 1179656 | tf_op jit(solution)/shard_map/ppermute | solution.py:522
  56.4 20.3 %collective-permute-start.13 = (bf16[1024,128]{1,0:T(8,128)(2,1)S(1)}, bf16[1024,128]{1,0:T(8,128)(2,1)}, u32[]{:S(2)}, u32[]{:S(2)}) collective-permute-start(bf16[1024,128]{1,0:T(8,128)(2,1)S(1)} %slice.244), channel_id=1, source_target_pairs={{0,4},{4,0},{8,12},{12,8},{16,20},{20,16},{24,28},{28,24},{1,5},{5... | collective-permute-start | bytes 786440 | tf_op jit(solution)/shard_map/ppermute | solution.py:506
  57.0 19.8 %collective-permute-start.9 = (bf16[1024,128]{1,0:T(8,128)(2,1)S(1)}, bf16[1024,128]{1,0:T(8,128)(2,1)}, u32[]{:S(2)}, u32[]{:S(2)}) collective-permute-start(bf16[1024,128]{1,0:T(8,128)(2,1)S(1)} %slice.244), channel_id=1, source_target_pairs={{0,8},{4,12},{8,0},{12,4},{16,24},{20,28},{24,16},{28,20},{1,9},{5... | collective-permute-start | bytes 786440 | tf_op jit(solution)/shard_map/ppermute | solution.py:518
  58.5 18.2 %collective-permute-start.11 = (bf16[2,1040,128]{2,1,0:T(8,128)(2,1)S(1)}, bf16[2,1040,128]{2,1,0:T(8,128)(2,1)}, u32[]{:S(2)}, u32[]{:S(2)}) collective-permute-start(bf16[2,1040,128]{2,1,0:T(8,128)(2,1)S(1)} %pad_maximum_fusion.11), channel_id=1, source_target_pairs={{0,2},{1,3},{2,0},{3,1},{4,6},{5,7},{6,4},{7,5},{8,10},{9,11},{10,... | collective-permute-start | bytes 1597448 | tf_op jit(solution)/shard_map/ppermute | solution.py:510
  81.4 18.3 %collective-permute-start.19 = (bf16[320,1024]{1,0:T(8,128)(2,1)}, bf16[320,1024]{1,0:T(8,128)(2,1)}, u32[]{:S(2)}, u32[]{:S(2)}) collective-permute-start(bf16[320,1024]{1,0:T(8,128)(2,1)} %collective-permute-done.8.refs_15_), channel_id=1, source_target_pairs={{0,1},{1,0},{2,3},{3,2},{4,5},{5,4},{6,7},{7,6},{8,9},{9,8},{10,11... | collective-permute-start | bytes 1966088 | tf_op jit(solution)/shard_map/ppermute | solution.py:514
  81.5 18.2 %collective-permute-start.18 = (bf16[1024,128]{1,0:T(8,128)(2,1)}, bf16[1024,128]{1,0:T(8,128)(2,1)}, u32[]{:S(2)}, u32[]{:S(2)}) collective-permute-start(bf16[1024,128]{1,0:T(8,128)(2,1)} %collective-permute-done.9), channel_id=1, source_target_pairs={{0,2},{1,3},{2,0},{3,1},{4,6},{5,7},{6,4},{7,5},{8,10},{9,11},{10,... | collective-permute-start | bytes 786440 | tf_op jit(solution)/shard_map/ppermute | solution.py:510
  90.1 150.7 %all-gather.5.cloned.1.call-start = ((), (), s32[]{:S(2)}) async-start(), calls=%async_computation.5 | async-start | bytes 2949120 | tf_op jit(solution)/shard_map/all_gather | solution.py:1182
  104.8 20.8 %collective-permute-start.23 = (bf16[320,1024]{1,0:T(8,128)(2,1)S(1)}, bf16[320,1024]{1,0:T(8,128)(2,1)S(1)}, u32[]{:S(2)}, u32[]{:S(2)}) collective-permute-start(bf16[320,1024]{1,0:T(8,128)(2,1)S(1)} %bitcast.288), channel_id=1, source_target_pairs={{0,2},{1,3},{2,0},{3,1},{4,6},{5,7},{6,4},{7,5},{8,10},{9,11},{10,... | collective-permute-start | bytes 1966088 | tf_op jit(solution)/shard_map/ppermute | solution.py:510
  106.1 19.5 %collective-permute-start.24 = (bf16[320,1024]{1,0:T(8,128)(2,1)S(1)}, bf16[320,1024]{1,0:T(8,128)(2,1)}, u32[]{:S(2)}, u32[]{:S(2)}) collective-permute-start(bf16[320,1024]{1,0:T(8,128)(2,1)S(1)} %bitcast.289), channel_id=1, source_target_pairs={{0,1},{1,0},{2,3},{3,2},{4,5},{5,4},{6,7},{7,6},{8,9},{9,8},{10,11... | collective-permute-start | bytes 1966088 | tf_op jit(solution)/shard_map/ppermute | solution.py:514
  107.8 17.8 %collective-permute-start.22 = (bf16[2,1024,128]{2,1,0:T(8,128)(2,1)S(1)}, bf16[2,1024,128]{2,1,0:T(8,128)(2,1)S(1)}, u32[]{:S(2)}, u32[]{:S(2)}) collective-permute-start(bf16[2,1024,128]{2,1,0:T(8,128)(2,1)S(1)} %pad_maximum_fusion.16), channel_id=1, source_target_pairs={{0,4},{4,0},{8,12},{12,8},{16,20},{20,16},{24,28},{28,24},{1,5},{5... | collective-permute-start | bytes 1572872 | tf_op jit(solution)/shard_map/ppermute | solution.py:506
  182.0 159.3 %reduce-scatter.3.cloned.1.call-start = ((), (), s32[]{:S(2)}) async-start(), calls=%async_computation.3 | async-start | bytes 5898240 | tf_op jit(solution)/shard_map/reduce_scatter | solution.py:1213
  240.8 150.8 %reduce-scatter.5.cloned.1.call-start = ((), (), s32[]{:S(2)}) async-start(), calls=%async_computation.4 | async-start | bytes 2949120 | tf_op jit(solution)/shard_map/reduce_scatter | solution.py:1213
  307.8 33.2 %collective-permute-start.46 = (bf16[160,1024]{1,0:T(8,128)(2,1)S(1)}, bf16[160,1024]{1,0:T(8,128)(2,1)S(1)}, u32[]{:S(2)}, u32[]{:S(2)}) collective-permute-start(bf16[160,1024]{1,0:T(8,128)(2,1)S(1)} %get-tuple-element.356), channel_id=1, source_target_pairs={{0,2},{1,3},{2,0},{3,1},{4,6},{5,7},{6,4},{7,5},{8,10},{9,11},{10,... | collective-permute-start | bytes 983048 | tf_op jit(solution)/shard_map/ppermute | solution.py:510
  308.6 32.3 %collective-permute-start.47 = (bf16[160,1024]{1,0:T(8,128)(2,1)S(1)}, bf16[160,1024]{1,0:T(8,128)(2,1)S(1)}, u32[]{:S(2)}, u32[]{:S(2)}) collective-permute-start(bf16[160,1024]{1,0:T(8,128)(2,1)S(1)} %get-tuple-element.357), channel_id=1, source_target_pairs={{0,4},{4,0},{8,12},{12,8},{16,20},{20,16},{24,28},{28,24},{1,5},{5... | collective-permute-start | bytes 983048 | tf_op jit(solution)/shard_map/ppermute | solution.py:506
  340.9 18.3 %collective-permute-start.50 = (bf16[2,4,256,512]{3,2,1,0:T(8,128)(2,1)}, bf16[2,4,256,512]{3,2,1,0:T(8,128)(2,1)S(1)}, u32[]{:S(2)}, u32[]{:S(2)}) collective-permute-start(bf16[2,4,256,512]{3,2,1,0:T(8,128)(2,1)} %get-tuple-element.374), channel_id=1, source_target_pairs={{0,1},{1,0},{2,3},{3,2},{4,5},{5,4},{6,7},{7,6},{8,9},{9,8},{10,11... | collective-permute-start | bytes 6291464 | tf_op jit(solution)/shard_map/ppermute | solution.py:514
  341.4 17.7 %collective-permute-start.48 = (bf16[320,1024]{1,0:T(8,128)(2,1)S(1)}, bf16[320,1024]{1,0:T(8,128)(2,1)S(1)}, u32[]{:S(2)}, u32[]{:S(2)}) collective-permute-start(bf16[320,1024]{1,0:T(8,128)(2,1)S(1)} %pad_maximum_fusion.9), channel_id=1, source_target_pairs={{0,2},{1,3},{2,0},{3,1},{4,6},{5,7},{6,4},{7,5},{8,10},{9,11},{10,... | collective-permute-start | bytes 1966088 | tf_op jit(solution)/shard_map/ppermute | solution.py:510
  359.0 19.3 %collective-permute-start.54 = (bf16[2,2,256,512]{3,2,1,0:T(8,128)(2,1)}, bf16[2,2,256,512]{3,2,1,0:T(8,128)(2,1)S(1)}, u32[]{:S(2)}, u32[]{:S(2)}) collective-permute-start(bf16[2,2,256,512]{3,2,1,0:T(8,128)(2,1)} %get-tuple-element.389), channel_id=1, source_target_pairs={{0,1},{1,0},{2,3},{3,2},{4,5},{5,4},{6,7},{7,6},{8,9},{9,8},{10,11... | collective-permute-start | bytes 3145736 | tf_op jit(solution)/shard_map/ppermute | solution.py:514
  360.7 17.7 %collective-permute-start.52 = (bf16[2,2,128,512]{3,2,0,1:T(8,128)(2,1)S(1)}, bf16[2,2,128,512]{3,2,0,1:T(8,128)(2,1)S(1)}, u32[]{:S(2)}, u32[]{:S(2)}) collective-permute-start(bf16[2,2,128,512]{3,2,0,1:T(8,128)(2,1)S(1)} %bitcast.261), channel_id=1, source_target_pairs={{0,2},{1,3},{2,0},{3,1},{4,6},{5,7},{6,4},{7,5},{8,10},{9,11},{10,... | collective-permute-start | bytes 1572872 | tf_op jit(solution)/shard_map/ppermute | solution.py:510
  396.4 21.0 %collective-permute-start.60 = (bf16[4,64,1024]{2,1,0:T(8,128)(2,1)}, bf16[4,64,1024]{2,1,0:T(8,128)(2,1)}, u32[]{:S(2)}, u32[]{:S(2)}) collective-permute-start(bf16[4,64,1024]{2,1,0:T(8,128)(2,1)} %get-tuple-element.410), channel_id=1, source_target_pairs={{0,4},{4,0},{8,12},{12,8},{16,20},{20,16},{24,28},{28,24},{1,5},{5... | collective-permute-start | bytes 1572872 | tf_op jit(solution)/shard_map/ppermute | solution.py:506
  441.3 25.7 %all-to-all-start = ((bf16[4,3,3,96,256]{4,3,2,1,0:T(8,128)(2,1)}), bf16[4,3,3,96,256]{4,3,2,1,0:T(8,128)(2,1)S(1)}, u32[]{:S(2)}, u32[]{:S(2)}) async-start(bf16[4,3,3,96,256]{4,3,2,1,0:T(8,128)(2,1)} %copy.156), calls=%async_computation.2 | async-start | bytes 3538944 | tf_op jit(solution)/shard_map/all_to_all | solution.py:1094
  (123 other events, 1096.0 us)
Sparse Core Ops, SparseCore 0:
  90.2 86.7 all-gather.6
  182.1 48.6 all-gather.4
  240.9 83.1 reduce-scatter.2
  326.2 48.5 reduce-scatter.4

commit v5 on v4

--- a/solution.py
+++ b/solution.py
@@ -939,7 +939,8 @@
                 continue
             k = rc * 5 + n
             copies.append(pltpu.make_async_copy(x_parts[k], x_scr.at[pl.ds(at, size)], sem.at[k, 0]))
-            copies.append(pltpu.make_async_copy(g_parts[k], g_scr.at[pl.ds(at, size)], sem.at[k, 1]))
+            src = g_parts[k].at[pl.ds(160 if n == 4 else 0, size)]
+            copies.append(pltpu.make_async_copy(src, g_scr.at[pl.ds(at, size)], sem.at[k, 1]))
     return copies
 
 
@@ -1188,21 +1189,21 @@
     c1, c3, *state = phase(move_c(t1), move_c(t3), *state)
     state = attend(((1, True), (3, False)), idx, all_low, windows, (t1, c1, t3, c3), state)
     *state, y2, g_x, g_c = phase(*state, move_y(s2), move_x(cot), move_c(cot))
-    t2, g_ya, g_xb, *state = phase(jnp.stack([s2, y2]), g_y[:160], g_x[160:], *state)
+    t2, *state = phase(jnp.stack([s2, y2]), *state)
     c2, *state = phase(move_c(t2), *state)
     state = attend(((2, True),), idx, all_low, windows, (t2, c2), state)
     marks_all = jnp.stack([t0[:, :, 1024:], c0[:, :, 1024:]]).reshape(2, 2, 2, 2048)[..., :960]
     marks_all = marks_all.transpose(0, 2, 1, 3).reshape(2560, 3).astype(F32)
     marks_all = jnp.pad(marks_all, ((0, 0), (0, 125)))
-    *state, g_a, g_b, g_cx, marks_all = phase(*state, move_x(g_ya), move_y(g_xb), move_c(g_x), marks_all)
+    *state, g_cx = phase(*state, move_c(g_x))
     probs, mixed, qkv, w_all = state
     hidden, normed = project_out(mixed, rows_own, gain_ffn_f, w_all)
-    hidden, normed, g_ca, g_cb = phase(hidden, normed, move_c(g_a), move_c(g_b))
-
-    x_x, x_y, x_c = phase(move_x(normed), move_y(normed), move_c(normed))
+    hidden, normed, g_xy = phase(hidden, normed, move_x(g_y))
+
+    x_x, x_y, x_c, g_cxy, marks_all = phase(move_x(normed), move_y(normed), move_c(normed), move_c(g_xy), marks_all)
     x_a, x_b, x_cx, x_cy = phase(move_x(x_y[:160]), move_y(x_x[160:]), move_c(x_x), move_c(x_y))
     x_parts = [normed, x_x, x_y, x_a, x_b, x_c, x_cx, x_cy, move_c(x_a), move_c(x_b)]
-    cot_parts = [cot, g_x, g_y, g_a, g_b, g_c, g_cx, g_cy, g_ca, g_cb]
+    cot_parts = [cot, g_x, g_y, g_xy, g_xy, g_c, g_cx, g_cy, g_cxy, g_cxy]
 
     def along_z(gw, dw):
         gw, dw = gw.astype(BF).reshape(-1, 2, 4, 96, 1024), dw.astype(BF).reshape(-1, 1, 4, 96, 1024)
@@ -1282,8 +1283,8 @@
     smalls = smalls + sm
     tot = here[0].astype(F32) + h_near.astype(F32) + f_opp.astype(F32)
     grad_tokens = finish(gp, gp_near, gp_opp, gn_all, rows_own, gain_attn_f, grad_hidden).reshape(1, 1, 320, 1024)
-    smalls = smalls + pair_z(smalls)
-    smalls = smalls + lax.ppermute(smalls, "ctx", [(i, i ^ 4) for i in range(8)])
+    sm_1, sm_2, sm_3 = [lax.ppermute(smalls, "ctx", [(i, i ^ n) for i in range(8)]) for n in (2, 4, 6)]
+    smalls = (smalls + sm_1) + (sm_2 + sm_3)
     mine = lax.dynamic_slice_in_dim(smalls, wt_index * 256, 256, 1)
     res_gain_attn, res_gain_ffn, res_router = mine[0], mine[1], mine[2:5].T
     res_bias = lax.dynamic_slice_in_dim(smalls[8:24, :BUCKETS], wt_index * 4, 4, 0).T

time: 482 us -> 477 us (0.990)
  waiting for transfers between devices: 97 us -> 90.8 us
    ppermute x1 -> x3, waiting for transfers between devices: 6.38 us -> 0.68 us  [local_fast(): lax.ppermute(smalls, 'ctx', [(i, i ^ n) for i in range(8)])]
    unnamed x140 -> x126, local copies, waits for them, and re-layouts: 12.5 us -> 10.3 us
    ppermute x19 -> x18, starting transfers between devices: 21.6 us -> 21.1 us  [move_y(): return lax.ppermute(v, 'ctx', SWAP_Y)]
    ppermute x19 -> x18, waiting for transfers between devices: 22.1 us -> 21.8 us  [move_y(): return lax.ppermute(v, 'ctx', SWAP_Y)]
    ppermute x7 -> x6, waiting for transfers between devices: 16.7 us -> 16.8 us  [pair_z(): return lax.ppermute(v, 'ctx', PAIR_Z)]
  transfers between devices with their start and end apart: 78 -> 77, of which waited for: 27 -> 29; matrix products, arithmetic and copies ran while one was open for 18% -> 18% of each run, Pallas kernels for 39% -> 39%
where the time goes in v5:
time: 477 us; the launch traced here: 471 us
  Pallas kernels  186 us (39%)
  waiting for transfers between devices  90.8 us (19%)
  starting transfers between devices  69.2 us (15%)
  other arithmetic  43.2 us (9%)
  local copies, waits for them, and re-layouts  38.1 us (8%)
  matrix products  28.1 us (6%)
  between operations  15.5 us (3%)
    pallas_call x2, Pallas kernels, expert_call(): pl.pallas_call(functools.partial(expert_kernel, group, last), grid=(total...  67.7 us
    pallas_call x3, Pallas kernels, attend_back(): pl.pallas_call(functools.partial(attend_back_kernel, gn_prev is None), gr...  54.3 us
    ppermute x19, waiting for transfers between devices, move_x(): return lax.ppermute(v, 'wt', SWAP_X)  39.6 us
    pallas_call x3, Pallas kernels, attend(): pl.pallas_call(functools.partial(attend_kernel, groups, prev is None), gr...  33.8 us
    dot_general x4, matrix products, dot_tn(): lax.dot_general(a, b, (((0,), (0,)), ((), ())), preferred_element_type=F32)  28.1 us
    ppermute x19, starting transfers between devices, move_x(): return lax.ppermute(v, 'wt', SWAP_X)  23.4 us
    ppermute x18, waiting for transfers between devices, move_y(): return lax.ppermute(v, 'ctx', SWAP_Y)  21.8 us
    ppermute x18, starting transfers between devices, move_y(): return lax.ppermute(v, 'ctx', SWAP_Y)  21.1 us
  transfers between devices with their start and end apart: 77, of which 29 were waited for; matrix products, arithmetic and copies ran while one was open for 18% of the time, Pallas kernels for 39%

profile of v5, /device:TPU:0, one launch (start us, length us, event | category | flops | bytes accessed | tf_op | source)
XLA Modules:
  0.0 470.9 jit_solution(1168947475130986988)
XLA Ops:
  31.2 5.6 %collective-permute-done.6 = bf16[1040,128]{1,0:T(8,128)(2,1)} collective-permute-done((bf16[1040,128]{1,0:T(8,128)(2,1)S(1)}, bf16[1040,128]{1,0:T(8,128)(2,1)}, u32[]{:S(2)}, u32[]{:S(2)}) %collective-permute-start.6) | collective-permute-done | bytes 266272 | tf_op jit(solution)/shard_map/ppermute | solution.py:506
  36.8 9.9 %collective-permute-done.3 = bf16[1536,128]{1,0:T(8,128)(2,1)} collective-permute-done((bf16[1536,128]{1,0:T(8,128)(2,1)}, bf16[1536,128]{1,0:T(8,128)(2,1)}, u32[]{:S(2)}, u32[]{:S(2)}) %collective-permute-start.3) | collective-permute-done | bytes 393248 | tf_op jit(solution)/shard_map/ppermute | solution.py:518
  66.7 10.0 %collective-permute-done.12 = bf16[1024,128]{1,0:T(8,128)(2,1)} collective-permute-done((bf16[1024,128]{1,0:T(8,128)(2,1)S(1)}, bf16[1024,128]{1,0:T(8,128)(2,1)}, u32[]{:S(2)}, u32[]{:S(2)}) %collective-permute-start.12) | collective-permute-done | bytes 262176 | tf_op jit(solution)/shard_map/ppermute | solution.py:510
  90.4 9.3 %shard_map.257 = (bf16[16,320,768]{2,1,0:T(8,128)(2,1)}, bf16[320,1024]{1,0:T(8,128)(2,1)}, bf16[8,768,384]{2,1,0:T(8,128)(2,1)}, bf16[8,1024,512]{2,1,0:T(8,128)(2,1)}) custom-call(s32[4]{0:T(128)} %pad_add_fusion.idx.refs_0_, bf16[768,1024]{1,0:T(8,128)(2,1)} %get-tuple-element.235.n_ref, f32[16,2,8,1024]{3,2,1,0:T(8,128)} %shard_map.255.w_ref, ...), custom_call_target="tpu_custom_call" | custom-call | flops 10000000000 | bytes 1000000 | tf_op jit(solution)/shard_map/pallas_call | solution.py:642
  109.5 15.3 %shard_map.258 = (bf16[16,320,768]{2,1,0:T(8,128)(2,1)}, bf16[320,1024]{1,0:T(8,128)(2,1)}, bf16[8,768,384]{2,1,0:T(8,128)(2,1)}, bf16[8,1024,512]{2,1,0:T(8,128)(2,1)}) custom-call(s32[4]{0:T(128)} %pad_add_fusion.idx.refs_0_, bf16[768,1024]{1,0:T(8,128)(2,1)} %get-tuple-element.235.n_ref, ...), custom_call_target="tpu_custom_call", output_to_operand_aliasing={{0}: (7, {}), {1}: (8, {}), {2}: (9, {}), {3}: (10, {})} | custom-call | flops 10000000000 | bytes 1000000 | tf_op jit(solution)/shard_map/pallas_call | solution.py:642
  128.8 9.3 %shard_map.259 = (bf16[16,320,768]{2,1,0:T(8,128)(2,1)}, bf16[320,1024]{1,0:T(8,128)(2,1)}, bf16[8,768,384]{2,1,0:T(8,128)(2,1)}, bf16[8,1024,512]{2,1,0:T(8,128)(2,1)}) custom-call(s32[4]{0:T(128)} %pad_add_fusion.idx.refs_0_, bf16[768,1024]{1,0:T(8,128)(2,1)} %get-tuple-element.235.n_ref, ...), custom_call_target="tpu_custom_call", output_to_operand_aliasing={{0}: (5, {}), {1}: (6, {}), {2}: (7, {}), {3}: (8, {})} | custom-call | flops 10000000000 | bytes 1000000 | tf_op jit(solution)/shard_map/pallas_call | solution.py:642
  138.2 6.9 %shard_map.260 = (f32[320,1024]{1,0:T(8,128)}, bf16[320,1024]{1,0:T(8,128)(2,1)}) custom-call(bf16[320,1024]{1,0:T(8,128)(2,1)} %get-tuple-element.297.m_ref, bf16[320,1024]{1,0:T(8,128)(2,1)} %bitcast.252, f32[1,1024]{1,0:T(1,128)} %convert.27.g_ref.gain_ref, bf16[8,1024,512]{2,1,0:T(8,128)(2,1)} %get-tuple-element.298.w_ref.wt_ref), custom_call_target="tpu_custom_call" | custom-call | flops 10000000000 | bytes 1000000 | tf_op jit(solution)/shard_map/pallas_call | solution.py:824
  152.2 10.2 %collective-permute-done.28.refs_4_ = bf16[320,1024]{1,0:T(8,128)(2,1)S(1)} collective-permute-done((bf16[320,1024]{1,0:T(8,128)(2,1)}, bf16[320,1024]{1,0:T(8,128)(2,1)S(1)}, u32[]{:S(2)}, u32[]{:S(2)}) %collective-permute-start.28) | collective-permute-done | bytes 655392 | tf_op jit(solution)/shard_map/ppermute | solution.py:510
  167.4 7.7 %collective-permute-done.32.refs_6_ = bf16[160,1024]{1,0:T(8,128)(2,1)S(1)} collective-permute-done((bf16[160,1024]{1,0:T(8,128)(2,1)S(1)}, bf16[160,1024]{1,0:T(8,128)(2,1)S(1)}, u32[]{:S(2)}, u32[]{:S(2)}) %collective-permute-start.32) | collective-permute-done | bytes 327712 | tf_op jit(solution)/shard_map/ppermute | solution.py:510
  178.0 37.2 %shard_map.261 = (bf16[2560,1024]{1,0:T(8,128)(2,1)}, bf16[2560,1024]{1,0:T(8,128)(2,1)}, bf16[2560,1536]{1,0:T(8,128)(2,1)}, bf16[2560,768]{1,0:T(8,128)(2,1)},...) custom-call(s32[4]{0:T(128)} %pad_add_fusion.idx.refs_0_, ...), custom_call_target="tpu_custom_call" | custom-call | flops 24999999488 | bytes 1000000 | tf_op jit(solution)/shard_map/pallas_call | solution.py:1075
  215.2 8.1 %convolution_convert_fusion.2 = bf16[768,1024]{1,0:T(8,128)(2,1)S(1)} fusion(bf16[2560,768]{1,0:T(8,128)(2,1)} %get-tuple-element.321, bf16[2560,1024]{1,0:T(8,128)(2,1)} %get-tuple-element.319.refs_4_), kind=kOutput, calls=%fused_computation.23 | convolution fusion | flops 4027318272 | bytes 10747904 | tf_op jit(solution)/shard_map/dot_general | solution.py:534
  223.3 9.3 %convolution_convert_fusion = bf16[1536,1024]{1,0:T(8,128)(2,1)S(1)} fusion(bf16[2560,1536]{1,0:T(8,128)(2,1)S(1)} %copy-done.58, bf16[2560,1024]{1,0:T(8,128)(2,1)S(1)} %copy-done.56), kind=kOutput, calls=%fused_computation.5 | convolution fusion | flops 8054636544 | bytes 16252928 | tf_op jit(solution)/shard_map/dot_general | solution.py:534
  235.5 30.5 %shard_map.262 = (bf16[1280,1024]{1,0:T(8,128)(2,1)}, bf16[1280,1024]{1,0:T(8,128)(2,1)}, bf16[1280,1024]{1,0:T(8,128)(2,1)}, bf16[1280,1024]{1,0:T(8,128)(2,1)}...) custom-call(s32[4]{0:T(128)} %pad_add_fusion.idx.refs_0_, bf16[4,4,1,3,96,256]{5,4,3,2,1,0:T(8,128)(2,1)} %bitcast.284, ...), custom_call_target="tpu_custom_call" | custom-call | flops 24999999488 | bytes 1000000 | tf_op jit(solution)/shard_map/pallas_call | solution.py:1075
  275.2 6.8 %convolution_convert_fusion.1 = bf16[768,1024]{1,0:T(8,128)(2,1)S(1)} fusion(bf16[2560,768]{1,0:T(8,128)(2,1)S(1)} %copy-done.57, bf16[2560,1024]{1,0:T(8,128)(2,1)} %get-tuple-element.318.refs_3_), kind=kOutput, calls=%fused_computation.22 | convolution fusion | flops 4027318272 | bytes 10747904 | tf_op jit(solution)/shard_map/dot_general | solution.py:534
  294.2 7.6 %collective-permute-done.42.b_ref = bf16[320,1024]{1,0:T(8,128)(2,1)} collective-permute-done((bf16[320,1024]{1,0:T(8,128)(2,1)}, bf16[320,1024]{1,0:T(8,128)(2,1)}, u32[]{:S(2)}, u32[]{:S(2)}) %collective-permute-start.42) | collective-permute-done | bytes 655392 | tf_op jit(solution)/shard_map/ppermute | solution.py:510
  304.5 7.9 %shard_map.263 = (f32[320,1024]{1,0:T(8,128)}, bf16[320,1024]{1,0:T(8,128)(2,1)}, bf16[320,1024]{1,0:T(8,128)(2,1)}, f32[8,1024]{1,0:T(8,128)}) custom-call(bf16[320,1024]{1,0:T(8,128)(2,1)} %slice.270.a_ref, bf16[320,1024]{1,0:T(8,128)(2,1)} %collective-permute-done.42.b_ref, bf16[320,1024]{1,0:T(8,128)(2,1)} %collective-permute-done.43.c_ref, ...), custom_call_target="tpu_custom_call" | custom-call | flops 10000000000 | bytes 1000000 | tf_op jit(solution)/shard_map/pallas_call | solution.py:797
  312.4 23.3 %shard_map.264 = (bf16[2,4,256,512]{3,2,1,0:T(8,128)(2,1)}, bf16[2,4,256,512]{3,2,1,0:T(8,128)(2,1)}, f32[768,1024]{1,0:T(8,128)}, f32[16,2,8,1024]{3,2,1,0:T(8,128)}) custom-call(s32[4]{0:T(128)} %pad_add_fusion.idx.refs_0_, bf16[768,1024]{1,0:T(8,128)(2,1)} %get-tuple-element.235.n_ref, bf16[16,320,768]{2,1,0:T(8,128)(2,1)} %get-tuple-element.350.p_ref, ...), custom_call_target="tpu_custom_call" | custom-call | flops 24999999488 | bytes 1000000 | tf_op jit(solution)/shard_map/pallas_call | solution.py:738
  338.2 15.4 %shard_map.265 = (bf16[2,2,256,512]{3,2,1,0:T(8,128)(2,1)}, bf16[2,2,256,512]{3,2,1,0:T(8,128)(2,1)}, f32[768,1024]{1,0:T(8,128)}, f32[16,2,8,1024]{3,2,1,0:T(8,128)}) custom-call(s32[4]{0:T(128)} %pad_add_fusion.idx.refs_0_, bf16[768,1024]{1,0:T(8,128)(2,1)} %get-tuple-element.235.n_ref, ...), custom_call_target="tpu_custom_call", output_to_operand_aliasing={{3}: (9, {})} | custom-call | flops 24999999488 | bytes 1000000 | tf_op jit(solution)/shard_map/pallas_call | solution.py:738
  357.5 15.6 %shard_map.266 = (bf16[2,2,256,512]{3,2,1,0:T(8,128)(2,1)}, bf16[2,2,256,512]{3,2,1,0:T(8,128)(2,1)}, f32[768,1024]{1,0:T(8,128)}, f32[16,2,8,1024]{3,2,1,0:T(8,128)}) custom-call(s32[4]{0:T(128)} %pad_add_fusion.idx.refs_0_, bf16[768,1024]{1,0:T(8,128)(2,1)} %get-tuple-element.235.n_ref, ...), custom_call_target="tpu_custom_call", output_to_operand_aliasing={{3}: (9, {})} | custom-call | flops 24999999488 | bytes 1000000 | tf_op jit(solution)/shard_map/pallas_call | solution.py:738
  376.6 4.9 %shard_map.267 = (f32[24,1024]{1,0:T(8,128)}, bf16[4,64,1024]{2,1,0:T(8,128)(2,1)}, bf16[4,64,1024]{2,1,0:T(8,128)(2,1)}) custom-call(s32[4]{0:T(128)} %pad_add_fusion.idx.refs_0_, s32[1,1920]{1,0:T(1,128)} %broadcast_in_dim.51.t_ref, f32[16,2,8,1024]{3,2,1,0:T(8,128)} %get-tuple-element.386.db_ref, f32[768,1024]{1,0:T(8,128)} %get-tuple-element.387.gn_ref, ...), custom_call_target="tpu_custom_call" | custom-call | flops 10000000000 | bytes 1000000 | tf_op jit(solution)/shard_map/pallas_call | solution.py:888
  394.8 5.4 %collective-permute-done.57 = bf16[256,512]{1,0:T(8,128)(2,1)S(1)} collective-permute-done((bf16[256,512]{1,0:T(8,128)(2,1)S(1)}, bf16[256,512]{1,0:T(8,128)(2,1)S(1)}, u32[]{:S(2)}, u32[]{:S(2)}) %collective-permute-start.57) | collective-permute-done | bytes 262176 | tf_op jit(solution)/shard_map/ppermute | solution.py:518
  403.5 8.6 %collective-permute-done.58 = bf16[4,64,1024]{2,1,0:T(8,128)(2,1)} collective-permute-done((bf16[4,64,1024]{2,1,0:T(8,128)(2,1)}, bf16[4,64,1024]{2,1,0:T(8,128)(2,1)}, u32[]{:S(2)}, u32[]{:S(2)}) %collective-permute-start.58) | collective-permute-done | bytes 524320 | tf_op jit(solution)/shard_map/ppermute | solution.py:506
  445.5 4.2 shard_map.268
  454.2 7.6 %all-to-all-done = bf16[4,3,3,96,256]{4,3,2,1,0:T(8,128)(2,1)S(1)} async-done(((bf16[4,3,3,96,256]{4,3,2,1,0:T(8,128)(2,1)}), bf16[4,3,3,96,256]{4,3,2,1,0:T(8,128)(2,1)S(1)}, u32[]{:S(2)}, u32[]{:S(2)}) %all-to-all-start) | async-done | bytes 1769504 | tf_op jit(solution)/shard_map/all_to_all | solution.py:1095
  (415 shorter events, 178.7 us)
Async XLA Ops:
  7.2 170.7 %all-gather.7.cloned.1.call-start = ((), (), s32[]{:S(2)}) async-start(), calls=%async_computation.6 | async-start | bytes 5898240 | tf_op jit(solution)/shard_map/all_gather | solution.py:1183
  13.5 33.3 %collective-permute-start.8 = (bf16[320,1024]{1,0:T(8,128)(2,1)}, bf16[320,1024]{1,0:T(8,128)(2,1)}, u32[]{:S(2)}, u32[]{:S(2)}) collective-permute-start(bf16[320,1024]{1,0:T(8,128)(2,1)} %bitcast.27.refs_13_.cot_ref), channel_id=1, source_target_pairs={{0,4},{4,0},{8,12},{12,8},{16,20},{20,16},{24,28},{28,24},{1,5},{5... | collective-permute-start | bytes 1966088 | tf_op jit(solution)/shard_map/ppermute | solution.py:506
  25.8 21.4 %collective-permute-start.7 = (bf16[2,3,3,96,256]{4,3,2,1,0:T(8,128)(2,1)S(1)}, bf16[2,3,3,96,256]{4,3,2,1,0:T(8,128)(2,1)S(1)}, u32[]{:S(2)}, u32[]{:S(2)}) collective-permute-start(bf16[2,3,3,96,256]{4,3,2,1,0:T(8,128)(2,1)S(1)} %get-tuple-element.218), channel_id=1, source_target_pairs={{0,2},{1,3},{2,0},{3,1},{4,6},{5,7},{6,4},{7,5},{8,10},{9,11},{10,... | collective-permute-start | bytes 2654216 | tf_op jit(solution)/shard_map/ppermute | solution.py:510
  27.4 19.3 %collective-permute-start.3 = (bf16[1536,128]{1,0:T(8,128)(2,1)}, bf16[1536,128]{1,0:T(8,128)(2,1)}, u32[]{:S(2)}, u32[]{:S(2)}) collective-permute-start(bf16[1536,128]{1,0:T(8,128)(2,1)} %pad_maximum_fusion.17), channel_id=1, source_target_pairs={{0,8},{4,12},{8,0},{12,4},{16,24},{20,28},{24,16},{28,20},{1,9},{5... | collective-permute-start | bytes 1179656 | tf_op jit(solution)/shard_map/ppermute | solution.py:518
  29.1 17.7 %collective-permute-start.4 = (bf16[1536,128]{1,0:T(8,128)(2,1)}, bf16[1536,128]{1,0:T(8,128)(2,1)}, u32[]{:S(2)}, u32[]{:S(2)}) collective-permute-start(bf16[1536,128]{1,0:T(8,128)(2,1)} %pad_maximum_fusion.17), channel_id=1, source_target_pairs={{0,24},{4,28},{8,16},{12,20},{16,8},{20,12},{24,0},{28,4},{1,25},{... | collective-permute-start | bytes 1179656 | tf_op jit(solution)/shard_map/ppermute | solution.py:522
  56.4 20.3 %collective-permute-start.13 = (bf16[1024,128]{1,0:T(8,128)(2,1)S(1)}, bf16[1024,128]{1,0:T(8,128)(2,1)}, u32[]{:S(2)}, u32[]{:S(2)}) collective-permute-start(bf16[1024,128]{1,0:T(8,128)(2,1)S(1)} %slice.238), channel_id=1, source_target_pairs={{0,4},{4,0},{8,12},{12,8},{16,20},{20,16},{24,28},{28,24},{1,5},{5... | collective-permute-start | bytes 786440 | tf_op jit(solution)/shard_map/ppermute | solution.py:506
  57.0 19.8 %collective-permute-start.9 = (bf16[1024,128]{1,0:T(8,128)(2,1)S(1)}, bf16[1024,128]{1,0:T(8,128)(2,1)}, u32[]{:S(2)}, u32[]{:S(2)}) collective-permute-start(bf16[1024,128]{1,0:T(8,128)(2,1)S(1)} %slice.238), channel_id=1, source_target_pairs={{0,8},{4,12},{8,0},{12,4},{16,24},{20,28},{24,16},{28,20},{1,9},{5... | collective-permute-start | bytes 786440 | tf_op jit(solution)/shard_map/ppermute | solution.py:518
  58.5 18.2 %collective-permute-start.11 = (bf16[2,1040,128]{2,1,0:T(8,128)(2,1)S(1)}, bf16[2,1040,128]{2,1,0:T(8,128)(2,1)}, u32[]{:S(2)}, u32[]{:S(2)}) collective-permute-start(bf16[2,1040,128]{2,1,0:T(8,128)(2,1)S(1)} %pad_maximum_fusion.11), channel_id=1, source_target_pairs={{0,2},{1,3},{2,0},{3,1},{4,6},{5,7},{6,4},{7,5},{8,10},{9,11},{10,... | collective-permute-start | bytes 1597448 | tf_op jit(solution)/shard_map/ppermute | solution.py:510
  81.4 18.3 %collective-permute-start.19 = (bf16[320,1024]{1,0:T(8,128)(2,1)}, bf16[320,1024]{1,0:T(8,128)(2,1)}, u32[]{:S(2)}, u32[]{:S(2)}) collective-permute-start(bf16[320,1024]{1,0:T(8,128)(2,1)} %collective-permute-done.8.refs_15_), channel_id=1, source_target_pairs={{0,1},{1,0},{2,3},{3,2},{4,5},{5,4},{6,7},{7,6},{8,9},{9,8},{10,11... | collective-permute-start | bytes 1966088 | tf_op jit(solution)/shard_map/ppermute | solution.py:514
  81.5 18.2 %collective-permute-start.18 = (bf16[1024,128]{1,0:T(8,128)(2,1)}, bf16[1024,128]{1,0:T(8,128)(2,1)}, u32[]{:S(2)}, u32[]{:S(2)}) collective-permute-start(bf16[1024,128]{1,0:T(8,128)(2,1)} %collective-permute-done.9), channel_id=1, source_target_pairs={{0,2},{1,3},{2,0},{3,1},{4,6},{5,7},{6,4},{7,5},{8,10},{9,11},{10,... | collective-permute-start | bytes 786440 | tf_op jit(solution)/shard_map/ppermute | solution.py:510
  90.1 145.3 %all-gather.5.cloned.1.call-start = ((), (), s32[]{:S(2)}) async-start(), calls=%async_computation.5 | async-start | bytes 2949120 | tf_op jit(solution)/shard_map/all_gather | solution.py:1183
  104.7 20.1 %collective-permute-start.23 = (bf16[320,1024]{1,0:T(8,128)(2,1)}, bf16[320,1024]{1,0:T(8,128)(2,1)}, u32[]{:S(2)}, u32[]{:S(2)}) collective-permute-start(bf16[320,1024]{1,0:T(8,128)(2,1)} %bitcast.27.refs_13_.cot_ref), channel_id=1, source_target_pairs={{0,2},{1,3},{2,0},{3,1},{4,6},{5,7},{6,4},{7,5},{8,10},{9,11},{10,... | collective-permute-start | bytes 1966088 | tf_op jit(solution)/shard_map/ppermute | solution.py:510
  106.0 18.8 %collective-permute-start.24 = (bf16[320,1024]{1,0:T(8,128)(2,1)}, bf16[320,1024]{1,0:T(8,128)(2,1)}, u32[]{:S(2)}, u32[]{:S(2)}) collective-permute-start(bf16[320,1024]{1,0:T(8,128)(2,1)} %bitcast.27.refs_13_.cot_ref), channel_id=1, source_target_pairs={{0,1},{1,0},{2,3},{3,2},{4,5},{5,4},{6,7},{7,6},{8,9},{9,8},{10,11... | collective-permute-start | bytes 1966088 | tf_op jit(solution)/shard_map/ppermute | solution.py:514
  106.0 18.8 %collective-permute-start.22 = (bf16[2,1024,128]{2,1,0:T(8,128)(2,1)S(1)}, bf16[2,1024,128]{2,1,0:T(8,128)(2,1)S(1)}, u32[]{:S(2)}, u32[]{:S(2)}) collective-permute-start(bf16[2,1024,128]{2,1,0:T(8,128)(2,1)S(1)} %pad_maximum_fusion.16), channel_id=1, source_target_pairs={{0,4},{4,0},{8,12},{12,8},{16,20},{20,16},{24,28},{28,24},{1,5},{5... | collective-permute-start | bytes 1572872 | tf_op jit(solution)/shard_map/ppermute | solution.py:506
  125.2 19.9 %collective-permute-start.27 = (bf16[320,1024]{1,0:T(8,128)(2,1)}, bf16[320,1024]{1,0:T(8,128)(2,1)}, u32[]{:S(2)}, u32[]{:S(2)}) collective-permute-start(bf16[320,1024]{1,0:T(8,128)(2,1)} %collective-permute-done.8.refs_15_), channel_id=1, source_target_pairs={{0,2},{1,3},{2,0},{3,1},{4,6},{5,7},{6,4},{7,5},{8,10},{9,11},{10,... | collective-permute-start | bytes 1966088 | tf_op jit(solution)/shard_map/ppermute | solution.py:510
  176.9 159.3 %reduce-scatter.3.cloned.1.call-start = ((), (), s32[]{:S(2)}) async-start(), calls=%async_computation.3 | async-start | bytes 5898240 | tf_op jit(solution)/shard_map/reduce_scatter | solution.py:1214
  235.4 150.9 %reduce-scatter.5.cloned.1.call-start = ((), (), s32[]{:S(2)}) async-start(), calls=%async_computation.4 | async-start | bytes 2949120 | tf_op jit(solution)/shard_map/reduce_scatter | solution.py:1214
  302.3 33.5 %collective-permute-start.44 = (bf16[160,1024]{1,0:T(8,128)(2,1)S(1)}, bf16[160,1024]{1,0:T(8,128)(2,1)S(1)}, u32[]{:S(2)}, u32[]{:S(2)}) collective-permute-start(bf16[160,1024]{1,0:T(8,128)(2,1)S(1)} %get-tuple-element.348), channel_id=1, source_target_pairs={{0,2},{1,3},{2,0},{3,1},{4,6},{5,7},{6,4},{7,5},{8,10},{9,11},{10,... | collective-permute-start | bytes 983048 | tf_op jit(solution)/shard_map/ppermute | solution.py:510
  303.5 32.3 %collective-permute-start.45 = (bf16[160,1024]{1,0:T(8,128)(2,1)S(1)}, bf16[160,1024]{1,0:T(8,128)(2,1)S(1)}, u32[]{:S(2)}, u32[]{:S(2)}) collective-permute-start(bf16[160,1024]{1,0:T(8,128)(2,1)S(1)} %get-tuple-element.349), channel_id=1, source_target_pairs={{0,4},{4,0},{8,12},{12,8},{16,20},{20,16},{24,28},{28,24},{1,5},{5... | collective-permute-start | bytes 983048 | tf_op jit(solution)/shard_map/ppermute | solution.py:506
  335.7 18.0 %collective-permute-start.48 = (bf16[2,4,256,512]{3,2,1,0:T(8,128)(2,1)}, bf16[2,4,256,512]{3,2,1,0:T(8,128)(2,1)S(1)}, u32[]{:S(2)}, u32[]{:S(2)}) collective-permute-start(bf16[2,4,256,512]{3,2,1,0:T(8,128)(2,1)} %get-tuple-element.366), channel_id=1, source_target_pairs={{0,1},{1,0},{2,3},{3,2},{4,5},{5,4},{6,7},{7,6},{8,9},{9,8},{10,11... | collective-permute-start | bytes 6291464 | tf_op jit(solution)/shard_map/ppermute | solution.py:514
  353.7 19.5 %collective-permute-start.52 = (bf16[2,2,256,512]{3,2,1,0:T(8,128)(2,1)}, bf16[2,2,256,512]{3,2,1,0:T(8,128)(2,1)S(1)}, u32[]{:S(2)}, u32[]{:S(2)}) collective-permute-start(bf16[2,2,256,512]{3,2,1,0:T(8,128)(2,1)} %get-tuple-element.381), channel_id=1, source_target_pairs={{0,1},{1,0},{2,3},{3,2},{4,5},{5,4},{6,7},{7,6},{8,9},{9,8},{10,11... | collective-permute-start | bytes 3145736 | tf_op jit(solution)/shard_map/ppermute | solution.py:514
  355.4 17.8 %collective-permute-start.50 = (bf16[2,2,128,512]{3,2,0,1:T(8,128)(2,1)S(1)}, bf16[2,2,128,512]{3,2,0,1:T(8,128)(2,1)S(1)}, u32[]{:S(2)}, u32[]{:S(2)}) collective-permute-start(bf16[2,2,128,512]{3,2,0,1:T(8,128)(2,1)S(1)} %bitcast.261), channel_id=1, source_target_pairs={{0,2},{1,3},{2,0},{3,1},{4,6},{5,7},{6,4},{7,5},{8,10},{9,11},{10,... | collective-permute-start | bytes 1572872 | tf_op jit(solution)/shard_map/ppermute | solution.py:510
  391.3 20.8 %collective-permute-start.58 = (bf16[4,64,1024]{2,1,0:T(8,128)(2,1)}, bf16[4,64,1024]{2,1,0:T(8,128)(2,1)}, u32[]{:S(2)}, u32[]{:S(2)}) collective-permute-start(bf16[4,64,1024]{2,1,0:T(8,128)(2,1)} %get-tuple-element.402), channel_id=1, source_target_pairs={{0,4},{4,0},{8,12},{12,8},{16,20},{20,16},{24,28},{28,24},{1,5},{5... | collective-permute-start | bytes 1572872 | tf_op jit(solution)/shard_map/ppermute | solution.py:506
  436.1 25.7 %all-to-all-start = ((bf16[4,3,3,96,256]{4,3,2,1,0:T(8,128)(2,1)}), bf16[4,3,3,96,256]{4,3,2,1,0:T(8,128)(2,1)S(1)}, u32[]{:S(2)}, u32[]{:S(2)}) async-start(bf16[4,3,3,96,256]{4,3,2,1,0:T(8,128)(2,1)} %copy.156), calls=%async_computation.2 | async-start | bytes 3538944 | tf_op jit(solution)/shard_map/all_to_all | solution.py:1095
  (115 other events, 1075.4 us)
Sparse Core Ops, SparseCore 0:
  90.3 86.7 all-gather.6
  178.6 48.9 all-gather.4
  235.5 83.6 reduce-scatter.2
  321.3 48.5 reduce-scatter.4

commit v6 on v5

--- a/solution.py
+++ b/solution.py
@@ -667,9 +667,11 @@
     )(idx, normed, windows, *pieces, *([] if prev is None else prev))
 
 
-def attend_back_kernel(first, idx, n_ref, p_ref, qkv_ref, wt_ref, g_ref, m_ref, gl_ref, *refs):
+def attend_back_kernel(first, final, idx, n_ref, p_ref, qkv_ref, wt_ref, g_ref, m_ref, gl_ref, *refs):
     if not first:
         gn_prev, refs = refs[0], refs[2:]
+    if final:
+        gp_ref, refs = refs[4], refs[:4] + refs[5:]
     keep_ref, send_ref, gn_ref, db_ref, dt_ref, qs_ref = refs
     z, y, x, c = idx[0], idx[1], idx[2], idx[3]
     own = pl.ds(pl.multiple_of((z * 2 + y) * 64, 64), 64)
@@ -730,13 +732,23 @@
     def _():
         gn_ref[...] += gn
 
+    if final:
+
+        @pl.when(pl.program_id(0) == pl.num_programs(0) - 1)
+        def _():
+            for sz in range(4):
+                for ry in range(2):
+                    rows = pl.ds(pl.multiple_of(((z ^ sz) * 2 + (y ^ ry)) * 64, 64), 64)
+                    gp_ref[sz, ry] = gn_ref[rows, :].astype(BF)
+
 
 def attend_back(base, count, idx, normed, p, qkv, wt, g, mixed, g_low, gn_prev, db_prev):
     rows, keys = p.shape[1], p.shape[2]
+    final = base == 0
     at = lambda i, d: (i + base) ^ (d[0] * 2 + d[1])
     whole = pl.BlockSpec((keys, 1024), lambda i, d: (0, 0))
     return pl.pallas_call(
-        functools.partial(attend_back_kernel, gn_prev is None),
+        functools.partial(attend_back_kernel, gn_prev is None, final),
         grid_spec=pltpu.PrefetchScalarGridSpec(
             num_scalar_prefetch=1,
             grid=(count,),
@@ -755,7 +767,8 @@
                 pl.BlockSpec((2, 1, 256, 512), lambda i, d: (0, i, 0, 0)),
                 whole,
                 pl.BlockSpec((2, 2, 8, 1024), lambda i, d: (at(i, d), 0, 0, 0)),
-            ),
+            )
+            + ((pl.BlockSpec((4, 2, 64, 1024), lambda i, d: (0, 0, 0, 0)),) if final else ()),
             scratch_shapes=[pltpu.VMEM((keys, 384), BF), pltpu.VMEM((keys, 128), BF)],
         ),
         out_shape=(
@@ -763,7 +776,8 @@
             jax.ShapeDtypeStruct((2, count, 256, 512), BF),
             jax.ShapeDtypeStruct((keys, 1024), F32),
             jax.ShapeDtypeStruct((16, 2, 8, 1024), F32),
-        ),
+        )
+        + ((jax.ShapeDtypeStruct((4, 2, 64, 1024), BF),) if final else ()),
         input_output_aliases={} if gn_prev is None else {9: 3},
         compiler_params=params(),
         cost_estimate=COST_E,
@@ -855,7 +869,7 @@
     )(idx, table_rev, bias_f)
 
 
-def pack_kernel(idx, t_ref, db_ref, gn_ref, src_ref, gf_ref, r_ref, small_ref, keep_ref, send_ref):
+def pack_kernel(idx, t_ref, db_ref, gn_ref, src_ref, gf_ref, r_ref, small_ref):
     z, y = idx[0], idx[1]
 
     def gather(n):
@@ -877,10 +891,6 @@
     small_ref[1:2, :] = gf_ref[0:1, :]
     small_ref[2:5, :] = r_ref[0:3, :]
     small_ref[8:24, 0:BUCKETS] = bias
-    for sz in range(4):
-        at = lambda yy: pl.ds(pl.multiple_of(((z ^ sz) * 2 + yy) * 64, 64), 64)
-        keep_ref[sz] = gn_ref[at(y), :].astype(BF)
-        send_ref[sz] = gn_ref[at(y ^ 1), :].astype(BF)
 
 
 def pack(idx, table_rev, dbias, gn, src, gain_ffn_part, router_part):
@@ -888,20 +898,16 @@
     return pl.pallas_call(
         pack_kernel,
         in_specs=[SMEM] + [whole] * 6,
-        out_specs=(whole,) * 3,
-        out_shape=(
-            jax.ShapeDtypeStruct((24, 1024), F32),
-            jax.ShapeDtypeStruct((4, 64, 1024), BF),
-            jax.ShapeDtypeStruct((4, 64, 1024), BF),
-        ),
+        out_specs=whole,
+        out_shape=jax.ShapeDtypeStruct((24, 1024), F32),
         compiler_params=params(),
         cost_estimate=COST_S,
     )(idx, table_rev, dbias, gn, src, gain_ffn_part, router_part)
 
 
-def final_kernel(p_ref, near_ref, opp_ref, gn_ref, src_ref, gain_ref, gh_ref, o_ref):
+def final_kernel(p_ref, q_ref, gn_ref, src_ref, gain_ref, gh_ref, o_ref):
     f = lambda t: t.astype(F32)
-    own = f(p_ref[0]) + f(near_ref[...]) + f(opp_ref[...])
+    own = f(p_ref[...]) + f(q_ref[...])
     grad = jnp.concatenate([own, gn_ref[512:, :]], axis=0) * gain_ref[...]
     src = f(src_ref[...])
     scale = lax.rsqrt(jnp.mean(src * src, axis=-1, keepdims=True) + epsilon)
@@ -910,16 +916,16 @@
     o_ref[...] = (gh_ref[...] + back).astype(BF)
 
 
-def finish(parts, near, opp, gn, src, gain, grad_hidden):
+def finish(own, other, gn, src, gain, grad_hidden):
     whole = pl.BlockSpec(memory_space=pltpu.VMEM)
     return pl.pallas_call(
         final_kernel,
-        in_specs=[whole] * 7,
+        in_specs=[whole] * 6,
         out_specs=whole,
         out_shape=jax.ShapeDtypeStruct((320, 1024), BF),
         compiler_params=params(),
         cost_estimate=COST_S,
-    )(parts, near, opp, gn, src, gain[None], grad_hidden)
+    )(own, other, gn, src, gain[None], grad_hidden)
 
 
 def add_low(a, b):
@@ -1256,33 +1262,34 @@
 
     fa, fb = cut_rows(add_low(keep_f, got).reshape(2, 2, 2, 256, 512))
     fa0, fa1, fb0, fb1, gn = phase(fa[0], fa[1], fb[:, :, 0], fb[:, :, 1], gn)
-    keep_h, send_h, gn_all, dbias = back_of(0, 2, gn, dbias)
-    fx, fy, got_n, gn_all = phase(move_x(fa1), move_y(fb1), move_c(send_n), gn_all)
+    keep_h, send_h, gn_all, dbias, gp = back_of(0, 2, gn, dbias)
+    fx, fy, got_n, gn_all, gp = phase(move_x(fa1), move_y(fb1), move_c(send_n), gn_all, gp)
     fa, fb = add_low(fa0, fx), add_low(fb0, fy)
-    packed = pack(idx, table_rev, dbias, gn_all, source_all, gain_ffn_part, router_part)
-    got, fy, fx, smalls, gp_keep, gp_send = phase(move_c(send_h), move_y(fa[:, 1]), move_x(fb[1]), *packed)
+    smalls = pack(idx, table_rev, dbias, gn_all, source_all, gain_ffn_part, router_part)
+    got, fy, fx, gp_cross, smalls = phase(
+        move_c(send_h), move_y(fa[:, 1]), move_x(fb[1]), pair_z(gp[2]), smalls
+    )
     fy, bulk[1] = phase(fy, bulk[1])
     far = jnp.concatenate([add_low(fa[:, 0], fy), add_low(fb[0], fx)], axis=1)
     block = lambda t: t.reshape(2, 1, 2, 256, 512)
     h = jnp.concatenate([add_low(block(keep_h), block(got)), add_low(block(keep_n), block(got_n))], axis=1)
     ha, hb = cut_rows(h)
-    hx, hy, f_cross, gp_got, sm = phase(
-        move_x(ha[1]), move_y(hb[:, :, 1]), pair_z(far[0]), move_y(gp_send), move_c(smalls)
+    hx, hy, f_cross, gp_opp, gp_near, sm = phase(
+        move_x(ha[1]), move_y(hb[:, :, 1]), pair_z(far[0]), flip_z(add_low(gp[3], gp_cross)), pair_z(gp[1]),
+        move_c(smalls),
     )
     ha, hb = add_low(ha[0], hx), add_low(hb[:, :, 0], hy)
-    gp = add_low(gp_keep, gp_got)
+    gp = (gp[0].astype(F32) + gp_near.astype(F32) + gp_opp.astype(F32)).astype(BF)
     smalls = smalls + sm
-    hy, hx, f_opp, gp_cross, sm = phase(
-        move_y(ha[:, 1]), move_x(hb[1]), flip_z(add_low(far[1], f_cross)), pair_z(gp[2]), move_x(smalls)
+    hy, hx, f_opp, gp_y, sm = phase(
+        move_y(ha[:, 1]), move_x(hb[1]), flip_z(add_low(far[1], f_cross)), move_y(gp[1]), move_x(smalls)
     )
     here = jnp.concatenate([add_low(ha[:, 0], hy), add_low(hb[0], hx)], axis=1)
     smalls = smalls + sm
-    h_near, gp_opp, gp_near, sm = phase(
-        pair_z(here[1]), flip_z(add_low(gp[3], gp_cross)), pair_z(gp[1]), move_y(smalls)
-    )
+    h_near, sm = phase(pair_z(here[1]), move_y(smalls))
     smalls = smalls + sm
     tot = here[0].astype(F32) + h_near.astype(F32) + f_opp.astype(F32)
-    grad_tokens = finish(gp, gp_near, gp_opp, gn_all, rows_own, gain_attn_f, grad_hidden).reshape(1, 1, 320, 1024)
+    grad_tokens = finish(gp[0], gp_y, gn_all, rows_own, gain_attn_f, grad_hidden).reshape(1, 1, 320, 1024)
     sm_1, sm_2, sm_3 = [lax.ppermute(smalls, "ctx", [(i, i ^ n) for i in range(8)]) for n in (2, 4, 6)]
     smalls = (smalls + sm_1) + (sm_2 + sm_3)
     mine = lax.dynamic_slice_in_dim(smalls, wt_index * 256, 256, 1)

time: 477 us -> 465 us (0.975)
  waiting for transfers between devices: 90.8 us -> 77 us
    ppermute x18, waiting for transfers between devices: 21.8 us -> 10.1 us  [move_y(): return lax.ppermute(v, 'ctx', SWAP_Y)]
    all_to_all x1, waiting for transfers between devices: 7.58 us -> 0.01 us  [trade_wt(): return lax.all_to_all(v, 'wt', 0, 0, tiled=True)]
    unnamed x126 -> x112, local copies, waits for them, and re-layouts: 10.3 us -> 8.61 us
    convert_element_type x20 -> x19, other arithmetic: 13.5 us -> 12.2 us  [add_low(): return (a.astype(F32) + b.astype(F32)).astype(BF)]
  transfers between devices with their start and end apart: 77 -> 77, of which waited for: 29 -> 23; matrix products, arithmetic and copies ran while one was open for 18% -> 19% of each run, Pallas kernels for 39% -> 40%
where the time goes in v6:
time: 465 us; the launch traced here: 459 us
  Pallas kernels  185 us (40%)
  waiting for transfers between devices  77 us (17%)
  starting transfers between devices  70.3 us (15%)
  other arithmetic  42.3 us (9%)
  local copies, waits for them, and re-layouts  38.6 us (8%)
  matrix products  29.6 us (6%)
  between operations  15.6 us (3%)
    pallas_call x2, Pallas kernels, expert_call(): pl.pallas_call(functools.partial(expert_kernel, group, last), grid=(total...  67.5 us
    pallas_call x3, Pallas kernels, attend_back(): pl.pallas_call(functools.partial(attend_back_kernel, gn_prev is None, fin...  54.8 us
    ppermute x19, waiting for transfers between devices, move_x(): return lax.ppermute(v, 'wt', SWAP_X)  38.6 us
    pallas_call x3, Pallas kernels, attend(): pl.pallas_call(functools.partial(attend_kernel, groups, prev is None), gr...  33.9 us
    dot_general x4, matrix products, dot_tn(): lax.dot_general(a, b, (((0,), (0,)), ((), ())), preferred_element_type=F32)  29.6 us
    ppermute x19, starting transfers between devices, move_x(): return lax.ppermute(v, 'wt', SWAP_X)  23.5 us
    ppermute x18, starting transfers between devices, move_y(): return lax.ppermute(v, 'ctx', SWAP_Y)  21.1 us
    ppermute x6, waiting for transfers between devices, pair_z(): return lax.ppermute(v, 'ctx', PAIR_Z)  20.3 us
  transfers between devices with their start and end apart: 77, of which 23 were waited for; matrix products, arithmetic and copies ran while one was open for 19% of the time, Pallas kernels for 40%

profile of v6, /device:TPU:0, one launch (start us, length us, event | category | flops | bytes accessed | tf_op | source)
XLA Modules:
  0.0 458.7 jit_solution(16823730086289936773)
XLA Ops:
  31.1 5.7 %collective-permute-done.6 = bf16[1040,128]{1,0:T(8,128)(2,1)} collective-permute-done((bf16[1040,128]{1,0:T(8,128)(2,1)S(1)}, bf16[1040,128]{1,0:T(8,128)(2,1)}, u32[]{:S(2)}, u32[]{:S(2)}) %collective-permute-start.6) | collective-permute-done | bytes 266272 | tf_op jit(solution)/shard_map/ppermute | solution.py:506
  36.8 9.9 %collective-permute-done.3 = bf16[1536,128]{1,0:T(8,128)(2,1)} collective-permute-done((bf16[1536,128]{1,0:T(8,128)(2,1)}, bf16[1536,128]{1,0:T(8,128)(2,1)}, u32[]{:S(2)}, u32[]{:S(2)}) %collective-permute-start.3) | collective-permute-done | bytes 393248 | tf_op jit(solution)/shard_map/ppermute | solution.py:518
  66.7 10.0 %collective-permute-done.12 = bf16[1024,128]{1,0:T(8,128)(2,1)} collective-permute-done((bf16[1024,128]{1,0:T(8,128)(2,1)S(1)}, bf16[1024,128]{1,0:T(8,128)(2,1)}, u32[]{:S(2)}, u32[]{:S(2)}) %collective-permute-start.12) | collective-permute-done | bytes 262176 | tf_op jit(solution)/shard_map/ppermute | solution.py:510
  90.3 9.3 %shard_map.257 = (bf16[16,320,768]{2,1,0:T(8,128)(2,1)}, bf16[320,1024]{1,0:T(8,128)(2,1)}, bf16[8,768,384]{2,1,0:T(8,128)(2,1)}, bf16[8,1024,512]{2,1,0:T(8,128)(2,1)}) custom-call(s32[4]{0:T(128)} %pad_add_fusion.idx.refs_0_, bf16[768,1024]{1,0:T(8,128)(2,1)} %get-tuple-element.232.n_ref, f32[16,2,8,1024]{3,2,1,0:T(8,128)} %shard_map.255.w_ref, ...), custom_call_target="tpu_custom_call" | custom-call | flops 10000000000 | bytes 1000000 | tf_op jit(solution)/shard_map/pallas_call | solution.py:642
  109.5 15.2 %shard_map.258 = (bf16[16,320,768]{2,1,0:T(8,128)(2,1)}, bf16[320,1024]{1,0:T(8,128)(2,1)}, bf16[8,768,384]{2,1,0:T(8,128)(2,1)}, bf16[8,1024,512]{2,1,0:T(8,128)(2,1)}) custom-call(s32[4]{0:T(128)} %pad_add_fusion.idx.refs_0_, bf16[768,1024]{1,0:T(8,128)(2,1)} %get-tuple-element.232.n_ref, ...), custom_call_target="tpu_custom_call", output_to_operand_aliasing={{0}: (7, {}), {1}: (8, {}), {2}: (9, {}), {3}: (10, {})} | custom-call | flops 10000000000 | bytes 1000000 | tf_op jit(solution)/shard_map/pallas_call | solution.py:642
  128.8 9.3 %shard_map.259 = (bf16[16,320,768]{2,1,0:T(8,128)(2,1)}, bf16[320,1024]{1,0:T(8,128)(2,1)}, bf16[8,768,384]{2,1,0:T(8,128)(2,1)}, bf16[8,1024,512]{2,1,0:T(8,128)(2,1)}) custom-call(s32[4]{0:T(128)} %pad_add_fusion.idx.refs_0_, bf16[768,1024]{1,0:T(8,128)(2,1)} %get-tuple-element.232.n_ref, ...), custom_call_target="tpu_custom_call", output_to_operand_aliasing={{0}: (5, {}), {1}: (6, {}), {2}: (7, {}), {3}: (8, {})} | custom-call | flops 10000000000 | bytes 1000000 | tf_op jit(solution)/shard_map/pallas_call | solution.py:642
  138.2 6.9 %shard_map.260 = (f32[320,1024]{1,0:T(8,128)}, bf16[320,1024]{1,0:T(8,128)(2,1)}) custom-call(bf16[320,1024]{1,0:T(8,128)(2,1)} %get-tuple-element.294.m_ref, bf16[320,1024]{1,0:T(8,128)(2,1)} %bitcast.257, f32[1,1024]{1,0:T(1,128)} %convert.28.g_ref.gain_ref, bf16[8,1024,512]{2,1,0:T(8,128)(2,1)} %get-tuple-element.295.w_ref.wt_ref), custom_call_target="tpu_custom_call" | custom-call | flops 10000000000 | bytes 1000000 | tf_op jit(solution)/shard_map/pallas_call | solution.py:838
  152.2 10.2 %collective-permute-done.28.refs_4_ = bf16[320,1024]{1,0:T(8,128)(2,1)S(1)} collective-permute-done((bf16[320,1024]{1,0:T(8,128)(2,1)}, bf16[320,1024]{1,0:T(8,128)(2,1)S(1)}, u32[]{:S(2)}, u32[]{:S(2)}) %collective-permute-start.28) | collective-permute-done | bytes 655392 | tf_op jit(solution)/shard_map/ppermute | solution.py:510
  167.4 7.7 %collective-permute-done.32.refs_6_ = bf16[160,1024]{1,0:T(8,128)(2,1)S(1)} collective-permute-done((bf16[160,1024]{1,0:T(8,128)(2,1)S(1)}, bf16[160,1024]{1,0:T(8,128)(2,1)S(1)}, u32[]{:S(2)}, u32[]{:S(2)}) %collective-permute-start.32) | collective-permute-done | bytes 327712 | tf_op jit(solution)/shard_map/ppermute | solution.py:510
  178.0 37.2 %shard_map.261 = (bf16[2560,1024]{1,0:T(8,128)(2,1)}, bf16[2560,1024]{1,0:T(8,128)(2,1)}, bf16[2560,1536]{1,0:T(8,128)(2,1)}, bf16[2560,768]{1,0:T(8,128)(2,1)},...) custom-call(s32[4]{0:T(128)} %pad_add_fusion.idx.refs_0_, ...), custom_call_target="tpu_custom_call" | custom-call | flops 24999999488 | bytes 1000000 | tf_op jit(solution)/shard_map/pallas_call | solution.py:1081
  215.2 8.1 %convolution_convert_fusion.2 = bf16[768,1024]{1,0:T(8,128)(2,1)S(1)} fusion(bf16[2560,768]{1,0:T(8,128)(2,1)} %get-tuple-element.318, bf16[2560,1024]{1,0:T(8,128)(2,1)} %get-tuple-element.316.refs_4_), kind=kOutput, calls=%fused_computation.23 | convolution fusion | flops 4027318272 | bytes 10747904 | tf_op jit(solution)/shard_map/dot_general | solution.py:534
  223.4 9.3 %convolution_convert_fusion = bf16[1536,1024]{1,0:T(8,128)(2,1)S(1)} fusion(bf16[2560,1536]{1,0:T(8,128)(2,1)S(1)} %copy-done.53, bf16[2560,1024]{1,0:T(8,128)(2,1)S(1)} %copy-done.51), kind=kOutput, calls=%fused_computation.5 | convolution fusion | flops 8054636544 | bytes 16252928 | tf_op jit(solution)/shard_map/dot_general | solution.py:534
  235.5 30.3 %shard_map.262 = (bf16[1280,1024]{1,0:T(8,128)(2,1)}, bf16[1280,1024]{1,0:T(8,128)(2,1)}, bf16[1280,1024]{1,0:T(8,128)(2,1)}, bf16[1280,1024]{1,0:T(8,128)(2,1)}...) custom-call(s32[4]{0:T(128)} %pad_add_fusion.idx.refs_0_, bf16[4,4,1,3,96,256]{5,4,3,2,1,0:T(8,128)(2,1)} %bitcast.290, ...), custom_call_target="tpu_custom_call" | custom-call | flops 24999999488 | bytes 1000000 | tf_op jit(solution)/shard_map/pallas_call | solution.py:1081
  266.4 5.4 %fusion.42 = bf16[384,1024]{1,0:T(8,128)(2,1)S(1)} fusion(bf16[2560,384]{1,0:T(8,128)(2,1)} %get-tuple-element.325, bf16[2560,1024]{1,0:T(8,128)(2,1)} %get-tuple-element.316.refs_4_), kind=kOutput, calls=%fused_computation.159 | convolution fusion | flops 2013265920 | bytes 7995392 | tf_op jit(solution)/shard_map/dot_general | solution.py:534
  275.9 6.8 %convolution_convert_fusion.1 = bf16[768,1024]{1,0:T(8,128)(2,1)S(1)} fusion(bf16[2560,768]{1,0:T(8,128)(2,1)S(1)} %copy-done.52, bf16[2560,1024]{1,0:T(8,128)(2,1)} %get-tuple-element.315.refs_3_), kind=kOutput, calls=%fused_computation.22 | convolution fusion | flops 4027318272 | bytes 10747904 | tf_op jit(solution)/shard_map/dot_general | solution.py:534
  294.9 7.4 %collective-permute-done.42.b_ref = bf16[320,1024]{1,0:T(8,128)(2,1)} collective-permute-done((bf16[320,1024]{1,0:T(8,128)(2,1)}, bf16[320,1024]{1,0:T(8,128)(2,1)}, u32[]{:S(2)}, u32[]{:S(2)}) %collective-permute-start.42) | collective-permute-done | bytes 655392 | tf_op jit(solution)/shard_map/ppermute | solution.py:510
  305.1 7.9 %shard_map.263 = (f32[320,1024]{1,0:T(8,128)}, bf16[320,1024]{1,0:T(8,128)(2,1)}, bf16[320,1024]{1,0:T(8,128)(2,1)}, f32[8,1024]{1,0:T(8,128)}) custom-call(bf16[320,1024]{1,0:T(8,128)(2,1)} %slice.279.a_ref, bf16[320,1024]{1,0:T(8,128)(2,1)} %collective-permute-done.42.b_ref, bf16[320,1024]{1,0:T(8,128)(2,1)} %collective-permute-done.43.c_ref, ...), custom_call_target="tpu_custom_call" | custom-call | flops 10000000000 | bytes 1000000 | tf_op jit(solution)/shard_map/pallas_call | solution.py:811
  312.9 23.3 %shard_map.264 = (bf16[2,4,256,512]{3,2,1,0:T(8,128)(2,1)}, bf16[2,4,256,512]{3,2,1,0:T(8,128)(2,1)}, f32[768,1024]{1,0:T(8,128)}, f32[16,2,8,1024]{3,2,1,0:T(8,128)}) custom-call(s32[4]{0:T(128)} %pad_add_fusion.idx.refs_0_, bf16[768,1024]{1,0:T(8,128)(2,1)} %get-tuple-element.232.n_ref, bf16[16,320,768]{2,1,0:T(8,128)(2,1)} %get-tuple-element.347.p_ref, ...), custom_call_target="tpu_custom_call" | custom-call | flops 24999999488 | bytes 1000000 | tf_op jit(solution)/shard_map/pallas_call | solution.py:750
  338.6 15.4 %shard_map.265 = (bf16[2,2,256,512]{3,2,1,0:T(8,128)(2,1)}, bf16[2,2,256,512]{3,2,1,0:T(8,128)(2,1)}, f32[768,1024]{1,0:T(8,128)}, f32[16,2,8,1024]{3,2,1,0:T(8,128)}) custom-call(s32[4]{0:T(128)} %pad_add_fusion.idx.refs_0_, bf16[768,1024]{1,0:T(8,128)(2,1)} %get-tuple-element.232.n_ref, ...), custom_call_target="tpu_custom_call", output_to_operand_aliasing={{3}: (9, {})} | custom-call | flops 24999999488 | bytes 1000000 | tf_op jit(solution)/shard_map/pallas_call | solution.py:750
  358.0 16.0 %shard_map.266 = (bf16[2,2,256,512]{3,2,1,0:T(8,128)(2,1)}, bf16[2,2,256,512]{3,2,1,0:T(8,128)(2,1)}, f32[768,1024]{1,0:T(8,128)}, f32[16,2,8,1024]{3,2,1,0:T(8,128)}, bf16[4,2,64,1024]{3,2,1,0:T(8,128)(2,1)}) custom-call(s32[4]{0:T(128)} %pad_add_fusion.idx.refs_0_, bf16[768,1024]{1,0:T(8,128)(2,1)} %get-tuple-element.232.n_ref, ...), custom_call_target="tpu_custom_call", output_to_operand_aliasing={{3}: (9, {})} | custom-call | flops 24999999488 | bytes 1000000 | tf_op jit(solution)/shard_map/pallas_call | solution.py:750
  379.4 4.4 shard_map.267
  428.8 4.0 shard_map.268
  432.8 4.4 collective-permute-done.67
  443.5 4.3 collective-permute-done.70
  (401 shorter events, 174.5 us)
Async XLA Ops:
  7.2 170.7 %all-gather.7.cloned.1.call-start = ((), (), s32[]{:S(2)}) async-start(), calls=%async_computation.6 | async-start | bytes 5898240 | tf_op jit(solution)/shard_map/all_gather | solution.py:1189
  13.5 33.3 %collective-permute-start.8 = (bf16[320,1024]{1,0:T(8,128)(2,1)}, bf16[320,1024]{1,0:T(8,128)(2,1)}, u32[]{:S(2)}, u32[]{:S(2)}) collective-permute-start(bf16[320,1024]{1,0:T(8,128)(2,1)} %bitcast.27.refs_13_.cot_ref), channel_id=1, source_target_pairs={{0,4},{4,0},{8,12},{12,8},{16,20},{20,16},{24,28},{28,24},{1,5},{5... | collective-permute-start | bytes 1966088 | tf_op jit(solution)/shard_map/ppermute | solution.py:506
  25.8 21.4 %collective-permute-start.7 = (bf16[2,3,3,96,256]{4,3,2,1,0:T(8,128)(2,1)S(1)}, bf16[2,3,3,96,256]{4,3,2,1,0:T(8,128)(2,1)S(1)}, u32[]{:S(2)}, u32[]{:S(2)}) collective-permute-start(bf16[2,3,3,96,256]{4,3,2,1,0:T(8,128)(2,1)S(1)} %get-tuple-element.215), channel_id=1, source_target_pairs={{0,2},{1,3},{2,0},{3,1},{4,6},{5,7},{6,4},{7,5},{8,10},{9,11},{10,... | collective-permute-start | bytes 2654216 | tf_op jit(solution)/shard_map/ppermute | solution.py:510
  27.4 19.3 %collective-permute-start.3 = (bf16[1536,128]{1,0:T(8,128)(2,1)}, bf16[1536,128]{1,0:T(8,128)(2,1)}, u32[]{:S(2)}, u32[]{:S(2)}) collective-permute-start(bf16[1536,128]{1,0:T(8,128)(2,1)} %pad_maximum_fusion.17), channel_id=1, source_target_pairs={{0,8},{4,12},{8,0},{12,4},{16,24},{20,28},{24,16},{28,20},{1,9},{5... | collective-permute-start | bytes 1179656 | tf_op jit(solution)/shard_map/ppermute | solution.py:518
  56.4 20.3 %collective-permute-start.13 = (bf16[1024,128]{1,0:T(8,128)(2,1)S(1)}, bf16[1024,128]{1,0:T(8,128)(2,1)}, u32[]{:S(2)}, u32[]{:S(2)}) collective-permute-start(bf16[1024,128]{1,0:T(8,128)(2,1)S(1)} %slice.247), channel_id=1, source_target_pairs={{0,4},{4,0},{8,12},{12,8},{16,20},{20,16},{24,28},{28,24},{1,5},{5... | collective-permute-start | bytes 786440 | tf_op jit(solution)/shard_map/ppermute | solution.py:506
  57.0 19.8 %collective-permute-start.9 = (bf16[1024,128]{1,0:T(8,128)(2,1)S(1)}, bf16[1024,128]{1,0:T(8,128)(2,1)}, u32[]{:S(2)}, u32[]{:S(2)}) collective-permute-start(bf16[1024,128]{1,0:T(8,128)(2,1)S(1)} %slice.247), channel_id=1, source_target_pairs={{0,8},{4,12},{8,0},{12,4},{16,24},{20,28},{24,16},{28,20},{1,9},{5... | collective-permute-start | bytes 786440 | tf_op jit(solution)/shard_map/ppermute | solution.py:518
  58.5 18.2 %collective-permute-start.11 = (bf16[2,1040,128]{2,1,0:T(8,128)(2,1)S(1)}, bf16[2,1040,128]{2,1,0:T(8,128)(2,1)}, u32[]{:S(2)}, u32[]{:S(2)}) collective-permute-start(bf16[2,1040,128]{2,1,0:T(8,128)(2,1)S(1)} %pad_maximum_fusion.11), channel_id=1, source_target_pairs={{0,2},{1,3},{2,0},{3,1},{4,6},{5,7},{6,4},{7,5},{8,10},{9,11},{10,... | collective-permute-start | bytes 1597448 | tf_op jit(solution)/shard_map/ppermute | solution.py:510
  81.4 18.2 %collective-permute-start.19 = (bf16[320,1024]{1,0:T(8,128)(2,1)}, bf16[320,1024]{1,0:T(8,128)(2,1)}, u32[]{:S(2)}, u32[]{:S(2)}) collective-permute-start(bf16[320,1024]{1,0:T(8,128)(2,1)} %collective-permute-done.8.refs_15_), channel_id=1, source_target_pairs={{0,1},{1,0},{2,3},{3,2},{4,5},{5,4},{6,7},{7,6},{8,9},{9,8},{10,11... | collective-permute-start | bytes 1966088 | tf_op jit(solution)/shard_map/ppermute | solution.py:514
  81.5 18.2 %collective-permute-start.18 = (bf16[1024,128]{1,0:T(8,128)(2,1)}, bf16[1024,128]{1,0:T(8,128)(2,1)}, u32[]{:S(2)}, u32[]{:S(2)}) collective-permute-start(bf16[1024,128]{1,0:T(8,128)(2,1)} %collective-permute-done.9), channel_id=1, source_target_pairs={{0,2},{1,3},{2,0},{3,1},{4,6},{5,7},{6,4},{7,5},{8,10},{9,11},{10,... | collective-permute-start | bytes 786440 | tf_op jit(solution)/shard_map/ppermute | solution.py:510
  90.1 145.4 %all-gather.5.cloned.1.call-start = ((), (), s32[]{:S(2)}) async-start(), calls=%async_computation.5 | async-start | bytes 2949120 | tf_op jit(solution)/shard_map/all_gather | solution.py:1189
  104.7 20.1 %collective-permute-start.23 = (bf16[320,1024]{1,0:T(8,128)(2,1)}, bf16[320,1024]{1,0:T(8,128)(2,1)}, u32[]{:S(2)}, u32[]{:S(2)}) collective-permute-start(bf16[320,1024]{1,0:T(8,128)(2,1)} %bitcast.27.refs_13_.cot_ref), channel_id=1, source_target_pairs={{0,2},{1,3},{2,0},{3,1},{4,6},{5,7},{6,4},{7,5},{8,10},{9,11},{10,... | collective-permute-start | bytes 1966088 | tf_op jit(solution)/shard_map/ppermute | solution.py:510
  106.0 18.8 %collective-permute-start.24 = (bf16[320,1024]{1,0:T(8,128)(2,1)}, bf16[320,1024]{1,0:T(8,128)(2,1)}, u32[]{:S(2)}, u32[]{:S(2)}) collective-permute-start(bf16[320,1024]{1,0:T(8,128)(2,1)} %bitcast.27.refs_13_.cot_ref), channel_id=1, source_target_pairs={{0,1},{1,0},{2,3},{3,2},{4,5},{5,4},{6,7},{7,6},{8,9},{9,8},{10,11... | collective-permute-start | bytes 1966088 | tf_op jit(solution)/shard_map/ppermute | solution.py:514
  106.0 18.8 %collective-permute-start.22 = (bf16[2,1024,128]{2,1,0:T(8,128)(2,1)S(1)}, bf16[2,1024,128]{2,1,0:T(8,128)(2,1)S(1)}, u32[]{:S(2)}, u32[]{:S(2)}) collective-permute-start(bf16[2,1024,128]{2,1,0:T(8,128)(2,1)S(1)} %pad_maximum_fusion.16), channel_id=1, source_target_pairs={{0,4},{4,0},{8,12},{12,8},{16,20},{20,16},{24,28},{28,24},{1,5},{5... | collective-permute-start | bytes 1572872 | tf_op jit(solution)/shard_map/ppermute | solution.py:506
  125.2 19.9 %collective-permute-start.27 = (bf16[320,1024]{1,0:T(8,128)(2,1)}, bf16[320,1024]{1,0:T(8,128)(2,1)}, u32[]{:S(2)}, u32[]{:S(2)}) collective-permute-start(bf16[320,1024]{1,0:T(8,128)(2,1)} %collective-permute-done.8.refs_15_), channel_id=1, source_target_pairs={{0,2},{1,3},{2,0},{3,1},{4,6},{5,7},{6,4},{7,5},{8,10},{9,11},{10,... | collective-permute-start | bytes 1966088 | tf_op jit(solution)/shard_map/ppermute | solution.py:510
  176.9 159.9 %reduce-scatter.3.cloned.1.call-start = ((), (), s32[]{:S(2)}) async-start(), calls=%async_computation.3 | async-start | bytes 5898240 | tf_op jit(solution)/shard_map/reduce_scatter | solution.py:1220
  235.4 153.4 %reduce-scatter.5.cloned.1.call-start = ((), (), s32[]{:S(2)}) async-start(), calls=%async_computation.4 | async-start | bytes 2949120 | tf_op jit(solution)/shard_map/reduce_scatter | solution.py:1220
  302.8 33.6 %collective-permute-start.44 = (bf16[160,1024]{1,0:T(8,128)(2,1)S(1)}, bf16[160,1024]{1,0:T(8,128)(2,1)S(1)}, u32[]{:S(2)}, u32[]{:S(2)}) collective-permute-start(bf16[160,1024]{1,0:T(8,128)(2,1)S(1)} %get-tuple-element.345), channel_id=1, source_target_pairs={{0,2},{1,3},{2,0},{3,1},{4,6},{5,7},{6,4},{7,5},{8,10},{9,11},{10,... | collective-permute-start | bytes 983048 | tf_op jit(solution)/shard_map/ppermute | solution.py:510
  304.0 32.4 %collective-permute-start.45 = (bf16[160,1024]{1,0:T(8,128)(2,1)S(1)}, bf16[160,1024]{1,0:T(8,128)(2,1)S(1)}, u32[]{:S(2)}, u32[]{:S(2)}) collective-permute-start(bf16[160,1024]{1,0:T(8,128)(2,1)S(1)} %get-tuple-element.346), channel_id=1, source_target_pairs={{0,4},{4,0},{8,12},{12,8},{16,20},{20,16},{24,28},{28,24},{1,5},{5... | collective-permute-start | bytes 983048 | tf_op jit(solution)/shard_map/ppermute | solution.py:506
  336.3 17.8 %collective-permute-start.48 = (bf16[2,4,256,512]{3,2,1,0:T(8,128)(2,1)}, bf16[2,4,256,512]{3,2,1,0:T(8,128)(2,1)S(1)}, u32[]{:S(2)}, u32[]{:S(2)}) collective-permute-start(bf16[2,4,256,512]{3,2,1,0:T(8,128)(2,1)} %get-tuple-element.363), channel_id=1, source_target_pairs={{0,1},{1,0},{2,3},{3,2},{4,5},{5,4},{6,7},{7,6},{8,9},{9,8},{10,11... | collective-permute-start | bytes 6291464 | tf_op jit(solution)/shard_map/ppermute | solution.py:514
  354.0 20.1 %collective-permute-start.51 = (bf16[2,2,256,512]{3,2,1,0:T(8,128)(2,1)}, bf16[2,2,256,512]{3,2,1,0:T(8,128)(2,1)S(1)}, u32[]{:S(2)}, u32[]{:S(2)}) collective-permute-start(bf16[2,2,256,512]{3,2,1,0:T(8,128)(2,1)} %get-tuple-element.374), channel_id=1, source_target_pairs={{0,1},{1,0},{2,3},{3,2},{4,5},{5,4},{6,7},{7,6},{8,9},{9,8},{10,11... | collective-permute-start | bytes 3145736 | tf_op jit(solution)/shard_map/ppermute | solution.py:514
  355.9 18.2 %collective-permute-start.49 = (bf16[2,2,128,512]{3,2,0,1:T(8,128)(2,1)S(1)}, bf16[2,2,128,512]{3,2,0,1:T(8,128)(2,1)S(1)}, u32[]{:S(2)}, u32[]{:S(2)}) collective-permute-start(bf16[2,2,128,512]{3,2,0,1:T(8,128)(2,1)S(1)} %bitcast.267), channel_id=1, source_target_pairs={{0,2},{1,3},{2,0},{3,1},{4,6},{5,7},{6,4},{7,5},{8,10},{9,11},{10,... | collective-permute-start | bytes 1572872 | tf_op jit(solution)/shard_map/ppermute | solution.py:510
  377.7 18.3 %collective-permute-start.60 = (bf16[2,64,1024]{2,1,0:T(8,128)(2,1)}, bf16[2,64,1024]{2,1,0:T(8,128)(2,1)}, u32[]{:S(2)}, u32[]{:S(2)}) collective-permute-start(bf16[2,64,1024]{2,1,0:T(8,128)(2,1)} %get-tuple-element.436), channel_id=1, source_target_pairs={{0,8},{4,12},{8,0},{12,4},{16,24},{20,28},{24,16},{28,20},{1,9},{5... | collective-permute-start | bytes 786440 | tf_op jit(solution)/shard_map/ppermute | solution.py:518
  405.9 18.5 %collective-permute-start.66 = (f32[24,1024]{1,0:T(8,128)}, f32[24,1024]{1,0:T(8,128)}, u32[]{:S(2)}, u32[]{:S(2)}) collective-permute-start(f32[24,1024]{1,0:T(8,128)} %add.231), channel_id=1, source_target_pairs={{0,2},{1,3},{2,0},{3,1},{4,6},{5,7},{6,4},{7,5},{8,10},{9,11},{10,... | collective-permute-start | bytes 294920 | tf_op jit(solution)/shard_map/ppermute | solution.py:510
  420.7 29.0 %all-to-all-start = ((bf16[4,3,3,96,256]{4,3,2,1,0:T(8,128)(2,1)}), bf16[4,3,3,96,256]{4,3,2,1,0:T(8,128)(2,1)S(1)}, u32[]{:S(2)}, u32[]{:S(2)}) async-start(bf16[4,3,3,96,256]{4,3,2,1,0:T(8,128)(2,1)} %copy.156), calls=%async_computation.2 | async-start | bytes 3538944 | tf_op jit(solution)/shard_map/all_to_all | solution.py:1101
  (108 other events, 991.9 us)
Sparse Core Ops, SparseCore 0:
  90.2 86.7 all-gather.6
  178.6 48.9 all-gather.4
  235.5 83.5 reduce-scatter.2
  321.3 48.5 reduce-scatter.4

commit v7 on v6

--- a/solution.py
+++ b/solution.py
@@ -1029,8 +1029,10 @@
         if last:
             ss = [s_prev[...][:, 0:1], s_prev[...][:, 1:2], s]
             dot = p[0] * ss[0] + p[1] * ss[1] + p[2] * ss[2]
+            edge = dg[:, :128]
             for n in range(3):
-                dg = jnp.where(lane == 88 + n, p[n] * (ss[n] - dot), dg)
+                edge = jnp.where(lane[:, :128] == 88 + n, p[n] * (ss[n] - dot), edge)
+            dg = jnp.concatenate([edge, dg[:, 128:]], axis=1)
         win = (inner * w).astype(BF)
         dh = jnp.concatenate([dg.astype(BF), du.astype(BF)], axis=1)
         dh_ref[:, 768 * k : 768 * k + 768] = dh

time: 465 us -> 465 us (level)
  no operation moved by 1% of the time
where the time goes in v7:
time: 465 us; the launch traced here: 459 us
  Pallas kernels  185 us (40%)
  waiting for transfers between devices  77 us (17%)
  starting transfers between devices  70.3 us (15%)
  other arithmetic  42.3 us (9%)
  local copies, waits for them, and re-layouts  38.6 us (8%)
  matrix products  29.6 us (6%)
  between operations  15.6 us (3%)
    pallas_call x2, Pallas kernels, expert_call(): pl.pallas_call(functools.partial(expert_kernel, group, last), grid=(total...  67.5 us
    pallas_call x3, Pallas kernels, attend_back(): pl.pallas_call(functools.partial(attend_back_kernel, gn_prev is None, fin...  54.8 us
    ppermute x19, waiting for transfers between devices, move_x(): return lax.ppermute(v, 'wt', SWAP_X)  38.6 us
    pallas_call x3, Pallas kernels, attend(): pl.pallas_call(functools.partial(attend_kernel, groups, prev is None), gr...  33.9 us
    dot_general x4, matrix products, dot_tn(): lax.dot_general(a, b, (((0,), (0,)), ((), ())), preferred_element_type=F32)  29.6 us
    ppermute x19, starting transfers between devices, move_x(): return lax.ppermute(v, 'wt', SWAP_X)  23.5 us
    ppermute x18, starting transfers between devices, move_y(): return lax.ppermute(v, 'ctx', SWAP_Y)  21.1 us
    ppermute x6, waiting for transfers between devices, pair_z(): return lax.ppermute(v, 'ctx', PAIR_Z)  20.3 us
  transfers between devices with their start and end apart: 77, of which 23 were waited for; matrix products, arithmetic and copies ran while one was open for 19% of the time, Pallas kernels for 40%

profile of v7, /device:TPU:0, one launch (start us, length us, event | category | flops | bytes accessed | tf_op | source)
XLA Modules:
  0.0 458.7 jit_solution(16823730086289936773)
XLA Ops:
  31.1 5.7 %collective-permute-done.6 = bf16[1040,128]{1,0:T(8,128)(2,1)} collective-permute-done((bf16[1040,128]{1,0:T(8,128)(2,1)S(1)}, bf16[1040,128]{1,0:T(8,128)(2,1)}, u32[]{:S(2)}, u32[]{:S(2)}) %collective-permute-start.6) | collective-permute-done | bytes 266272 | tf_op jit(solution)/shard_map/ppermute | solution.py:506
  36.8 9.9 %collective-permute-done.3 = bf16[1536,128]{1,0:T(8,128)(2,1)} collective-permute-done((bf16[1536,128]{1,0:T(8,128)(2,1)}, bf16[1536,128]{1,0:T(8,128)(2,1)}, u32[]{:S(2)}, u32[]{:S(2)}) %collective-permute-start.3) | collective-permute-done | bytes 393248 | tf_op jit(solution)/shard_map/ppermute | solution.py:518
  66.7 10.0 %collective-permute-done.12 = bf16[1024,128]{1,0:T(8,128)(2,1)} collective-permute-done((bf16[1024,128]{1,0:T(8,128)(2,1)S(1)}, bf16[1024,128]{1,0:T(8,128)(2,1)}, u32[]{:S(2)}, u32[]{:S(2)}) %collective-permute-start.12) | collective-permute-done | bytes 262176 | tf_op jit(solution)/shard_map/ppermute | solution.py:510
  90.3 9.3 %shard_map.257 = (bf16[16,320,768]{2,1,0:T(8,128)(2,1)}, bf16[320,1024]{1,0:T(8,128)(2,1)}, bf16[8,768,384]{2,1,0:T(8,128)(2,1)}, bf16[8,1024,512]{2,1,0:T(8,128)(2,1)}) custom-call(s32[4]{0:T(128)} %pad_add_fusion.idx.refs_0_, bf16[768,1024]{1,0:T(8,128)(2,1)} %get-tuple-element.232.n_ref, f32[16,2,8,1024]{3,2,1,0:T(8,128)} %shard_map.255.w_ref, ...), custom_call_target="tpu_custom_call" | custom-call | flops 10000000000 | bytes 1000000 | tf_op jit(solution)/shard_map/pallas_call | solution.py:642
  109.5 15.2 %shard_map.258 = (bf16[16,320,768]{2,1,0:T(8,128)(2,1)}, bf16[320,1024]{1,0:T(8,128)(2,1)}, bf16[8,768,384]{2,1,0:T(8,128)(2,1)}, bf16[8,1024,512]{2,1,0:T(8,128)(2,1)}) custom-call(s32[4]{0:T(128)} %pad_add_fusion.idx.refs_0_, bf16[768,1024]{1,0:T(8,128)(2,1)} %get-tuple-element.232.n_ref, ...), custom_call_target="tpu_custom_call", output_to_operand_aliasing={{0}: (7, {}), {1}: (8, {}), {2}: (9, {}), {3}: (10, {})} | custom-call | flops 10000000000 | bytes 1000000 | tf_op jit(solution)/shard_map/pallas_call | solution.py:642
  128.8 9.3 %shard_map.259 = (bf16[16,320,768]{2,1,0:T(8,128)(2,1)}, bf16[320,1024]{1,0:T(8,128)(2,1)}, bf16[8,768,384]{2,1,0:T(8,128)(2,1)}, bf16[8,1024,512]{2,1,0:T(8,128)(2,1)}) custom-call(s32[4]{0:T(128)} %pad_add_fusion.idx.refs_0_, bf16[768,1024]{1,0:T(8,128)(2,1)} %get-tuple-element.232.n_ref, ...), custom_call_target="tpu_custom_call", output_to_operand_aliasing={{0}: (5, {}), {1}: (6, {}), {2}: (7, {}), {3}: (8, {})} | custom-call | flops 10000000000 | bytes 1000000 | tf_op jit(solution)/shard_map/pallas_call | solution.py:642
  138.2 6.9 %shard_map.260 = (f32[320,1024]{1,0:T(8,128)}, bf16[320,1024]{1,0:T(8,128)(2,1)}) custom-call(bf16[320,1024]{1,0:T(8,128)(2,1)} %get-tuple-element.294.m_ref, bf16[320,1024]{1,0:T(8,128)(2,1)} %bitcast.257, f32[1,1024]{1,0:T(1,128)} %convert.28.g_ref.gain_ref, bf16[8,1024,512]{2,1,0:T(8,128)(2,1)} %get-tuple-element.295.w_ref.wt_ref), custom_call_target="tpu_custom_call" | custom-call | flops 10000000000 | bytes 1000000 | tf_op jit(solution)/shard_map/pallas_call | solution.py:838
  152.2 10.2 %collective-permute-done.28.refs_4_ = bf16[320,1024]{1,0:T(8,128)(2,1)S(1)} collective-permute-done((bf16[320,1024]{1,0:T(8,128)(2,1)}, bf16[320,1024]{1,0:T(8,128)(2,1)S(1)}, u32[]{:S(2)}, u32[]{:S(2)}) %collective-permute-start.28) | collective-permute-done | bytes 655392 | tf_op jit(solution)/shard_map/ppermute | solution.py:510
  167.4 7.7 %collective-permute-done.32.refs_6_ = bf16[160,1024]{1,0:T(8,128)(2,1)S(1)} collective-permute-done((bf16[160,1024]{1,0:T(8,128)(2,1)S(1)}, bf16[160,1024]{1,0:T(8,128)(2,1)S(1)}, u32[]{:S(2)}, u32[]{:S(2)}) %collective-permute-start.32) | collective-permute-done | bytes 327712 | tf_op jit(solution)/shard_map/ppermute | solution.py:510
  178.0 37.2 %shard_map.261 = (bf16[2560,1024]{1,0:T(8,128)(2,1)}, bf16[2560,1024]{1,0:T(8,128)(2,1)}, bf16[2560,1536]{1,0:T(8,128)(2,1)}, bf16[2560,768]{1,0:T(8,128)(2,1)},...) custom-call(s32[4]{0:T(128)} %pad_add_fusion.idx.refs_0_, ...), custom_call_target="tpu_custom_call" | custom-call | flops 24999999488 | bytes 1000000 | tf_op jit(solution)/shard_map/pallas_call | solution.py:1083
  215.2 8.1 %convolution_convert_fusion.2 = bf16[768,1024]{1,0:T(8,128)(2,1)S(1)} fusion(bf16[2560,768]{1,0:T(8,128)(2,1)} %get-tuple-element.318, bf16[2560,1024]{1,0:T(8,128)(2,1)} %get-tuple-element.316.refs_4_), kind=kOutput, calls=%fused_computation.23 | convolution fusion | flops 4027318272 | bytes 10747904 | tf_op jit(solution)/shard_map/dot_general | solution.py:534
  223.4 9.3 %convolution_convert_fusion = bf16[1536,1024]{1,0:T(8,128)(2,1)S(1)} fusion(bf16[2560,1536]{1,0:T(8,128)(2,1)S(1)} %copy-done.53, bf16[2560,1024]{1,0:T(8,128)(2,1)S(1)} %copy-done.51), kind=kOutput, calls=%fused_computation.5 | convolution fusion | flops 8054636544 | bytes 16252928 | tf_op jit(solution)/shard_map/dot_general | solution.py:534
  235.5 30.3 %shard_map.262 = (bf16[1280,1024]{1,0:T(8,128)(2,1)}, bf16[1280,1024]{1,0:T(8,128)(2,1)}, bf16[1280,1024]{1,0:T(8,128)(2,1)}, bf16[1280,1024]{1,0:T(8,128)(2,1)}...) custom-call(s32[4]{0:T(128)} %pad_add_fusion.idx.refs_0_, bf16[4,4,1,3,96,256]{5,4,3,2,1,0:T(8,128)(2,1)} %bitcast.290, ...), custom_call_target="tpu_custom_call" | custom-call | flops 24999999488 | bytes 1000000 | tf_op jit(solution)/shard_map/pallas_call | solution.py:1083
  266.4 5.4 %fusion.42 = bf16[384,1024]{1,0:T(8,128)(2,1)S(1)} fusion(bf16[2560,384]{1,0:T(8,128)(2,1)} %get-tuple-element.325, bf16[2560,1024]{1,0:T(8,128)(2,1)} %get-tuple-element.316.refs_4_), kind=kOutput, calls=%fused_computation.159 | convolution fusion | flops 2013265920 | bytes 7995392 | tf_op jit(solution)/shard_map/dot_general | solution.py:534
  275.9 6.8 %convolution_convert_fusion.1 = bf16[768,1024]{1,0:T(8,128)(2,1)S(1)} fusion(bf16[2560,768]{1,0:T(8,128)(2,1)S(1)} %copy-done.52, bf16[2560,1024]{1,0:T(8,128)(2,1)} %get-tuple-element.315.refs_3_), kind=kOutput, calls=%fused_computation.22 | convolution fusion | flops 4027318272 | bytes 10747904 | tf_op jit(solution)/shard_map/dot_general | solution.py:534
  294.9 7.4 %collective-permute-done.42.b_ref = bf16[320,1024]{1,0:T(8,128)(2,1)} collective-permute-done((bf16[320,1024]{1,0:T(8,128)(2,1)}, bf16[320,1024]{1,0:T(8,128)(2,1)}, u32[]{:S(2)}, u32[]{:S(2)}) %collective-permute-start.42) | collective-permute-done | bytes 655392 | tf_op jit(solution)/shard_map/ppermute | solution.py:510
  305.1 7.9 %shard_map.263 = (f32[320,1024]{1,0:T(8,128)}, bf16[320,1024]{1,0:T(8,128)(2,1)}, bf16[320,1024]{1,0:T(8,128)(2,1)}, f32[8,1024]{1,0:T(8,128)}) custom-call(bf16[320,1024]{1,0:T(8,128)(2,1)} %slice.279.a_ref, bf16[320,1024]{1,0:T(8,128)(2,1)} %collective-permute-done.42.b_ref, bf16[320,1024]{1,0:T(8,128)(2,1)} %collective-permute-done.43.c_ref, ...), custom_call_target="tpu_custom_call" | custom-call | flops 10000000000 | bytes 1000000 | tf_op jit(solution)/shard_map/pallas_call | solution.py:811
  312.9 23.3 %shard_map.264 = (bf16[2,4,256,512]{3,2,1,0:T(8,128)(2,1)}, bf16[2,4,256,512]{3,2,1,0:T(8,128)(2,1)}, f32[768,1024]{1,0:T(8,128)}, f32[16,2,8,1024]{3,2,1,0:T(8,128)}) custom-call(s32[4]{0:T(128)} %pad_add_fusion.idx.refs_0_, bf16[768,1024]{1,0:T(8,128)(2,1)} %get-tuple-element.232.n_ref, bf16[16,320,768]{2,1,0:T(8,128)(2,1)} %get-tuple-element.347.p_ref, ...), custom_call_target="tpu_custom_call" | custom-call | flops 24999999488 | bytes 1000000 | tf_op jit(solution)/shard_map/pallas_call | solution.py:750
  338.6 15.4 %shard_map.265 = (bf16[2,2,256,512]{3,2,1,0:T(8,128)(2,1)}, bf16[2,2,256,512]{3,2,1,0:T(8,128)(2,1)}, f32[768,1024]{1,0:T(8,128)}, f32[16,2,8,1024]{3,2,1,0:T(8,128)}) custom-call(s32[4]{0:T(128)} %pad_add_fusion.idx.refs_0_, bf16[768,1024]{1,0:T(8,128)(2,1)} %get-tuple-element.232.n_ref, ...), custom_call_target="tpu_custom_call", output_to_operand_aliasing={{3}: (9, {})} | custom-call | flops 24999999488 | bytes 1000000 | tf_op jit(solution)/shard_map/pallas_call | solution.py:750
  358.0 16.0 %shard_map.266 = (bf16[2,2,256,512]{3,2,1,0:T(8,128)(2,1)}, bf16[2,2,256,512]{3,2,1,0:T(8,128)(2,1)}, f32[768,1024]{1,0:T(8,128)}, f32[16,2,8,1024]{3,2,1,0:T(8,128)}, bf16[4,2,64,1024]{3,2,1,0:T(8,128)(2,1)}) custom-call(s32[4]{0:T(128)} %pad_add_fusion.idx.refs_0_, bf16[768,1024]{1,0:T(8,128)(2,1)} %get-tuple-element.232.n_ref, ...), custom_call_target="tpu_custom_call", output_to_operand_aliasing={{3}: (9, {})} | custom-call | flops 24999999488 | bytes 1000000 | tf_op jit(solution)/shard_map/pallas_call | solution.py:750
  379.4 4.4 shard_map.267
  428.8 4.0 shard_map.268
  432.8 4.4 collective-permute-done.67
  443.5 4.3 collective-permute-done.70
  (401 shorter events, 174.5 us)
Async XLA Ops:
  7.2 170.7 %all-gather.7.cloned.1.call-start = ((), (), s32[]{:S(2)}) async-start(), calls=%async_computation.6 | async-start | bytes 5898240 | tf_op jit(solution)/shard_map/all_gather | solution.py:1191
  13.5 33.3 %collective-permute-start.8 = (bf16[320,1024]{1,0:T(8,128)(2,1)}, bf16[320,1024]{1,0:T(8,128)(2,1)}, u32[]{:S(2)}, u32[]{:S(2)}) collective-permute-start(bf16[320,1024]{1,0:T(8,128)(2,1)} %bitcast.27.refs_13_.cot_ref), channel_id=1, source_target_pairs={{0,4},{4,0},{8,12},{12,8},{16,20},{20,16},{24,28},{28,24},{1,5},{5... | collective-permute-start | bytes 1966088 | tf_op jit(solution)/shard_map/ppermute | solution.py:506
  25.8 21.4 %collective-permute-start.7 = (bf16[2,3,3,96,256]{4,3,2,1,0:T(8,128)(2,1)S(1)}, bf16[2,3,3,96,256]{4,3,2,1,0:T(8,128)(2,1)S(1)}, u32[]{:S(2)}, u32[]{:S(2)}) collective-permute-start(bf16[2,3,3,96,256]{4,3,2,1,0:T(8,128)(2,1)S(1)} %get-tuple-element.215), channel_id=1, source_target_pairs={{0,2},{1,3},{2,0},{3,1},{4,6},{5,7},{6,4},{7,5},{8,10},{9,11},{10,... | collective-permute-start | bytes 2654216 | tf_op jit(solution)/shard_map/ppermute | solution.py:510
  27.4 19.3 %collective-permute-start.3 = (bf16[1536,128]{1,0:T(8,128)(2,1)}, bf16[1536,128]{1,0:T(8,128)(2,1)}, u32[]{:S(2)}, u32[]{:S(2)}) collective-permute-start(bf16[1536,128]{1,0:T(8,128)(2,1)} %pad_maximum_fusion.17), channel_id=1, source_target_pairs={{0,8},{4,12},{8,0},{12,4},{16,24},{20,28},{24,16},{28,20},{1,9},{5... | collective-permute-start | bytes 1179656 | tf_op jit(solution)/shard_map/ppermute | solution.py:518
  56.4 20.3 %collective-permute-start.13 = (bf16[1024,128]{1,0:T(8,128)(2,1)S(1)}, bf16[1024,128]{1,0:T(8,128)(2,1)}, u32[]{:S(2)}, u32[]{:S(2)}) collective-permute-start(bf16[1024,128]{1,0:T(8,128)(2,1)S(1)} %slice.247), channel_id=1, source_target_pairs={{0,4},{4,0},{8,12},{12,8},{16,20},{20,16},{24,28},{28,24},{1,5},{5... | collective-permute-start | bytes 786440 | tf_op jit(solution)/shard_map/ppermute | solution.py:506
  57.0 19.8 %collective-permute-start.9 = (bf16[1024,128]{1,0:T(8,128)(2,1)S(1)}, bf16[1024,128]{1,0:T(8,128)(2,1)}, u32[]{:S(2)}, u32[]{:S(2)}) collective-permute-start(bf16[1024,128]{1,0:T(8,128)(2,1)S(1)} %slice.247), channel_id=1, source_target_pairs={{0,8},{4,12},{8,0},{12,4},{16,24},{20,28},{24,16},{28,20},{1,9},{5... | collective-permute-start | bytes 786440 | tf_op jit(solution)/shard_map/ppermute | solution.py:518
  58.5 18.2 %collective-permute-start.11 = (bf16[2,1040,128]{2,1,0:T(8,128)(2,1)S(1)}, bf16[2,1040,128]{2,1,0:T(8,128)(2,1)}, u32[]{:S(2)}, u32[]{:S(2)}) collective-permute-start(bf16[2,1040,128]{2,1,0:T(8,128)(2,1)S(1)} %pad_maximum_fusion.11), channel_id=1, source_target_pairs={{0,2},{1,3},{2,0},{3,1},{4,6},{5,7},{6,4},{7,5},{8,10},{9,11},{10,... | collective-permute-start | bytes 1597448 | tf_op jit(solution)/shard_map/ppermute | solution.py:510
  81.4 18.2 %collective-permute-start.19 = (bf16[320,1024]{1,0:T(8,128)(2,1)}, bf16[320,1024]{1,0:T(8,128)(2,1)}, u32[]{:S(2)}, u32[]{:S(2)}) collective-permute-start(bf16[320,1024]{1,0:T(8,128)(2,1)} %collective-permute-done.8.refs_15_), channel_id=1, source_target_pairs={{0,1},{1,0},{2,3},{3,2},{4,5},{5,4},{6,7},{7,6},{8,9},{9,8},{10,11... | collective-permute-start | bytes 1966088 | tf_op jit(solution)/shard_map/ppermute | solution.py:514
  81.5 18.2 %collective-permute-start.18 = (bf16[1024,128]{1,0:T(8,128)(2,1)}, bf16[1024,128]{1,0:T(8,128)(2,1)}, u32[]{:S(2)}, u32[]{:S(2)}) collective-permute-start(bf16[1024,128]{1,0:T(8,128)(2,1)} %collective-permute-done.9), channel_id=1, source_target_pairs={{0,2},{1,3},{2,0},{3,1},{4,6},{5,7},{6,4},{7,5},{8,10},{9,11},{10,... | collective-permute-start | bytes 786440 | tf_op jit(solution)/shard_map/ppermute | solution.py:510
  90.1 145.4 %all-gather.5.cloned.1.call-start = ((), (), s32[]{:S(2)}) async-start(), calls=%async_computation.5 | async-start | bytes 2949120 | tf_op jit(solution)/shard_map/all_gather | solution.py:1191
  104.7 20.1 %collective-permute-start.23 = (bf16[320,1024]{1,0:T(8,128)(2,1)}, bf16[320,1024]{1,0:T(8,128)(2,1)}, u32[]{:S(2)}, u32[]{:S(2)}) collective-permute-start(bf16[320,1024]{1,0:T(8,128)(2,1)} %bitcast.27.refs_13_.cot_ref), channel_id=1, source_target_pairs={{0,2},{1,3},{2,0},{3,1},{4,6},{5,7},{6,4},{7,5},{8,10},{9,11},{10,... | collective-permute-start | bytes 1966088 | tf_op jit(solution)/shard_map/ppermute | solution.py:510
  106.0 18.8 %collective-permute-start.24 = (bf16[320,1024]{1,0:T(8,128)(2,1)}, bf16[320,1024]{1,0:T(8,128)(2,1)}, u32[]{:S(2)}, u32[]{:S(2)}) collective-permute-start(bf16[320,1024]{1,0:T(8,128)(2,1)} %bitcast.27.refs_13_.cot_ref), channel_id=1, source_target_pairs={{0,1},{1,0},{2,3},{3,2},{4,5},{5,4},{6,7},{7,6},{8,9},{9,8},{10,11... | collective-permute-start | bytes 1966088 | tf_op jit(solution)/shard_map/ppermute | solution.py:514
  106.0 18.8 %collective-permute-start.22 = (bf16[2,1024,128]{2,1,0:T(8,128)(2,1)S(1)}, bf16[2,1024,128]{2,1,0:T(8,128)(2,1)S(1)}, u32[]{:S(2)}, u32[]{:S(2)}) collective-permute-start(bf16[2,1024,128]{2,1,0:T(8,128)(2,1)S(1)} %pad_maximum_fusion.16), channel_id=1, source_target_pairs={{0,4},{4,0},{8,12},{12,8},{16,20},{20,16},{24,28},{28,24},{1,5},{5... | collective-permute-start | bytes 1572872 | tf_op jit(solution)/shard_map/ppermute | solution.py:506
  125.2 19.9 %collective-permute-start.27 = (bf16[320,1024]{1,0:T(8,128)(2,1)}, bf16[320,1024]{1,0:T(8,128)(2,1)}, u32[]{:S(2)}, u32[]{:S(2)}) collective-permute-start(bf16[320,1024]{1,0:T(8,128)(2,1)} %collective-permute-done.8.refs_15_), channel_id=1, source_target_pairs={{0,2},{1,3},{2,0},{3,1},{4,6},{5,7},{6,4},{7,5},{8,10},{9,11},{10,... | collective-permute-start | bytes 1966088 | tf_op jit(solution)/shard_map/ppermute | solution.py:510
  176.9 159.9 %reduce-scatter.3.cloned.1.call-start = ((), (), s32[]{:S(2)}) async-start(), calls=%async_computation.3 | async-start | bytes 5898240 | tf_op jit(solution)/shard_map/reduce_scatter | solution.py:1222
  235.4 153.4 %reduce-scatter.5.cloned.1.call-start = ((), (), s32[]{:S(2)}) async-start(), calls=%async_computation.4 | async-start | bytes 2949120 | tf_op jit(solution)/shard_map/reduce_scatter | solution.py:1222
  302.8 33.6 %collective-permute-start.44 = (bf16[160,1024]{1,0:T(8,128)(2,1)S(1)}, bf16[160,1024]{1,0:T(8,128)(2,1)S(1)}, u32[]{:S(2)}, u32[]{:S(2)}) collective-permute-start(bf16[160,1024]{1,0:T(8,128)(2,1)S(1)} %get-tuple-element.345), channel_id=1, source_target_pairs={{0,2},{1,3},{2,0},{3,1},{4,6},{5,7},{6,4},{7,5},{8,10},{9,11},{10,... | collective-permute-start | bytes 983048 | tf_op jit(solution)/shard_map/ppermute | solution.py:510
  304.0 32.4 %collective-permute-start.45 = (bf16[160,1024]{1,0:T(8,128)(2,1)S(1)}, bf16[160,1024]{1,0:T(8,128)(2,1)S(1)}, u32[]{:S(2)}, u32[]{:S(2)}) collective-permute-start(bf16[160,1024]{1,0:T(8,128)(2,1)S(1)} %get-tuple-element.346), channel_id=1, source_target_pairs={{0,4},{4,0},{8,12},{12,8},{16,20},{20,16},{24,28},{28,24},{1,5},{5... | collective-permute-start | bytes 983048 | tf_op jit(solution)/shard_map/ppermute | solution.py:506
  336.3 17.8 %collective-permute-start.48 = (bf16[2,4,256,512]{3,2,1,0:T(8,128)(2,1)}, bf16[2,4,256,512]{3,2,1,0:T(8,128)(2,1)S(1)}, u32[]{:S(2)}, u32[]{:S(2)}) collective-permute-start(bf16[2,4,256,512]{3,2,1,0:T(8,128)(2,1)} %get-tuple-element.363), channel_id=1, source_target_pairs={{0,1},{1,0},{2,3},{3,2},{4,5},{5,4},{6,7},{7,6},{8,9},{9,8},{10,11... | collective-permute-start | bytes 6291464 | tf_op jit(solution)/shard_map/ppermute | solution.py:514
  354.0 20.1 %collective-permute-start.51 = (bf16[2,2,256,512]{3,2,1,0:T(8,128)(2,1)}, bf16[2,2,256,512]{3,2,1,0:T(8,128)(2,1)S(1)}, u32[]{:S(2)}, u32[]{:S(2)}) collective-permute-start(bf16[2,2,256,512]{3,2,1,0:T(8,128)(2,1)} %get-tuple-element.374), channel_id=1, source_target_pairs={{0,1},{1,0},{2,3},{3,2},{4,5},{5,4},{6,7},{7,6},{8,9},{9,8},{10,11... | collective-permute-start | bytes 3145736 | tf_op jit(solution)/shard_map/ppermute | solution.py:514
  355.9 18.2 %collective-permute-start.49 = (bf16[2,2,128,512]{3,2,0,1:T(8,128)(2,1)S(1)}, bf16[2,2,128,512]{3,2,0,1:T(8,128)(2,1)S(1)}, u32[]{:S(2)}, u32[]{:S(2)}) collective-permute-start(bf16[2,2,128,512]{3,2,0,1:T(8,128)(2,1)S(1)} %bitcast.267), channel_id=1, source_target_pairs={{0,2},{1,3},{2,0},{3,1},{4,6},{5,7},{6,4},{7,5},{8,10},{9,11},{10,... | collective-permute-start | bytes 1572872 | tf_op jit(solution)/shard_map/ppermute | solution.py:510
  377.7 18.3 %collective-permute-start.60 = (bf16[2,64,1024]{2,1,0:T(8,128)(2,1)}, bf16[2,64,1024]{2,1,0:T(8,128)(2,1)}, u32[]{:S(2)}, u32[]{:S(2)}) collective-permute-start(bf16[2,64,1024]{2,1,0:T(8,128)(2,1)} %get-tuple-element.436), channel_id=1, source_target_pairs={{0,8},{4,12},{8,0},{12,4},{16,24},{20,28},{24,16},{28,20},{1,9},{5... | collective-permute-start | bytes 786440 | tf_op jit(solution)/shard_map/ppermute | solution.py:518
  405.9 18.5 %collective-permute-start.66 = (f32[24,1024]{1,0:T(8,128)}, f32[24,1024]{1,0:T(8,128)}, u32[]{:S(2)}, u32[]{:S(2)}) collective-permute-start(f32[24,1024]{1,0:T(8,128)} %add.231), channel_id=1, source_target_pairs={{0,2},{1,3},{2,0},{3,1},{4,6},{5,7},{6,4},{7,5},{8,10},{9,11},{10,... | collective-permute-start | bytes 294920 | tf_op jit(solution)/shard_map/ppermute | solution.py:510
  420.7 29.0 %all-to-all-start = ((bf16[4,3,3,96,256]{4,3,2,1,0:T(8,128)(2,1)}), bf16[4,3,3,96,256]{4,3,2,1,0:T(8,128)(2,1)S(1)}, u32[]{:S(2)}, u32[]{:S(2)}) async-start(bf16[4,3,3,96,256]{4,3,2,1,0:T(8,128)(2,1)} %copy.156), calls=%async_computation.2 | async-start | bytes 3538944 | tf_op jit(solution)/shard_map/all_to_all | solution.py:1103
  (108 other events, 991.9 us)
Sparse Core Ops, SparseCore 0:
  90.2 86.7 all-gather.6
  178.6 48.9 all-gather.4
  235.5 83.5 reduce-scatter.2
  321.3 48.5 reduce-scatter.4
